TPU v7x, 128 devices: a whole 4x4x4 slice. The times are simulated.
128 devices in a mesh: fsdp: 16 (over z, y), pre: 8 (over x, core).
Axes of the slice: x: 4, y: 4, z: 4, core: 2. Of those that a mesh axis runs over, the one named last changes fastest.
Arguments:
- inputs: bfloat16 [4096, 8192], P('fsdp', 'pre'), may hold values from -15 to 15
- grads_out: bfloat16 [4096, 8192], P('fsdp', 'pre'), may hold values from -0.234375 to 0.234375
- owner: int32 [16, 16], replicated, may hold values from 0 to 15, as said below
- offsets: int32 [16, 16], replicated, may hold values from 0 to 2, as said below
- prev_roots: float32 [384, 2, 512, 512], P(('fsdp', 'pre')), may hold values from -1 to 1, as said below
Outputs:
- update: bfloat16 [384, 512, 512], P(('fsdp', 'pre'))
- new_roots: float32 [384, 2, 512, 512], P(('fsdp', 'pre'))
Inputs may be any that keep to these rules, and one draw needn't show every extreme that they name: Within each group of 2 block columns that one pre index holds, at most 3 blocks share an owner and some owner holds exactly 3; of the blocks in the rows of one fsdp index and one column group, at most 1 share an owner, and some reach 1. `offsets`: blocks of one column group with the same owner have distinct slots. `prev_roots`: each matrix is symmetric.
All inputs are finite; a program needn't handle non-finite values.
Results may differ from a plain program's by a relative error of at most 0.04.
Values may be sent and summed in bfloat16 or wider, within the bound.
No kernel may reach another device: no remote copies, remote signals or barrier semaphores. Data moves between devices by JAX's collectives and lax.ppermute only.
A program may use at most 192 MiB of HBM per device.

v0:
```python
import jax
import jax.numpy as jnp
from jax import lax
from jax.sharding import PartitionSpec as P

ITERS = 2


def multiply(first_arg, second_arg):
    return jnp.einsum(
        "snab,snbc->snac",
        first_arg.astype(jnp.bfloat16),
        second_arg.astype(jnp.bfloat16),
        preferred_element_type=jnp.float32,
    )


def body(inputs, grads_out, owner, offsets, prev_roots):
    slot_count = prev_roots.shape[0]
    block_size = prev_roots.shape[-1]
    col_blocks = grads_out.shape[1] // block_size
    column = lax.axis_index("pre")
    self_index = lax.axis_index("fsdp")
    features = lax.all_gather(inputs, "pre", axis=1, tiled=True)
    owner_here = lax.dynamic_slice_in_dim(owner, column * col_blocks, col_blocks, 1)
    offset_here = lax.dynamic_slice_in_dim(offsets, column * col_blocks, col_blocks, 1)
    slot_key = owner_here * slot_count + offset_here
    home_rows = lax.psum_scatter(
        lax.dot_general(
            features, grads_out, (((0,), (0,)), ((), ())), preferred_element_type=jnp.float32
        ).astype(jnp.bfloat16),
        "fsdp",
        scatter_dimension=0,
        tiled=True,
    )
    wanted_slots = self_index * slot_count + jnp.arange(slot_count, dtype=jnp.int32)
    fragment = lax.all_gather(home_rows, "fsdp", axis=0, tiled=True)
    count_blocks = fragment.shape[0] // block_size
    rows_here = jnp.arange(count_blocks, dtype=jnp.int32)
    keys_here = jnp.take(slot_key, rows_here, axis=0)
    chosen = (keys_here[:, :, None] == wanted_slots[None, None, :]).astype(jnp.bfloat16)
    fragment_tiles = fragment.reshape(count_blocks, block_size, col_blocks, block_size)
    grad_slots = jnp.einsum(
        "rcs,racb->sab", chosen, fragment_tiles, preferred_element_type=jnp.float32
    ).astype(jnp.bfloat16)
    left_stat = jnp.einsum(
        "sab,scb->sac", grad_slots, grad_slots, preferred_element_type=jnp.float32
    )
    right_stat = jnp.einsum(
        "sba,sbc->sac", grad_slots, grad_slots, preferred_element_type=jnp.float32
    )
    statistics = jnp.stack([left_stat, right_stat], axis=1)
    identity = jnp.eye(block_size, dtype=jnp.float32)
    traces = jnp.einsum("snaa->sn", statistics)
    damped = 0.1 * statistics / (traces / block_size + 1e-06)[:, :, None, None] + identity
    square = multiply(prev_roots, prev_roots)
    fourth = multiply(square, square)
    product_now = multiply(fourth, damped)
    root_now = prev_roots
    for iteration in range(ITERS):
        factor = (5.0 * identity - product_now) * 0.25
        factor_sq = multiply(factor, factor)
        factor_four = multiply(factor_sq, factor_sq)
        product_now = multiply(factor_four, product_now)
        root_now = multiply(root_now, factor)
    halfway = jnp.einsum(
        "sab,sbc->sac",
        root_now[:, 0].astype(jnp.bfloat16),
        grad_slots,
        preferred_element_type=jnp.float32,
    ).astype(jnp.bfloat16)
    update = jnp.einsum(
        "sab,sbc->sac",
        halfway,
        root_now[:, 1].astype(jnp.bfloat16),
        preferred_element_type=jnp.float32,
    ).astype(jnp.bfloat16)
    return (update, root_now)


def solution(mesh):
    in_specs = (P("fsdp", "pre"), P("fsdp", "pre"), P(), P(), P(("fsdp", "pre"), None, None, None))
    out_specs = (P(("fsdp", "pre"), None, None), P(("fsdp", "pre"), None, None, None))
    return jax.shard_map(body, mesh=mesh, in_specs=in_specs, out_specs=out_specs, check_vma=False)
```

profile of v0, /device:TPU:0, one launch (start us, length us, event | category | flops | bytes accessed | tf_op | source)
XLA Modules:
  0.0 378.0 jit_solution(15130678935705167599)
XLA Ops:
  7.2 0.0 copy-start
  7.2 0.0 all-gather.3.cloned.1.call-start
  7.2 0.7 all-gather.3.cloned.1.call-update
  7.9 0.0 reduce-scatter.2.cloned.1.call-start
  8.0 36.3 %all-gather.3.cloned.1.call-done = bf16[256,8192]{1,0:T(8,128)(2,1)} async-done(((bf16[256,1024]{1,0:T(8,128)(2,1)}), bf16[256,8192]{1,0:T(8,128)(2,1)}) %all-gather.3.cloned.1.call-update) | async-done | bytes 4194320 | tf_op jit(solution)/shard_map/all_gather | solution.py:24
  44.3 0.0 copy-done
  44.3 10.5 %convolution_convert_fusion = bf16[8192,1024]{1,0:T(8,128)(2,1)} fusion(bf16[256,8192]{1,0:T(8,128)(2,1)} %all-gather.3.cloned.1.call-done, bf16[256,1024]{1,0:T(8,128)(2,1)S(1)} %copy-done), kind=kOutput, calls=%fused_computation.3 | convolution fusion | flops 4303355904 | bytes 21495808 | tf_op jit(solution)/shard_map/dot_general | solution.py:29
  54.7 0.0 copy-start.5
  54.7 0.0 copy-start.6
  54.8 0.0 reduce-scatter.2.cloned.1.call-update
  54.8 0.0 all-gather.5.cloned.1.call-start
  54.8 110.8 %reduce-scatter.2.cloned.1.call-done = bf16[512,1024]{1,0:T(8,128)(2,1)} async-done(((bf16[8192,1024]{1,0:T(8,128)(2,1)}), bf16[512,1024]{1,0:T(8,128)(2,1)}) %reduce-scatter.2.cloned.1.call-update) | async-done | bytes 1048592 | tf_op jit(solution)/shard_map/reduce_scatter | solution.py:28
  165.7 0.0 all-gather.5.cloned.1.call-update
  165.7 0.0 copy-done.5
  165.7 0.0 copy-done.6
  165.7 0.1 dynamic-slice_add_fusion
  165.8 0.6 gather_fusion
  166.4 0.1 broadcast_select_fusion
  166.5 0.1 copy.14
  166.5 0.1 iota_compare_fusion
  166.6 0.1 fusion.33
  166.8 0.1 fusion.34
  166.9 8.1 %fusion.31 = bf16[3,2,512,512]{3,2,1,0:T(8,128)(2,1)} fusion(f32[3,2,512,512]{3,2,1,0:T(8,128)} %param.9), kind=kOutput, calls=%fused_computation.33 | convolution fusion | flops 1612185600 | bytes 9437184 | tf_op jit(solution)/shard_map/snab,snbc->snac/dot_general | solution.py:10
  174.9 103.7 %all-gather.5.cloned.1.call-done = bf16[8192,1024]{1,0:T(8,128)(2,1)} async-done(((bf16[512,1024]{1,0:T(8,128)(2,1)}), bf16[8192,1024]{1,0:T(8,128)(2,1)}) %all-gather.5.cloned.1.call-update) | async-done | bytes 16777232 | tf_op jit(solution)/shard_map/all_gather | solution.py:37
  278.7 27.8 %reshape.50 = bf16[16,512,2,512]{3,2,1,0:T(2,128)(2,1)} reshape(bf16[8192,1024]{1,0:T(8,128)(2,1)} %all-gather.5.cloned.1.call-done) | data formatting | bytes 33554432 | tf_op jit(solution)/shard_map/reshape | solution.py:42
  306.5 16.0 %fusion.26 = bf16[3,512,512]{2,0,1:T(4,128)(2,1)S(1)} fusion(bf16[16,512,2,512]{3,2,1,0:T(2,128)(2,1)} %reshape.50, s32[16,2]{0,1:T(2,128)S(1)} %copy.14, s32[3]{0:T(128)S(1)} %iota_add_fusion), kind=kOutput, calls=%fused_computation.25 | convolution fusion | flops 50331744 | bytes 18350220 | tf_op jit(solution)/shard_map/rcs,racb->sab/dot_general | solution.py:43
  322.4 0.0 copy-start.4
  322.4 1.1 convolution_bitcast_fusion
  323.5 0.0 copy-start.2
  323.5 1.4 convolution_bitcast_fusion.1
  324.9 0.0 copy-done.4
  324.9 0.0 copy-start.3
  324.9 1.1 select_reduce_fusion
  326.1 0.0 copy-done.2
  326.1 0.5 copy-done.3
  326.6 10.8 %fusion.3 = f32[3,2,512,512]{3,2,1,0:T(8,128)} fusion(bf16[3,2,512,512]{3,2,1,0:T(8,128)(2,1)} %fusion.31, f32[3,1,512,512]{3,2,0,1:T(8,128)} %copy-done.2, f32[3,1,512,512]{3,2,0,1:T(8,128)} %copy-done.3, f32[512,512]{1,0:T(8,128)S(1)} %fusion.33, f32[3,2]{0,1:T(2,128)S(1)} %multiply_add_fusion), kind=kOutput, calls=%fused_computation.10 | convolution fusion | flops 3230662656 | bytes 16777240 | tf_op jit(solution)/shard_map/snab,snbc->snac/dot_general | solution.py:10
  337.4 12.3 %fusion.8 = bf16[3,2,512,512]{3,2,1,0:T(8,128)(2,1)} fusion(f32[3,2,512,512]{3,2,1,0:T(8,128)} %fusion.3, f32[512,512]{1,0:T(8,128)S(1)} %fusion.34), kind=kOutput, calls=%fused_computation.16 | convolution fusion | flops 3227516928 | bytes 10485760 | tf_op jit(solution)/shard_map/snab,snbc->snac/dot_general | solution.py:10
  349.7 16.2 %fusion.49 = (bf16[3,2,512,512]{3,2,1,0:T(8,128)(2,1)}, f32[3,2,512,512]{3,2,1,0:T(8,128)}) fusion(f32[512,512]{1,0:T(8,128)S(1)} %fusion.34, f32[3,2,512,512]{3,2,1,0:T(8,128)} %fusion.3, bf16[3,2,512,512]{3,2,1,0:T(8,128)(2,1)} %fusion.8, f32[3,2,512,512]{3,2,1,0:T(8,128)} %param.9), kind=kOutput, calls=%fused_computation.52 | convolution fusion | flops 4847566848 | bytes 26214400 | tf_op jit(solution)/shard_map/snab,snbc->snac/dot_general | solution.py:10
  365.8 0.0 copy-start.1
  365.8 5.6 %convolution_convert_fusion.1 = bf16[3,512,512]{2,1,0:T(8,128)(2,1)} fusion(bf16[3,2,512,512]{3,2,1,0:T(8,128)(2,1)} %get-tuple-element.2, bf16[3,512,512]{2,0,1:T(4,128)(2,1)} %copy-done.4), kind=kOutput, calls=%fused_computation.28 | convolution fusion | flops 1612185600 | bytes 6291456 | tf_op jit(solution)/shard_map/sab,sbc->sac/dot_general | solution.py:72
  371.4 0.0 copy-done.1
  (5 shorter events, 0.0 us)
Async XLA Ops:
  7.2 37.1 %copy-start = (bf16[256,1024]{1,0:T(8,128)(2,1)S(1)}, bf16[256,1024]{1,0:T(8,128)(2,1)}, u32[]{:S(2)}) copy-start(bf16[256,1024]{1,0:T(8,128)(2,1)} %param.6) | copy-start | bytes 1572868
  7.2 37.1 %all-gather.3.cloned.1.call-start = ((), (), s32[]{:S(2)}) async-start(), calls=%async_computation.1 | async-start | bytes 4718592 | tf_op jit(solution)/shard_map/all_gather | solution.py:24
  7.9 157.7 %reduce-scatter.2.cloned.1.call-start = ((), (), s32[]{:S(2)}) async-start(), calls=%async_computation.2 | async-start | bytes 17825792 | tf_op jit(solution)/shard_map/reduce_scatter | solution.py:28
  54.7 111.0 %copy-start.5 = (s32[16,16]{1,0:T(8,128)S(1)}, s32[16,16]{1,0:T(8,128)}, u32[]{:S(2)}) copy-start(s32[16,16]{1,0:T(8,128)} %param.8) | copy-start | bytes 3076
  54.7 111.0 %copy-start.6 = (s32[16,16]{1,0:T(8,128)S(1)}, s32[16,16]{1,0:T(8,128)}, u32[]{:S(2)}) copy-start(s32[16,16]{1,0:T(8,128)} %param.7) | copy-start | bytes 3076
  54.8 223.9 %all-gather.5.cloned.1.call-start = ((), (), s32[]{:S(2)}) async-start(), calls=%async_computation.3 | async-start | bytes 17825792 | tf_op jit(solution)/shard_map/all_gather | solution.py:37
  322.4 2.5 copy-start.4
  323.5 2.5 copy-start.2
  324.9 1.6 copy-start.3
  365.8 5.6 %copy-start.1 = (bf16[256,1024]{1,0:T(8,128)(2,1)S(1)}, bf16[256,1024]{1,0:T(8,128)(2,1)}, u32[]{:S(2)}) copy-start(bf16[256,1024]{1,0:T(8,128)(2,1)} %param.6) | copy-start | bytes 1572868
Sparse Core Ops, SparseCore 0:
  9.7 34.5 all-gather.2
  54.9 110.7 reduce-scatter.1
  167.8 110.8 all-gather.4
where the time goes:
time: 380 us; the launch traced here: 378 us
  waiting for transfers between devices  252 us (66%)
  matrix products  81.8 us (22%)
  local copies, waits for them, and re-layouts  28.9 us (8%)
  between operations  13.9 us (4%)
    reduce_scatter x1, waiting for transfers between devices, body(): lax.psum_scatter(lax.dot_general(features, grads_out, (((0,), (0,)), ((),...  111 us
    all_gather x1, waiting for transfers between devices, body(): fragment = lax.all_gather(home_rows, 'fsdp', axis=0, tiled=True)  104 us
    dot_general x4, matrix products, multiply(): jnp.einsum('snab,snbc->snac', first_arg.astype(jnp.bfloat16), second_arg....  47.4 us
    all_gather x1, waiting for transfers between devices, body(): features = lax.all_gather(inputs, 'pre', axis=1, tiled=True)  36.3 us
    reshape x1, local copies, waits for them, and re-layouts, body(): fragment.reshape(count_blocks, block_size, col_blocks, block_size)  27.8 us
    dot_general x1, matrix products, body(): jnp.einsum('rcs,racb->sab', chosen, fragment_tiles, preferred_element_typ...  16 us
    dot_general x1, matrix products, body(): lax.dot_general(features, grads_out, (((0,), (0,)), ((), ())), preferred_...  10.5 us
  transfers between devices with their start and end apart: 3, of which 3 were waited for; matrix products, arithmetic and copies ran while one was open for 2% of the time, Pallas kernels for 0%

commit v1 on v0

v1 whole, which is shorter than its diff:
```python
import jax
import jax.numpy as jnp
from jax import lax
from jax.experimental import pallas as pl
from jax.experimental.pallas import tpu as pltpu
from jax.sharding import PartitionSpec as P

ITERS = 2
BF = jnp.bfloat16
F32 = jnp.float32
VMEM = 56 * 1024 * 1024


def dot(a, b):
    return jnp.dot(a, b, preferred_element_type=F32)


def params(**kw):
    return pltpu.CompilerParams(vmem_limit_bytes=VMEM, **kw)


def split_kernel(a_ref, o_ref):
    pieces, rows, tokens = o_ref.shape
    half = rows // 2
    flipped = a_ref[...].T
    for r in range(2):
        for f in range(pieces):
            start = r * pieces * half + f * half
            o_ref[f, r * half : (r + 1) * half, :] = flipped[start : start + half, :]


def split_features(a):
    tokens, feats = a.shape
    return pl.pallas_call(
        split_kernel,
        out_shape=jax.ShapeDtypeStruct((16, feats // 16, tokens), BF),
        compiler_params=params(),
    )(a)


def fourth_kernel(x_ref, xb_ref, f_ref):
    xb = x_ref[0].astype(BF)
    xb_ref[0] = xb
    sq = dot(xb, xb).astype(BF)
    f_ref[0] = dot(sq, sq).astype(BF)


def fourth_powers(roots):
    n, b, _ = roots.shape
    spec = pl.BlockSpec((1, b, b), lambda i: (i, 0, 0))
    return pl.pallas_call(
        fourth_kernel,
        grid=(n,),
        in_specs=[spec],
        out_specs=[spec, spec],
        out_shape=[jax.ShapeDtypeStruct((n, b, b), BF)] * 2,
        compiler_params=params(),
        cost_estimate=pl.CostEstimate(flops=4 * n * b**3, bytes_accessed=8 * n * b * b, transcendentals=0),
    )(roots)


def grad_kernel(me_ref, owner_ref, offs_ref, *refs):
    a_refs, (b_ref, o_ref, acc) = refs[:-3], refs[-3:]
    step = pl.program_id(0)
    chunk = a_refs[0].shape[0]
    rows = a_refs[0].shape[1]
    lhs = jnp.concatenate(
        [jnp.concatenate([a[j] for a in a_refs], axis=0) for j in range(chunk)], axis=1
    )
    part = dot(lhs, b_ref[...].reshape(lhs.shape[1], -1))

    @pl.when(step == 0)
    def _():
        acc[...] = part

    @pl.when(step > 0)
    def _():
        acc[...] += part

    @pl.when(step == pl.num_programs(0) - 1)
    def _():
        o_ref[...] = jnp.zeros_like(o_ref)
        me = me_ref[0]
        half = rows // 2
        block = o_ref.shape[2]
        for j in range(len(a_refs)):
            dx, dc = j // 2, j % 2
            p = 2 * lax.rem(me // 2 + dx, 4) + lax.rem(me % 2 + dc, 2)
            for r in range(2):
                for c in range(2):
                    key = owner_ref[2 * p + r, 2 * me + c] * 3 + offs_ref[2 * p + r, 2 * me + c]
                    o_ref[key] = acc[
                        j * rows + r * half : j * rows + (r + 1) * half, c * block : (c + 1) * block
                    ].astype(BF)


def gradient_pieces(me, owner, offsets, a_list, b):
    n, rows, tokens = a_list[0].shape
    cols = b.shape[1]
    chunk = 4
    smem = pl.BlockSpec(memory_space=pltpu.SMEM)
    return pl.pallas_call(
        grad_kernel,
        grid=(n // chunk,),
        in_specs=[smem] * 3
        + [pl.BlockSpec((chunk, rows, tokens), lambda i: (i, 0, 0))] * len(a_list)
        + [pl.BlockSpec((chunk * tokens, cols), lambda i: (i, 0))],
        out_specs=pl.BlockSpec((48, rows // 2, cols // 2), lambda i: (0, 0, 0)),
        out_shape=jax.ShapeDtypeStruct((48, rows // 2, cols // 2), BF),
        scratch_shapes=[pltpu.VMEM((len(a_list) * rows, cols), F32)],
        compiler_params=params(),
    )(me, owner, offsets, *a_list, b)


def newton_kernel(g_ref, xb_ref, f_ref, u_ref, n_ref):
    size = g_ref.shape[3]
    g = g_ref[...].reshape(size, size)
    gt = g.T
    g32 = g.astype(F32)
    scale = 0.1 / (jnp.sum(g32 * g32) / size + 1e-6)
    eye = (
        lax.broadcasted_iota(jnp.int32, (size, size), 0) == lax.broadcasted_iota(jnp.int32, (size, size), 1)
    ).astype(F32)
    roots = []
    for k in range(2):
        stat = dot(g, gt) if k == 0 else dot(gt, g)
        damped = (stat * scale + eye).astype(BF)
        m = dot(f_ref[0, k], damped)
        x = xb_ref[0, k]
        for it in range(ITERS):
            f = ((5.0 * eye - m) * 0.25).astype(BF)
            x32 = dot(x, f)
            x = x32.astype(BF)
            if it < ITERS - 1:
                f2 = dot(f, f).astype(BF)
                f4 = dot(f2, f2).astype(BF)
                m = dot(f4, m.astype(BF))
        n_ref[0, k] = x32
        roots.append(x)
    u_ref[0] = dot(dot(roots[0], g).astype(BF), roots[1]).astype(BF)


def newton(pieces, roots, fourth):
    n_src, slots, rows, b = pieces.shape
    pair = pl.BlockSpec((1, 2, b, b), lambda i: (i, 0, 0, 0))
    return pl.pallas_call(
        newton_kernel,
        grid=(slots,),
        in_specs=[pl.BlockSpec((n_src, 1, rows, b), lambda i: (0, i, 0, 0)), pair, pair],
        out_specs=[pl.BlockSpec((1, b, b), lambda i: (i, 0, 0)), pair],
        out_shape=[
            jax.ShapeDtypeStruct((slots, b, b), BF),
            jax.ShapeDtypeStruct((slots, 2, b, b), F32),
        ],
        compiler_params=params(),
    )(pieces, roots, fourth)


def gather_over_pre(s):
    up = [(2 * a + c, 2 * ((a + 1) % 4) + c) for a in range(4) for c in range(2)]
    down = [(b, a) for a, b in up]
    swap = [(2 * a + c, 2 * a + 1 - c) for a in range(4) for c in range(2)]
    h = s.shape[0] // 2
    from_below = lax.ppermute(s, "pre", up)
    from_above = lax.ppermute(s, "pre", down)
    far_a = lax.ppermute(from_below[:h], "pre", up)
    far_b = lax.ppermute(from_above[h:], "pre", down)
    far = jnp.concatenate([far_a, far_b], axis=0)
    out = []
    for one in (s, from_above, far, from_below):
        out += [one, lax.ppermute(one, "pre", swap)]
    return out


def body(inputs, grads_out, owner, offsets, prev_roots):
    slots, _, b, _ = prev_roots.shape
    tokens = inputs.shape[0]
    me = lax.axis_index("pre").astype(jnp.int32).reshape(1)
    b_all = lax.all_gather(grads_out, "fsdp", axis=0, tiled=True)
    mine = split_features(inputs)
    mine = lax.all_to_all(mine, "fsdp", 0, 0, tiled=True)
    a_list = gather_over_pre(mine)
    xb, fourth = fourth_powers(prev_roots.reshape(slots * 2, b, b))
    pieces = gradient_pieces(me, owner, offsets, a_list, b_all)
    pieces = lax.all_to_all(pieces, "fsdp", 0, 0, tiled=True)
    update, roots = newton(
        pieces.reshape(16, slots, -1, b), xb.reshape(slots, 2, b, b), fourth.reshape(slots, 2, b, b)
    )
    return update, roots


def solution(mesh):
    in_specs = (P("fsdp", "pre"), P("fsdp", "pre"), P(), P(), P(("fsdp", "pre"), None, None, None))
    out_specs = (P(("fsdp", "pre"), None, None), P(("fsdp", "pre"), None, None, None))
    return jax.shard_map(body, mesh=mesh, in_specs=in_specs, out_specs=out_specs, check_vma=False)
```

time: 380 us -> 150 us (0.39)
  waiting for transfers between devices: 252 us -> 62.9 us
  matrix products: 81.8 us -> 0 us
  Pallas kernels: 0 us -> 38.8 us
  local copies, waits for them, and re-layouts: 28.9 us -> 1.24 us
  blocking collectives: 0 us -> 20.1 us
  starting transfers between devices: 0.12 us -> 12.5 us
    reduce_scatter x1 -> x0, waiting for transfers between devices: 111 us -> none  [body(): lax.psum_scatter(lax.dot_general(features, grads_out, (((0,), (0,)), ((),...]
    all_gather x2 -> x1, waiting for transfers between devices: 140 us -> 30.7 us  [body(): b_all = lax.all_gather(grads_out, 'fsdp', axis=0, tiled=True)]
    dot_general x9 -> x0, matrix products: 81.8 us -> none  [the longest x4 47.4 us: multiply(): jnp.einsum('snab,snbc->snac', first_arg.astype(jnp.bfloat16), second_arg....]
    pallas_call x0 -> x4, Pallas kernels: none -> 38.8 us  [the longest x1 18.6 us: newton(): pl.pallas_call(newton_kernel, grid=(slots,), in_specs=[pl.BlockSpec((n_sr...]
    reshape x1 -> x0, local copies, waits for them, and re-layouts: 27.8 us -> none  [body(): fragment.reshape(count_blocks, block_size, col_blocks, block_size)]
    all_to_all x0 -> x1, blocking collectives: none -> 20.1 us  [body(): mine = lax.all_to_all(mine, 'fsdp', 0, 0, tiled=True)]
    all_to_all x0 -> x1, waiting for transfers between devices: none -> 16 us  [body(): pieces = lax.all_to_all(pieces, 'fsdp', 0, 0, tiled=True)]
    ppermute x0 -> x8, waiting for transfers between devices: none -> 15.6 us  [the longest x1 9.85 us: gather_over_pre(): from_below = lax.ppermute(s, 'pre', up)]
  transfers between devices with their start and end apart: 3 -> 10, of which waited for: 3 -> 5; matrix products, arithmetic and copies ran while one was open for 2% -> 0% of each run, Pallas kernels for 0% -> 7%
where the time goes in v1:
time: 150 us
  waiting for transfers between devices  62.9 us (42%)
  Pallas kernels  38.8 us (26%)
  blocking collectives  20.1 us (13%)
  between operations  14.2 us (9%)
  starting transfers between devices  12.5 us (8%)
    all_gather x1, waiting for transfers between devices, body(): b_all = lax.all_gather(grads_out, 'fsdp', axis=0, tiled=True)  30.7 us
    all_to_all x1, blocking collectives, body(): mine = lax.all_to_all(mine, 'fsdp', 0, 0, tiled=True)  20.1 us
    pallas_call x1, Pallas kernels, newton(): pl.pallas_call(newton_kernel, grid=(slots,), in_specs=[pl.BlockSpec((n_sr...  18.6 us
    all_to_all x1, waiting for transfers between devices, body(): pieces = lax.all_to_all(pieces, 'fsdp', 0, 0, tiled=True)  16 us
    ppermute x1, waiting for transfers between devices, gather_over_pre(): from_below = lax.ppermute(s, 'pre', up)  9.85 us
    pallas_call x1, Pallas kernels, gradient_pieces(): pl.pallas_call(grad_kernel, grid=(n // chunk,), in_specs=[smem] * 3 + [pl...  9.75 us
    pallas_call x1, Pallas kernels, fourth_powers(): pl.pallas_call(fourth_kernel, grid=(n,), in_specs=[spec], out_specs=[spec...  8.46 us
    all_to_all x1, starting transfers between devices, body(): pieces = lax.all_to_all(pieces, 'fsdp', 0, 0, tiled=True)  5.29 us
  transfers between devices with their start and end apart: 10, of which 5 were waited for; matrix products, arithmetic and copies ran while one was open for 0% of the time, Pallas kernels for 7%

profile of v1, /device:TPU:0, one launch (start us, length us, event | category | flops | bytes accessed | tf_op | source)
XLA Modules:
  0.0 149.8 jit_solution(2908220697680600566)
XLA Ops:
  7.2 0.0 all-gather.2.cloned.1.call-start
  7.2 0.7 all-gather.2.cloned.1.call-update
  7.9 2.0 %shard_map.68 = bf16[16,64,256]{2,1,0:T(8,128)(2,1)} custom-call(bf16[256,1024]{1,0:T(8,128)(2,1)} %a_ref.1), custom_call_target="tpu_custom_call" | custom-call | tf_op jit(solution)/shard_map/pallas_call | solution.py:34
  9.9 20.1 %all_to_all.10.refs_0_ = bf16[16,64,256]{2,1,0:T(8,128)(2,1)S(1)} all-to-all(bf16[16,64,256]{2,1,0:T(8,128)(2,1)} %shard_map.68), channel_id=1, replica_groups=mesh['fsdp'=16,'pre'=8] {'fsdp'}, dimensions={0} | all-to-all | bytes 1048576 | tf_op jit(solution)/shard_map/all_to_all | solution.py:181
  30.1 0.0 copy-start.1
  30.1 1.5 %collective-permute-start.3 = (bf16[16,64,256]{2,1,0:T(8,128)(2,1)S(1)}, bf16[16,64,256]{2,1,0:T(8,128)(2,1)S(1)}, u32[]{:S(2)}, u32[]{:S(2)}) collective-permute-start(bf16[16,64,256]{2,1,0:T(8,128)(2,1)S(1)} %all_to_all.10.refs_0_), channel_id=1, source_target_pairs={{0,2},{1,3},{2,4},{3,5},{4,6},{5,7},{6,0},{7,1},{8,10},{9,11},{10,... | collective-permute-start | bytes 1572872 | tf_op jit(solution)/shard_map/ppermute | solution.py:164
  31.6 1.7 %collective-permute-start.1 = (bf16[16,64,256]{2,1,0:T(8,128)(2,1)S(1)}, bf16[16,64,256]{2,1,0:T(8,128)(2,1)S(1)}, u32[]{:S(2)}, u32[]{:S(2)}) collective-permute-start(bf16[16,64,256]{2,1,0:T(8,128)(2,1)S(1)} %all_to_all.10.refs_0_), channel_id=1, source_target_pairs={{2,0},{3,1},{4,2},{5,3},{6,4},{7,5},{0,6},{1,7},{10,8},{11,9},{12,... | collective-permute-start | bytes 1572872 | tf_op jit(solution)/shard_map/ppermute | solution.py:165
  33.3 9.8 %collective-permute-done.3.refs_6_ = bf16[16,64,256]{2,1,0:T(8,128)(2,1)S(1)} collective-permute-done((bf16[16,64,256]{2,1,0:T(8,128)(2,1)S(1)}, bf16[16,64,256]{2,1,0:T(8,128)(2,1)S(1)}, u32[]{:S(2)}, u32[]{:S(2)}) %collective-permute-start.3) | collective-permute-done | bytes 524320 | tf_op jit(solution)/shard_map/ppermute | solution.py:164
  43.2 0.0 copy-start.2
  43.2 0.5 collective-permute-start.4
  43.6 0.0 collective-permute-done.1.refs_2_
  43.7 0.0 copy-start.3
  43.7 2.9 %collective-permute-start.5 = (bf16[8,64,256]{2,1,0:T(8,128)(2,1)S(1)}, bf16[8,64,256]{2,1,0:T(8,128)(2,1)S(1)}, u32[]{:S(2)}, u32[]{:S(2)}) collective-permute-start(bf16[8,64,256]{2,1,0:T(8,128)(2,1)S(1)} %slice.9), channel_id=1, source_target_pairs={{2,0},{3,1},{4,2},{5,3},{6,4},{7,5},{0,6},{1,7},{10,8},{11,9},{12,... | collective-permute-start | bytes 786440 | tf_op jit(solution)/shard_map/ppermute | solution.py:167
  46.6 0.0 collective-permute-start
  46.6 0.5 collective-permute-start.7
  47.1 0.0 collective-permute-start.2
  47.1 3.7 %collective-permute-done.4 = bf16[8,64,256]{2,1,0:T(8,128)(2,1)S(1)} collective-permute-done((bf16[8,64,256]{2,1,0:T(8,128)(2,1)S(1)}, bf16[8,64,256]{2,1,0:T(8,128)(2,1)S(1)}, u32[]{:S(2)}, u32[]{:S(2)}) %collective-permute-start.4) | collective-permute-done | bytes 262176 | tf_op jit(solution)/shard_map/ppermute | solution.py:166
  50.9 0.0 collective-permute-done.5
  50.9 0.0 copy-start.4
  50.9 0.1 collective-permute-start.6
  51.0 0.0 collective-permute-done.refs_1_
  51.0 0.0 copy-start.5
  51.0 0.0 collective-permute-done.7.refs_7_
  51.0 0.0 copy-start.6
  51.0 0.0 collective-permute-done.2.refs_3_
  51.1 2.0 %collective-permute-done.6.refs_5_ = bf16[16,64,256]{2,1,0:T(8,128)(2,1)} collective-permute-done((bf16[16,64,256]{2,1,0:T(8,128)(2,1)S(1)}, bf16[16,64,256]{2,1,0:T(8,128)(2,1)}, u32[]{:S(2)}, u32[]{:S(2)}) %collective-permute-start.6) | collective-permute-done | bytes 524320 | tf_op jit(solution)/shard_map/ppermute | solution.py:171
  53.0 30.7 %all-gather.2.cloned.1.call-done.refs_8_ = bf16[4096,1024]{1,0:T(8,128)(2,1)} async-done(((bf16[256,1024]{1,0:T(8,128)(2,1)}), bf16[4096,1024]{1,0:T(8,128)(2,1)}) %all-gather.2.cloned.1.call-update) | async-done | bytes 8388624 | tf_op jit(solution)/shard_map/all_gather | solution.py:179
  83.7 0.0 copy-done.1
  83.7 0.0 copy-done.2
  83.7 0.0 copy-done.3
  83.7 0.0 copy-done.4
  83.7 0.0 copy-done.5
  83.7 0.0 copy-done.6
  83.7 9.7 %shard_map.69 = bf16[48,32,512]{2,1,0:T(8,128)(2,1)} custom-call(s32[1]{0:T(128)} %bitcast.me_ref, s32[16,16]{1,0:T(8,128)} %owner_ref.1, s32[16,16]{1,0:T(8,128)} %offs_ref.1, bf16[16,64,256]{2,1,0:T(8,128)(2,1)} %copy-done.1, bf16[16,64,256]{2,1,0:T(8,128)(2,1)} %copy-done.5, bf16[16,64,256]{2,1,0:T(8,128)(2,1)} %copy-done.3, ...), custom_call_target="tpu_custom_call" | custom-call | tf_op jit(solution)/shard_map/pallas_call | solution.py:102
  93.5 5.3 %all-to-all-start.1 = ((bf16[48,32,512]{2,1,0:T(8,128)(2,1)}), bf16[48,32,512]{2,1,0:T(8,128)(2,1)S(1)}, u32[]{:S(2)}, u32[]{:S(2)}) async-start(bf16[48,32,512]{2,1,0:T(8,128)(2,1)} %shard_map.69), calls=%async_computation.1 | async-start | bytes 3145728 | tf_op jit(solution)/shard_map/all_to_all | solution.py:185
  98.8 8.5 %shard_map.70 = (bf16[6,512,512]{2,1,0:T(8,128)(2,1)}, bf16[6,512,512]{2,1,0:T(8,128)(2,1)}) custom-call(f32[6,512,512]{2,1,0:T(8,128)} %bitcast.8), custom_call_target="tpu_custom_call" | custom-call | flops 3221225472 | bytes 12582912 | tf_op jit(solution)/shard_map/pallas_call | solution.py:51
  107.2 16.0 %all-to-all-done.1 = bf16[48,32,512]{2,1,0:T(8,128)(2,1)S(1)} async-done(((bf16[48,32,512]{2,1,0:T(8,128)(2,1)}), bf16[48,32,512]{2,1,0:T(8,128)(2,1)S(1)}, u32[]{:S(2)}, u32[]{:S(2)}) %all-to-all-start.1) | async-done | bytes 1572896 | tf_op jit(solution)/shard_map/all_to_all | solution.py:185
  123.3 0.0 copy-start
  123.3 1.1 copy-done
  124.4 18.6 %shard_map.71 = (bf16[3,512,512]{2,1,0:T(8,128)(2,1)}, f32[3,2,512,512]{3,2,1,0:T(8,128)}) custom-call(bf16[16,3,32,512]{3,2,1,0:T(8,128)(2,1)} %bitcast.5, bf16[3,2,512,512]{3,2,1,0:T(8,128)(2,1)} %bitcast.6, bf16[3,2,512,512]{3,2,1,0:T(8,128)(2,1)} %bitcast.7), custom_call_target="tpu_custom_call" | custom-call | tf_op jit(solution)/shard_map/pallas_call | solution.py:146
  (4 shorter events, 0.1 us)
Async XLA Ops:
  7.2 76.5 %all-gather.2.cloned.1.call-start = ((), (), s32[]{:S(2)}) async-start(), calls=%async_computation.2 | async-start | bytes 8912896 | tf_op jit(solution)/shard_map/all_gather | solution.py:179
  30.1 53.6 %copy-start.1 = (bf16[16,64,256]{2,1,0:T(8,128)(2,1)}, bf16[16,64,256]{2,1,0:T(8,128)(2,1)S(1)}, u32[]{:S(2)}) copy-start(bf16[16,64,256]{2,1,0:T(8,128)(2,1)S(1)} %all_to_all.10.refs_0_) | copy-start | bytes 1572868
  30.1 13.1 %collective-permute-start.3 = (bf16[16,64,256]{2,1,0:T(8,128)(2,1)S(1)}, bf16[16,64,256]{2,1,0:T(8,128)(2,1)S(1)}, u32[]{:S(2)}, u32[]{:S(2)}) collective-permute-start(bf16[16,64,256]{2,1,0:T(8,128)(2,1)S(1)} %all_to_all.10.refs_0_), channel_id=1, source_target_pairs={{0,2},{1,3},{2,4},{3,5},{4,6},{5,7},{6,0},{7,1},{8,10},{9,11},{10,... | collective-permute-start | bytes 1572872 | tf_op jit(solution)/shard_map/ppermute | solution.py:164
  31.6 12.0 %collective-permute-start.1 = (bf16[16,64,256]{2,1,0:T(8,128)(2,1)S(1)}, bf16[16,64,256]{2,1,0:T(8,128)(2,1)S(1)}, u32[]{:S(2)}, u32[]{:S(2)}) collective-permute-start(bf16[16,64,256]{2,1,0:T(8,128)(2,1)S(1)} %all_to_all.10.refs_0_), channel_id=1, source_target_pairs={{2,0},{3,1},{4,2},{5,3},{6,4},{7,5},{0,6},{1,7},{10,8},{11,9},{12,... | collective-permute-start | bytes 1572872 | tf_op jit(solution)/shard_map/ppermute | solution.py:165
  43.2 40.6 %copy-start.2 = (bf16[16,64,256]{2,1,0:T(8,128)(2,1)}, bf16[16,64,256]{2,1,0:T(8,128)(2,1)S(1)}, u32[]{:S(2)}) copy-start(bf16[16,64,256]{2,1,0:T(8,128)(2,1)S(1)} %collective-permute-done.3.refs_6_) | copy-start | bytes 1572868
  43.2 7.7 %collective-permute-start.4 = (bf16[8,64,256]{2,1,0:T(8,128)(2,1)S(1)}, bf16[8,64,256]{2,1,0:T(8,128)(2,1)S(1)}, u32[]{:S(2)}, u32[]{:S(2)}) collective-permute-start(bf16[8,64,256]{2,1,0:T(8,128)(2,1)S(1)} %slice.8), channel_id=1, source_target_pairs={{0,2},{1,3},{2,4},{3,5},{4,6},{5,7},{6,0},{7,1},{8,10},{9,11},{10,... | collective-permute-start | bytes 786440 | tf_op jit(solution)/shard_map/ppermute | solution.py:166
  43.7 40.1 %copy-start.3 = (bf16[16,64,256]{2,1,0:T(8,128)(2,1)}, bf16[16,64,256]{2,1,0:T(8,128)(2,1)S(1)}, u32[]{:S(2)}) copy-start(bf16[16,64,256]{2,1,0:T(8,128)(2,1)S(1)} %collective-permute-done.1.refs_2_) | copy-start | bytes 1572868
  43.7 7.2 %collective-permute-start.5 = (bf16[8,64,256]{2,1,0:T(8,128)(2,1)S(1)}, bf16[8,64,256]{2,1,0:T(8,128)(2,1)S(1)}, u32[]{:S(2)}, u32[]{:S(2)}) collective-permute-start(bf16[8,64,256]{2,1,0:T(8,128)(2,1)S(1)} %slice.9), channel_id=1, source_target_pairs={{2,0},{3,1},{4,2},{5,3},{6,4},{7,5},{0,6},{1,7},{10,8},{11,9},{12,... | collective-permute-start | bytes 786440 | tf_op jit(solution)/shard_map/ppermute | solution.py:167
  46.6 4.4 %collective-permute-start = (bf16[16,64,256]{2,1,0:T(8,128)(2,1)S(1)}, bf16[16,64,256]{2,1,0:T(8,128)(2,1)S(1)}, u32[]{:S(2)}, u32[]{:S(2)}) collective-permute-start(bf16[16,64,256]{2,1,0:T(8,128)(2,1)S(1)} %all_to_all.10.refs_0_), channel_id=1, source_target_pairs={{0,1},{1,0},{2,3},{3,2},{4,5},{5,4},{6,7},{7,6},{8,9},{9,8},{10,11... | collective-permute-start | bytes 1572872 | tf_op jit(solution)/shard_map/ppermute | solution.py:171
  46.6 4.4 %collective-permute-start.7 = (bf16[16,64,256]{2,1,0:T(8,128)(2,1)S(1)}, bf16[16,64,256]{2,1,0:T(8,128)(2,1)S(1)}, u32[]{:S(2)}, u32[]{:S(2)}) collective-permute-start(bf16[16,64,256]{2,1,0:T(8,128)(2,1)S(1)} %collective-permute-done.3.refs_6_), channel_id=1, source_target_pairs={{0,1},{1,0},{2,3},{3,2},{4,5},{5,4},{6,7},{7,6},{8,9},{9,8},{10,11... | collective-permute-start | bytes 1572872 | tf_op jit(solution)/shard_map/ppermute | solution.py:171
  47.1 4.0 %collective-permute-start.2 = (bf16[16,64,256]{2,1,0:T(8,128)(2,1)S(1)}, bf16[16,64,256]{2,1,0:T(8,128)(2,1)}, u32[]{:S(2)}, u32[]{:S(2)}) collective-permute-start(bf16[16,64,256]{2,1,0:T(8,128)(2,1)S(1)} %collective-permute-done.1.refs_2_), channel_id=1, source_target_pairs={{0,1},{1,0},{2,3},{3,2},{4,5},{5,4},{6,7},{7,6},{8,9},{9,8},{10,11... | collective-permute-start | bytes 1572872 | tf_op jit(solution)/shard_map/ppermute | solution.py:171
  50.9 32.8 %copy-start.4 = (bf16[16,64,256]{2,1,0:T(8,128)(2,1)}, bf16[16,64,256]{2,1,0:T(8,128)(2,1)S(1)}, u32[]{:S(2)}) copy-start(bf16[16,64,256]{2,1,0:T(8,128)(2,1)S(1)} %constant_dynamic-update-slice_fusion.refs_4_) | copy-start | bytes 1572868
  50.9 2.1 %collective-permute-start.6 = (bf16[16,64,256]{2,1,0:T(8,128)(2,1)S(1)}, bf16[16,64,256]{2,1,0:T(8,128)(2,1)}, u32[]{:S(2)}, u32[]{:S(2)}) collective-permute-start(bf16[16,64,256]{2,1,0:T(8,128)(2,1)S(1)} %constant_dynamic-update-slice_fusion.refs_4_), channel_id=1, source_target_pairs={{0,1},{1,0},{2,3},{3,2},{4,5},{5,4},{6,7},{7,6},{8,9},{9,8},{10,11... | collective-permute-start | bytes 1572872 | tf_op jit(solution)/shard_map/ppermute | solution.py:171
  51.0 32.7 %copy-start.5 = (bf16[16,64,256]{2,1,0:T(8,128)(2,1)}, bf16[16,64,256]{2,1,0:T(8,128)(2,1)S(1)}, u32[]{:S(2)}) copy-start(bf16[16,64,256]{2,1,0:T(8,128)(2,1)S(1)} %collective-permute-done.refs_1_) | copy-start | bytes 1572868
  51.0 32.7 %copy-start.6 = (bf16[16,64,256]{2,1,0:T(8,128)(2,1)}, bf16[16,64,256]{2,1,0:T(8,128)(2,1)S(1)}, u32[]{:S(2)}) copy-start(bf16[16,64,256]{2,1,0:T(8,128)(2,1)S(1)} %collective-permute-done.7.refs_7_) | copy-start | bytes 1572868
  93.5 29.8 %all-to-all-start.1 = ((bf16[48,32,512]{2,1,0:T(8,128)(2,1)}), bf16[48,32,512]{2,1,0:T(8,128)(2,1)S(1)}, u32[]{:S(2)}, u32[]{:S(2)}) async-start(bf16[48,32,512]{2,1,0:T(8,128)(2,1)} %shard_map.69), calls=%async_computation.1 | async-start | bytes 3145728 | tf_op jit(solution)/shard_map/all_to_all | solution.py:185
  123.3 1.1 copy-start
Sparse Core Ops, SparseCore 0:
  10.1 73.5 all-gather.1

commit v2 on v1

v2 whole, which is shorter than its diff:
```python
import jax
import jax.numpy as jnp
from jax import lax
from jax.experimental import pallas as pl
from jax.experimental.pallas import tpu as pltpu
from jax.sharding import PartitionSpec as P

ITERS = 2
BF = jnp.bfloat16
F32 = jnp.float32
VMEM = 20 * 1024 * 1024
SHORT = pl.CostEstimate(flops=1, bytes_accessed=1, transcendentals=0)


def dot(a, b):
    return jnp.dot(a, b, preferred_element_type=F32)


def params(**kw):
    return pltpu.CompilerParams(vmem_limit_bytes=VMEM, **kw)


def split_kernel(core_ref, a_ref, r_ref, o_ref):
    pieces, rows, tokens = o_ref.shape
    part = rows // 4
    start = pl.multiple_of(core_ref[0] * tokens, tokens)
    for o in range(2):
        flipped = (a_ref[pl.ds(start, tokens), :] if o == 0 else r_ref[0]).T
        for r in range(2):
            for f in range(pieces):
                at, to = (r * pieces + f) * part, (2 * o + r) * part
                o_ref[f, to : to + part, :] = flipped[at : at + part, :]


def split_features(core, a, recv):
    tokens, feats = a.shape
    whole = lambda s: pl.BlockSpec(s, lambda i: (0,) * len(s))
    return pl.pallas_call(
        split_kernel,
        grid=(1,),
        in_specs=[pl.BlockSpec(memory_space=pltpu.SMEM), whole(a.shape), whole((1,) + recv.shape[1:])],
        out_specs=whole((16, feats // 8, tokens // 2)),
        out_shape=jax.ShapeDtypeStruct((16, feats // 8, tokens // 2), BF),
        compiler_params=params(),
        cost_estimate=SHORT,
    )(core, a, recv)


def fourth_kernel(x_ref, xb_ref, f_ref):
    xb = x_ref[0].astype(BF)
    xb_ref[0] = xb
    sq = dot(xb, xb).astype(BF)
    f_ref[0] = dot(sq, sq).astype(BF)


def fourth_powers(roots):
    n, b, _ = roots.shape
    spec = pl.BlockSpec((1, b, b), lambda i: (i, 0, 0))
    return pl.pallas_call(
        fourth_kernel,
        grid=(n,),
        in_specs=[spec],
        out_specs=[spec, spec],
        out_shape=[jax.ShapeDtypeStruct((n, b, b), BF)] * 2,
        compiler_params=params(),
        cost_estimate=SHORT,
    )(roots)


def join_kernel(*refs):
    for i, v in enumerate(refs[:-1]):
        refs[-1][i] = v[0]


def join(parts):
    n, rows, cols = parts[0].shape
    return pl.pallas_call(
        join_kernel,
        grid=(n,),
        in_specs=[pl.BlockSpec((1, rows, cols), lambda i: (i, 0, 0))] * len(parts),
        out_specs=pl.BlockSpec((len(parts), rows, cols), lambda i: (i, 0, 0)),
        out_shape=jax.ShapeDtypeStruct((n * len(parts), rows, cols), BF),
        compiler_params=params(),
        cost_estimate=SHORT,
    )(*parts)


def token_pieces(place_ref, j):
    z, y, core = place_ref[0], place_ref[1], place_ref[3]
    out = []
    for i in range(4):
        dz = jnp.where(core == 0, j, i)
        dy = jnp.where(core == 0, i, j)
        out.append(lax.rem(z + dz, 4) * 4 + lax.rem(y + dy, 4))
    return out


def left_operand(place_ref, a_refs, j):
    at = token_pieces(place_ref, j)
    rows = [jnp.concatenate([a[f] for f in at], axis=1) for a in a_refs]
    return jnp.concatenate(rows, axis=0)


def product(lhs, b):
    return dot(lhs, b.reshape(lhs.shape[1], b.shape[-1]))


def first_kernel(place_ref, *refs):
    a_refs, b_refs, o_ref, lhs = refs[:4], refs[4:7], refs[7], refs[-1]

    @pl.when(pl.program_id(0) == 0)
    def _():
        for n, j in enumerate((0, 1, 3)):
            lhs[n] = left_operand(place_ref, a_refs, j)
        if len(refs) == 10:
            refs[8][...] = left_operand(place_ref, a_refs, 2)

    o_ref[...] = sum(product(lhs[n], b_refs[n][...]) for n in range(3)).astype(o_ref.dtype)


def first_chunks(place, a_list, chunks, other):
    n, rows, tokens = a_list[0].shape
    cols = chunks[0].shape[-1]
    width = cols // 4
    full = (4 * rows, 4 * tokens)
    out_specs = [pl.BlockSpec((4 * rows, width), lambda i: (0, i))]
    out_shape = [jax.ShapeDtypeStruct((4 * rows, cols), BF if other else F32)]
    if other:
        out_specs.append(pl.BlockSpec(full, lambda i: (0, 0)))
        out_shape.append(jax.ShapeDtypeStruct(full, BF))
    return pl.pallas_call(
        first_kernel,
        grid=(cols // width,),
        in_specs=[pl.BlockSpec(memory_space=pltpu.SMEM)]
        + [pl.BlockSpec((n, rows, tokens), lambda i: (0, 0, 0))] * 4
        + [pl.BlockSpec((4, tokens, width), lambda i: (int(other), 0, i))] * 3,
        out_specs=out_specs,
        out_shape=out_shape,
        scratch_shapes=[pltpu.VMEM((3,) + full, BF)],
        compiler_params=params(),
        cost_estimate=SHORT,
    )(place, *a_list, *chunks)


def last_kernel(place_ref, owner_ref, offs_ref, lhs_ref, cross_ref, own_ref, far_ref, acc_ref, share_ref, o_ref):
    x, core = place_ref[2], place_ref[3]
    part, block = o_ref.shape[1:]
    o_ref[...] = jnp.zeros_like(o_ref)
    for c in range(2):
        at_cols = slice(c * block, (c + 1) * block)
        total = acc_ref[:, at_cols] + product(lhs_ref[...], own_ref[:, :, at_cols])
        cross = share_ref[:, at_cols].astype(F32) + product(cross_ref[...], far_ref[:, :, at_cols])
        col = 2 * (2 * x + core) + c
        for dx in range(4):
            for o in range(2):
                p = 2 * lax.rem(x + dx, 4) + lax.rem(core + o, 2)
                for r in range(2):
                    at = ((dx * 2 + o) * 2 + r) * part
                    to = ((dx * 2 + 1 - o) * 2 + r) * part
                    row = 2 * p + r
                    key = owner_ref[row, col] * 3 + offs_ref[row, col]
                    o_ref[key] = (total[at : at + part] + cross[to : to + part]).astype(BF)


def last_chunk(place, owner, offsets, lhs, cross_lhs, own, far, acc, share):
    rows, cols = acc.shape
    operands = (lhs, cross_lhs, own, far, acc, share)
    return pl.pallas_call(
        last_kernel,
        grid=(1,),
        in_specs=[pl.BlockSpec(memory_space=pltpu.SMEM)] * 3
        + [pl.BlockSpec(v.shape, lambda i, n=v.ndim: (0,) * n) for v in operands],
        out_specs=pl.BlockSpec((48, rows // 16, cols // 2), lambda i: (0, 0, 0)),
        out_shape=jax.ShapeDtypeStruct((48, rows // 16, cols // 2), BF),
        compiler_params=params(),
        cost_estimate=SHORT,
    )(place, owner, offsets, *operands)


def newton_kernel(g_ref, xb_ref, f_ref, u_ref, n_ref):
    size = g_ref.shape[3]
    g = g_ref[...].reshape(size, size)
    gt = g.T
    g32 = g.astype(F32)
    scale = 0.1 / (jnp.sum(g32 * g32) / size + 1e-6)
    eye = (
        lax.broadcasted_iota(jnp.int32, (size, size), 0) == lax.broadcasted_iota(jnp.int32, (size, size), 1)
    ).astype(F32)
    roots = []
    for k in range(2):
        stat = dot(g, gt) if k == 0 else dot(gt, g)
        damped = (stat * scale + eye).astype(BF)
        m = dot(f_ref[0, k], damped)
        x = xb_ref[0, k]
        for it in range(ITERS):
            f = ((5.0 * eye - m) * 0.25).astype(BF)
            x32 = dot(x, f)
            x = x32.astype(BF)
            if it < ITERS - 1:
                f2 = dot(f, f).astype(BF)
                f4 = dot(f2, f2).astype(BF)
                m = dot(f4, m.astype(BF))
        n_ref[0, k] = x32
        roots.append(x)
    u_ref[0] = dot(dot(roots[0], g).astype(BF), roots[1]).astype(BF)


def newton(pieces, roots, fourth):
    n_src, slots, rows, b = pieces.shape
    pair = pl.BlockSpec((1, 2, b, b), lambda i: (i, 0, 0, 0))
    return pl.pallas_call(
        newton_kernel,
        grid=(slots,),
        in_specs=[pl.BlockSpec((n_src, 1, rows, b), lambda i: (0, i, 0, 0)), pair, pair],
        out_specs=[pl.BlockSpec((1, b, b), lambda i: (i, 0, 0)), pair],
        out_shape=[
            jax.ShapeDtypeStruct((slots, b, b), BF),
            jax.ShapeDtypeStruct((slots, 2, b, b), F32),
        ],
        compiler_params=params(),
        cost_estimate=SHORT,
    )(pieces, roots, fourth)


def device(z, y, x, core):
    return ((z % 4) * 4 + y % 4) * 8 + (x % 4) * 2 + core


def chips():
    return [(z, y, x) for z in range(4) for y in range(4) for x in range(4)]


def swap_cores(v):
    return lax.ppermute(
        v, ("fsdp", "pre"), [(device(*p, c), device(*p, 1 - c)) for p in chips() for c in range(2)]
    )


def from_x(v, d):
    return lax.ppermute(
        v, ("fsdp", "pre"), [(device(z, y, x + d, c), device(z, y, x, c)) for z, y, x in chips() for c in range(2)]
    )


def from_ring(v, phase, d):
    pairs = []
    for z, y, x in chips():
        for c in range(2):
            dz, dy = (0, d) if phase == c else (d, 0)
            pairs.append((device(z + dz, y + dy, x, c), device(z, y, x, c)))
    return lax.ppermute(v, ("fsdp", "pre"), pairs)


def from_ring_across(v, d):
    pairs = []
    for z, y, x in chips():
        for c in range(2):
            dz, dy = (0, d) if c == 0 else (d, 0)
            pairs.append((device(z + dz, y + dy, x, 1 - c), device(z, y, x, c)))
    return lax.ppermute(v, ("fsdp", "pre"), pairs)


def body(inputs, grads_out, owner, offsets, prev_roots):
    slots, _, b, _ = prev_roots.shape
    tokens, cols = grads_out.shape
    half = tokens // 2
    f = lax.axis_index("fsdp").astype(jnp.int32)
    p = lax.axis_index("pre").astype(jnp.int32)
    core = p % 2
    place = jnp.stack([f // 4, f % 4, p // 2, core])
    rows_of = lambda v, c: lax.dynamic_slice_in_dim(v, c * half, half, 0)

    sent = jnp.stack([rows_of(inputs, 1 - core), rows_of(grads_out, 1 - core)])
    recv = swap_cores(sent)
    shard = jnp.stack([rows_of(grads_out, core), recv[1]])

    near = [shard, from_ring(shard, 0, 1), from_ring(shard, 0, 2), from_ring(shard, 0, 3)]
    both = join(near)

    mine = split_features(core.reshape(1), inputs, recv)
    mine = lax.all_to_all(mine, "fsdp", 0, 0, tiled=True)
    both, mine = lax.optimization_barrier((both, mine))
    up = from_ring(both, 1, 1)
    down = from_ring(both, 1, 3)
    a_list = [mine, from_x(mine, 1), from_x(mine, 2), from_x(mine, 3)]
    own_2 = from_ring(up[:4], 1, 1)
    far_2 = from_ring_across(down[4:], 3)

    xb, fourth = fourth_powers(prev_roots.reshape(slots * 2, b, b))
    share, lhs = first_chunks(place, a_list, [both, up, down], True)
    (acc,) = first_chunks(place, a_list, [both, up, down], False)
    pieces = last_chunk(
        place, owner, offsets, lhs, swap_cores(lhs), own_2, far_2, acc, swap_cores(share)
    )
    pieces = lax.all_to_all(pieces, "fsdp", 0, 0, tiled=True)
    update, roots = newton(
        pieces.reshape(16, slots, -1, b), xb.reshape(slots, 2, b, b), fourth.reshape(slots, 2, b, b)
    )
    return update, roots


def solution(mesh):
    in_specs = (P("fsdp", "pre"), P("fsdp", "pre"), P(), P(), P(("fsdp", "pre"), None, None, None))
    out_specs = (P(("fsdp", "pre"), None, None), P(("fsdp", "pre"), None, None, None))
    return jax.shard_map(body, mesh=mesh, in_specs=in_specs, out_specs=out_specs, check_vma=False)
```

time: 150 us -> 130 us (0.87)
  blocking collectives: 20.1 us -> 0 us
  waiting for transfers between devices: 62.9 us -> 43.8 us
  local copies, waits for them, and re-layouts: 1.24 us -> 19.2 us
  starting transfers between devices: 12.5 us -> 30 us
  between operations: 14.2 us -> 0.84 us
  Pallas kernels: 38.8 us -> 35.7 us
    all_gather x1 -> x0, waiting for transfers between devices: 30.7 us -> none  [body(): b_all = lax.all_gather(grads_out, 'fsdp', axis=0, tiled=True)]
    all_to_all x1 -> x0, blocking collectives: 20.1 us -> none  [body(): mine = lax.all_to_all(mine, 'fsdp', 0, 0, tiled=True)]
    unnamed x15 -> x28, local copies, waits for them, and re-layouts: 1.19 us -> 15.4 us
    ppermute x8 -> x13, waiting for transfers between devices: 15.6 us -> 27.9 us  [the longest x6 24.7 us: from_ring(): return lax.ppermute(v, ('fsdp', 'pre'), pairs)]
    ppermute x8 -> x13, starting transfers between devices: 7.21 us -> 18.3 us  [the longest x6 11.1 us: from_ring(): return lax.ppermute(v, ('fsdp', 'pre'), pairs)]
    all_to_all x0 -> x1, starting transfers between devices: none -> 5.53 us  [body(): mine = lax.all_to_all(mine, 'fsdp', 0, 0, tiled=True)]
    pallas_call x1, Pallas kernels: 8.46 us -> 4.81 us  [fourth_powers(): pl.pallas_call(fourth_kernel, grid=(n,), in_specs=[spec], out_specs=[spec...]
    all_to_all x1, waiting for transfers between devices: 16 us -> 13.1 us  [body(): pieces = lax.all_to_all(pieces, 'fsdp', 0, 0, tiled=True)]
  transfers between devices with their start and end apart: 10 -> 15, of which waited for: 5 -> 7; matrix products, arithmetic and copies ran while one was open for 0% -> 2% of each run, Pallas kernels for 7% -> 12%
where the time goes in v2:
time: 130 us
  waiting for transfers between devices  43.8 us (34%)
  Pallas kernels  35.7 us (27%)
  starting transfers between devices  30 us (23%)
  local copies, waits for them, and re-layouts  19.2 us (15%)
    ppermute x6, waiting for transfers between devices, from_ring(): return lax.ppermute(v, ('fsdp', 'pre'), pairs)  24.7 us
    pallas_call x1, Pallas kernels, newton(): pl.pallas_call(newton_kernel, grid=(slots,), in_specs=[pl.BlockSpec((n_sr...  17 us
    unnamed x28, local copies, waits for them, and re-layouts  15.4 us
    all_to_all x1, waiting for transfers between devices, body(): pieces = lax.all_to_all(pieces, 'fsdp', 0, 0, tiled=True)  13.1 us
    ppermute x6, starting transfers between devices, from_ring(): return lax.ppermute(v, ('fsdp', 'pre'), pairs)  11.1 us
    pallas_call x2, Pallas kernels, first_chunks(): pl.pallas_call(first_kernel, grid=(cols // width,), in_specs=[pl.BlockSpe...  9.5 us
    all_to_all x1, starting transfers between devices, body(): pieces = lax.all_to_all(pieces, 'fsdp', 0, 0, tiled=True)  6.12 us
    ppermute x3, starting transfers between devices, from_x(): lax.ppermute(v, ('fsdp', 'pre'), [(device(z, y, x + d, c), device(z, y, x...  5.65 us
  transfers between devices with their start and end apart: 15, of which 7 were waited for; matrix products, arithmetic and copies ran while one was open for 2% of the time, Pallas kernels for 12%

profile of v2, /device:TPU:0, one launch (start us, length us, event | category | flops | bytes accessed | tf_op | source)
XLA Modules:
  0.0 129.7 jit_solution(7274607518231355746)
XLA Ops:
  0.7 0.0 copy-start.5
  0.7 1.2 dynamic-slice_bitcast_fusion.2
  1.9 0.1 pad_maximum_fusion
  1.9 0.1 collective-permute-start
  2.0 1.9 %collective-permute-done.r_ref = bf16[2,128,1024]{2,1,0:T(8,128)(2,1)S(1)} collective-permute-done((bf16[2,128,1024]{2,1,0:T(8,128)(2,1)S(1)}, bf16[2,128,1024]{2,1,0:T(8,128)(2,1)S(1)}, u32[]{:S(2)}, u32[]{:S(2)}) %collective-permute-start) | collective-permute-done | bytes 524320 | tf_op jit(solution)/shard_map/ppermute | solution.py:234
  4.0 0.1 pad_maximum_fusion.1.refs_0_
  4.0 1.7 %collective-permute-start.3 = (bf16[2,128,1024]{2,1,0:T(8,128)(2,1)S(1)}, bf16[2,128,1024]{2,1,0:T(8,128)(2,1)S(1)}, u32[]{:S(2)}, u32[]{:S(2)}) collective-permute-start(bf16[2,128,1024]{2,1,0:T(8,128)(2,1)S(1)} %pad_maximum_fusion.1.refs_0_), channel_id=1, source_target_pairs={{24,0},{97,1},{26,2},{99,3},{28,4},{101,5},{30,6},{103,7},{0,8},{1... | collective-permute-start | bytes 1572872 | tf_op jit(solution)/shard_map/ppermute | solution.py:251
  5.7 2.9 %collective-permute-start.2 = (bf16[2,128,1024]{2,1,0:T(8,128)(2,1)S(1)}, bf16[2,128,1024]{2,1,0:T(8,128)(2,1)S(1)}, u32[]{:S(2)}, u32[]{:S(2)}) collective-permute-start(bf16[2,128,1024]{2,1,0:T(8,128)(2,1)S(1)} %pad_maximum_fusion.1.refs_0_), channel_id=1, source_target_pairs={{16,0},{65,1},{18,2},{67,3},{20,4},{69,5},{22,6},{71,7},{24,8},{73... | collective-permute-start | bytes 1572872 | tf_op jit(solution)/shard_map/ppermute | solution.py:251
  8.6 1.3 %collective-permute-start.1 = (bf16[2,128,1024]{2,1,0:T(8,128)(2,1)S(1)}, bf16[2,128,1024]{2,1,0:T(8,128)(2,1)S(1)}, u32[]{:S(2)}, u32[]{:S(2)}) collective-permute-start(bf16[2,128,1024]{2,1,0:T(8,128)(2,1)S(1)} %pad_maximum_fusion.1.refs_0_), channel_id=1, source_target_pairs={{8,0},{33,1},{10,2},{35,3},{12,4},{37,5},{14,6},{39,7},{16,8},{41,... | collective-permute-start | bytes 1572872 | tf_op jit(solution)/shard_map/ppermute | solution.py:251
  10.0 0.0 copy-done.5
  10.0 1.0 shard_map.69
  11.0 5.5 %all-to-all-start = ((bf16[16,128,128]{2,1,0:T(8,128)(2,1)}), bf16[16,128,128]{2,1,0:T(8,128)(2,1)S(1)}, u32[]{:S(2)}, u32[]{:S(2)}) async-start(bf16[16,128,128]{2,1,0:T(8,128)(2,1)} %shard_map.69), calls=%async_computation | async-start | bytes 1048576 | tf_op jit(solution)/shard_map/all_to_all | solution.py:281
  16.5 0.0 collective-permute-done.3.refs_3_
  16.5 0.0 copy-start.6
  16.5 0.8 copy-done.6
  17.3 5.6 %collective-permute-done.2.refs_2_ = bf16[2,128,1024]{2,1,0:T(8,128)(2,1)S(1)} collective-permute-done((bf16[2,128,1024]{2,1,0:T(8,128)(2,1)S(1)}, bf16[2,128,1024]{2,1,0:T(8,128)(2,1)S(1)}, u32[]{:S(2)}, u32[]{:S(2)}) %collective-permute-start.2) | collective-permute-done | bytes 524320 | tf_op jit(solution)/shard_map/ppermute | solution.py:251
  22.9 0.0 copy-start.8
  22.9 0.8 copy-done.8
  23.7 0.0 collective-permute-done.1.refs_1_
  23.7 0.0 copy-start.10
  23.7 0.8 copy-done.10
  24.5 0.0 copy-start.7
  24.5 1.0 copy-done.7
  25.5 1.0 copy-done.9
  26.6 1.0 copy-done.11
  27.6 0.2 shard_map.68.refs_4_
  27.8 2.8 %all-to-all-done.refs_0_ = bf16[16,128,128]{2,1,0:T(8,128)(2,1)S(1)} async-done(((bf16[16,128,128]{2,1,0:T(8,128)(2,1)}), bf16[16,128,128]{2,1,0:T(8,128)(2,1)S(1)}, u32[]{:S(2)}, u32[]{:S(2)}) %all-to-all-start) | async-done | bytes 524320 | tf_op jit(solution)/shard_map/all_to_all | solution.py:281
  30.6 0.0 collective-permute-start.8
  30.6 3.2 %collective-permute-start.7 = (bf16[8,128,1024]{2,1,0:T(8,128)(2,1)S(1)}, bf16[8,128,1024]{2,1,0:T(8,128)(2,1)}, u32[]{:S(2)}, u32[]{:S(2)}) collective-permute-start(bf16[8,128,1024]{2,1,0:T(8,128)(2,1)S(1)} %shard_map.68.refs_4_), channel_id=1, source_target_pairs={{32,0},{9,1},{34,2},{11,3},{36,4},{13,5},{38,6},{15,7},{40,8},{17,... | collective-permute-start | bytes 6291464 | tf_op jit(solution)/shard_map/ppermute | solution.py:251
  33.8 1.5 %collective-permute-start.6 = (bf16[16,128,128]{2,1,0:T(8,128)(2,1)S(1)}, bf16[16,128,128]{2,1,0:T(8,128)(2,1)S(1)}, u32[]{:S(2)}, u32[]{:S(2)}) collective-permute-start(bf16[16,128,128]{2,1,0:T(8,128)(2,1)S(1)} %all-to-all-done.refs_0_), channel_id=1, source_target_pairs={{6,0},{7,1},{0,2},{1,3},{2,4},{3,5},{4,6},{5,7},{14,8},{15,9},{8,1... | collective-permute-start | bytes 1572872 | tf_op jit(solution)/shard_map/ppermute | solution.py:240
  35.3 2.7 %collective-permute-start.5 = (bf16[16,128,128]{2,1,0:T(8,128)(2,1)S(1)}, bf16[16,128,128]{2,1,0:T(8,128)(2,1)}, u32[]{:S(2)}, u32[]{:S(2)}) collective-permute-start(bf16[16,128,128]{2,1,0:T(8,128)(2,1)S(1)} %all-to-all-done.refs_0_), channel_id=1, source_target_pairs={{4,0},{5,1},{6,2},{7,3},{0,4},{1,5},{2,6},{3,7},{12,8},{13,9},{14,... | collective-permute-start | bytes 1572872 | tf_op jit(solution)/shard_map/ppermute | solution.py:240
  38.0 1.4 %collective-permute-start.4 = (bf16[16,128,128]{2,1,0:T(8,128)(2,1)S(1)}, bf16[16,128,128]{2,1,0:T(8,128)(2,1)}, u32[]{:S(2)}, u32[]{:S(2)}) collective-permute-start(bf16[16,128,128]{2,1,0:T(8,128)(2,1)S(1)} %all-to-all-done.refs_0_), channel_id=1, source_target_pairs={{2,0},{3,1},{4,2},{5,3},{6,4},{7,5},{0,6},{1,7},{10,8},{11,9},{12,... | collective-permute-start | bytes 1572872 | tf_op jit(solution)/shard_map/ppermute | solution.py:240
  39.4 0.1 pad_add_fusion.place_ref
  39.5 18.4 %collective-permute-done.8.refs_6_ = bf16[8,128,1024]{2,1,0:T(8,128)(2,1)} collective-permute-done((bf16[8,128,1024]{2,1,0:T(8,128)(2,1)S(1)}, bf16[8,128,1024]{2,1,0:T(8,128)(2,1)}, u32[]{:S(2)}, u32[]{:S(2)}) %collective-permute-start.8) | collective-permute-done | bytes 2097184 | tf_op jit(solution)/shard_map/ppermute | solution.py:251
  57.9 1.3 %slice.14 = bf16[4,128,1024]{2,1,0:T(8,128)(2,1)S(1)} slice(bf16[8,128,1024]{2,1,0:T(8,128)(2,1)} %collective-permute-done.8.refs_6_), slice={[4:8], [0:128], [0:1024]} | slice | bytes 2097152 | tf_op jit(solution)/shard_map/slice | solution.py:287
  59.2 0.1 collective-permute-start.11
  59.3 0.0 collective-permute-done.7.refs_5_
  59.3 1.3 %slice.13 = bf16[4,128,1024]{2,1,0:T(8,128)(2,1)S(1)} slice(bf16[8,128,1024]{2,1,0:T(8,128)(2,1)} %collective-permute-done.7.refs_5_), slice={[0:4], [0:128], [0:1024]} | slice | bytes 2097152 | tf_op jit(solution)/shard_map/slice | solution.py:286
  60.6 1.9 %collective-permute-start.10 = (bf16[4,128,1024]{2,1,0:T(8,128)(2,1)S(1)}, bf16[4,128,1024]{2,1,0:T(8,128)(2,1)S(1)}, u32[]{:S(2)}, u32[]{:S(2)}) collective-permute-start(bf16[4,128,1024]{2,1,0:T(8,128)(2,1)S(1)} %slice.13), channel_id=1, source_target_pairs={{32,0},{9,1},{34,2},{11,3},{36,4},{13,5},{38,6},{15,7},{40,8},{17,... | collective-permute-start | bytes 3145736 | tf_op jit(solution)/shard_map/ppermute | solution.py:251
  62.5 0.0 collective-permute-done.6.refs_3_
  62.5 0.0 collective-permute-done.5.refs_2_
  62.5 0.0 collective-permute-done.4.refs_1_
  62.5 4.8 %shard_map.70 = (bf16[512,1024]{1,0:T(8,128)(2,1)S(1)}, bf16[512,512]{1,0:T(8,128)(2,1)S(1)}) custom-call(s32[4]{0:T(128)S(1)} %pad_add_fusion.place_ref, bf16[16,128,128]{2,1,0:T(8,128)(2,1)S(1)} %all-to-all-done.refs_0_, bf16[16,128,128]{2,1,0:T(8,128)(2,1)} %collective-permute-done.4.refs_1_, bf16[16,128,128]{2,1,0:T(8,128)(2,1)} %collective-permute-done.5.refs_2_, ...), custom_call_target="tpu_custom_call" | custom-call | flops 1 | bytes 1 | tf_op jit(solution)/shard_map/pallas_call | solution.py:131
  67.3 1.3 collective-permute-start.12
  68.6 0.1 collective-permute-start.9
  68.8 4.7 %shard_map.71.acc_ref = f32[512,1024]{1,0:T(8,128)S(1)} custom-call(s32[4]{0:T(128)S(1)} %pad_add_fusion.place_ref, bf16[16,128,128]{2,1,0:T(8,128)(2,1)S(1)} %all-to-all-done.refs_0_, bf16[16,128,128]{2,1,0:T(8,128)(2,1)} %collective-permute-done.4.refs_1_, bf16[16,128,128]{2,1,0:T(8,128)(2,1)} %collective-permute-done.5.refs_2_, ...), custom_call_target="tpu_custom_call" | custom-call | flops 1 | bytes 1 | tf_op jit(solution)/shard_map/pallas_call | solution.py:131
  73.5 0.0 collective-permute-done.9.cross_ref
  73.5 1.2 collective-permute-done.11.far_ref
  74.7 0.8 collective-permute-done.10.own_ref
  75.5 0.0 collective-permute-done.12.share_ref
  75.5 0.0 copy-done.12
  75.5 0.0 copy-done.13
  75.5 3.2 %shard_map.72 = bf16[48,32,512]{2,1,0:T(8,128)(2,1)} custom-call(s32[4]{0:T(128)S(1)} %pad_add_fusion.place_ref, s32[16,16]{1,0:T(8,128)S(1)} %copy-done.12, s32[16,16]{1,0:T(8,128)S(1)} %copy-done.13, bf16[512,512]{1,0:T(8,128)(2,1)S(1)} %get-tuple-element.10.lhs_ref, bf16[512,512]{1,0:T(8,128)(2,1)S(1)} %collective-permute-done.9.cross_ref, ...), custom_call_target="tpu_custom_call" | custom-call | flops 1 | bytes 1 | tf_op jit(solution)/shard_map/pallas_call | solution.py:168
  78.7 6.1 %all-to-all-start.1 = ((bf16[48,32,512]{2,1,0:T(8,128)(2,1)}), bf16[48,32,512]{2,1,0:T(8,128)(2,1)S(1)}, u32[]{:S(2)}, u32[]{:S(2)}) async-start(bf16[48,32,512]{2,1,0:T(8,128)(2,1)} %shard_map.72), calls=%async_computation.1 | async-start | bytes 3145728 | tf_op jit(solution)/shard_map/all_to_all | solution.py:295
  84.8 0.0 copy-start
  84.9 2.8 %copy-done = f32[3,2,512,512]{3,2,1,0:T(8,128)S(1)} copy-done((f32[3,2,512,512]{3,2,1,0:T(8,128)S(1)}, f32[3,2,512,512]{3,2,1,0:T(8,128)}, u32[]{:S(2)}) %copy-start) | copy-done | bytes 6291480
  87.6 4.8 %shard_map.73 = (bf16[6,512,512]{2,1,0:T(8,128)(2,1)S(1)}, bf16[6,512,512]{2,1,0:T(8,128)(2,1)S(1)}) custom-call(f32[6,512,512]{2,1,0:T(8,128)S(1)} %bitcast.14), custom_call_target="tpu_custom_call" | custom-call | flops 1 | bytes 1 | tf_op jit(solution)/shard_map/pallas_call | solution.py:59
  92.5 0.0 copy-start.1
  92.5 1.7 %copy-done.1 = bf16[6,512,512]{2,1,0:T(8,128)(2,1)} copy-done((bf16[6,512,512]{2,1,0:T(8,128)(2,1)}, bf16[6,512,512]{2,1,0:T(8,128)(2,1)S(1)}, u32[]{:S(2)}) %copy-start.1) | copy-done | bytes 3145752
  94.1 1.6 %copy-done.3 = bf16[6,512,512]{2,1,0:T(8,128)(2,1)} copy-done((bf16[6,512,512]{2,1,0:T(8,128)(2,1)}, bf16[6,512,512]{2,1,0:T(8,128)(2,1)S(1)}, u32[]{:S(2)}) %copy-start.3) | copy-done | bytes 3145752
  95.7 13.1 %all-to-all-done.1 = bf16[48,32,512]{2,1,0:T(8,128)(2,1)S(1)} async-done(((bf16[48,32,512]{2,1,0:T(8,128)(2,1)}), bf16[48,32,512]{2,1,0:T(8,128)(2,1)S(1)}, u32[]{:S(2)}, u32[]{:S(2)}) %all-to-all-start.1) | async-done | bytes 1572896 | tf_op jit(solution)/shard_map/all_to_all | solution.py:295
  108.9 1.9 %copy-done.2 = bf16[6,512,512]{2,1,0:T(8,128)(2,1)S(1)} copy-done((bf16[6,512,512]{2,1,0:T(8,128)(2,1)S(1)}, bf16[6,512,512]{2,1,0:T(8,128)(2,1)}, u32[]{:S(2)}) %copy-start.2) | copy-done | bytes 3145752
  110.8 1.9 %copy-done.4 = bf16[6,512,512]{2,1,0:T(8,128)(2,1)S(1)} copy-done((bf16[6,512,512]{2,1,0:T(8,128)(2,1)S(1)}, bf16[6,512,512]{2,1,0:T(8,128)(2,1)}, u32[]{:S(2)}) %copy-start.4) | copy-done | bytes 3145752
  112.7 17.0 %shard_map.74 = (bf16[3,512,512]{2,1,0:T(8,128)(2,1)}, f32[3,2,512,512]{3,2,1,0:T(8,128)}) custom-call(bf16[16,3,32,512]{3,2,1,0:T(8,128)(2,1)S(1)} %bitcast.15, bf16[3,2,512,512]{3,2,1,0:T(8,128)(2,1)S(1)} %bitcast.16, bf16[3,2,512,512]{3,2,1,0:T(8,128)(2,1)S(1)} %bitcast.17), custom_call_target="tpu_custom_call" | custom-call | flops 1 | bytes 1 | tf_op jit(solution)/shard_map/pallas_call | solution.py:211
  (8 shorter events, 0.0 us)
Async XLA Ops:
  0.7 9.3 %copy-start.5 = (bf16[256,1024]{1,0:T(8,128)(2,1)S(1)}, bf16[256,1024]{1,0:T(8,128)(2,1)}, u32[]{:S(2)}) copy-start(bf16[256,1024]{1,0:T(8,128)(2,1)} %a_ref.1) | copy-start | bytes 1572868
  1.9 2.0 %collective-permute-start = (bf16[2,128,1024]{2,1,0:T(8,128)(2,1)S(1)}, bf16[2,128,1024]{2,1,0:T(8,128)(2,1)S(1)}, u32[]{:S(2)}, u32[]{:S(2)}) collective-permute-start(bf16[2,128,1024]{2,1,0:T(8,128)(2,1)S(1)} %pad_maximum_fusion), channel_id=1, source_target_pairs={{0,1},{1,0},{2,3},{3,2},{4,5},{5,4},{6,7},{7,6},{8,9},{9,8},{10,11... | collective-permute-start | bytes 1572872 | tf_op jit(solution)/shard_map/ppermute | solution.py:234
  4.0 12.5 %collective-permute-start.3 = (bf16[2,128,1024]{2,1,0:T(8,128)(2,1)S(1)}, bf16[2,128,1024]{2,1,0:T(8,128)(2,1)S(1)}, u32[]{:S(2)}, u32[]{:S(2)}) collective-permute-start(bf16[2,128,1024]{2,1,0:T(8,128)(2,1)S(1)} %pad_maximum_fusion.1.refs_0_), channel_id=1, source_target_pairs={{24,0},{97,1},{26,2},{99,3},{28,4},{101,5},{30,6},{103,7},{0,8},{1... | collective-permute-start | bytes 1572872 | tf_op jit(solution)/shard_map/ppermute | solution.py:251
  5.7 17.1 %collective-permute-start.2 = (bf16[2,128,1024]{2,1,0:T(8,128)(2,1)S(1)}, bf16[2,128,1024]{2,1,0:T(8,128)(2,1)S(1)}, u32[]{:S(2)}, u32[]{:S(2)}) collective-permute-start(bf16[2,128,1024]{2,1,0:T(8,128)(2,1)S(1)} %pad_maximum_fusion.1.refs_0_), channel_id=1, source_target_pairs={{16,0},{65,1},{18,2},{67,3},{20,4},{69,5},{22,6},{71,7},{24,8},{73... | collective-permute-start | bytes 1572872 | tf_op jit(solution)/shard_map/ppermute | solution.py:251
  8.6 15.0 %collective-permute-start.1 = (bf16[2,128,1024]{2,1,0:T(8,128)(2,1)S(1)}, bf16[2,128,1024]{2,1,0:T(8,128)(2,1)S(1)}, u32[]{:S(2)}, u32[]{:S(2)}) collective-permute-start(bf16[2,128,1024]{2,1,0:T(8,128)(2,1)S(1)} %pad_maximum_fusion.1.refs_0_), channel_id=1, source_target_pairs={{8,0},{33,1},{10,2},{35,3},{12,4},{37,5},{14,6},{39,7},{16,8},{41,... | collective-permute-start | bytes 1572872 | tf_op jit(solution)/shard_map/ppermute | solution.py:251
  11.0 19.6 %all-to-all-start = ((bf16[16,128,128]{2,1,0:T(8,128)(2,1)}), bf16[16,128,128]{2,1,0:T(8,128)(2,1)S(1)}, u32[]{:S(2)}, u32[]{:S(2)}) async-start(bf16[16,128,128]{2,1,0:T(8,128)(2,1)} %shard_map.69), calls=%async_computation | async-start | bytes 1048576 | tf_op jit(solution)/shard_map/all_to_all | solution.py:281
  16.5 0.8 copy-start.6
  22.9 0.8 copy-start.8
  23.7 0.8 copy-start.10
  24.5 1.0 copy-start.7
  25.5 1.0 copy-start.9
  26.6 1.0 copy-start.11
  30.6 27.4 %collective-permute-start.8 = (bf16[8,128,1024]{2,1,0:T(8,128)(2,1)S(1)}, bf16[8,128,1024]{2,1,0:T(8,128)(2,1)}, u32[]{:S(2)}, u32[]{:S(2)}) collective-permute-start(bf16[8,128,1024]{2,1,0:T(8,128)(2,1)S(1)} %shard_map.68.refs_4_), channel_id=1, source_target_pairs={{96,0},{25,1},{98,2},{27,3},{100,4},{29,5},{102,6},{31,7},{104,8},... | collective-permute-start | bytes 6291464 | tf_op jit(solution)/shard_map/ppermute | solution.py:251
  30.6 28.7 %collective-permute-start.7 = (bf16[8,128,1024]{2,1,0:T(8,128)(2,1)S(1)}, bf16[8,128,1024]{2,1,0:T(8,128)(2,1)}, u32[]{:S(2)}, u32[]{:S(2)}) collective-permute-start(bf16[8,128,1024]{2,1,0:T(8,128)(2,1)S(1)} %shard_map.68.refs_4_), channel_id=1, source_target_pairs={{32,0},{9,1},{34,2},{11,3},{36,4},{13,5},{38,6},{15,7},{40,8},{17,... | collective-permute-start | bytes 6291464 | tf_op jit(solution)/shard_map/ppermute | solution.py:251
  33.8 28.7 %collective-permute-start.6 = (bf16[16,128,128]{2,1,0:T(8,128)(2,1)S(1)}, bf16[16,128,128]{2,1,0:T(8,128)(2,1)S(1)}, u32[]{:S(2)}, u32[]{:S(2)}) collective-permute-start(bf16[16,128,128]{2,1,0:T(8,128)(2,1)S(1)} %all-to-all-done.refs_0_), channel_id=1, source_target_pairs={{6,0},{7,1},{0,2},{1,3},{2,4},{3,5},{4,6},{5,7},{14,8},{15,9},{8,1... | collective-permute-start | bytes 1572872 | tf_op jit(solution)/shard_map/ppermute | solution.py:240
  35.3 27.2 %collective-permute-start.5 = (bf16[16,128,128]{2,1,0:T(8,128)(2,1)S(1)}, bf16[16,128,128]{2,1,0:T(8,128)(2,1)}, u32[]{:S(2)}, u32[]{:S(2)}) collective-permute-start(bf16[16,128,128]{2,1,0:T(8,128)(2,1)S(1)} %all-to-all-done.refs_0_), channel_id=1, source_target_pairs={{4,0},{5,1},{6,2},{7,3},{0,4},{1,5},{2,6},{3,7},{12,8},{13,9},{14,... | collective-permute-start | bytes 1572872 | tf_op jit(solution)/shard_map/ppermute | solution.py:240
  38.0 24.5 %collective-permute-start.4 = (bf16[16,128,128]{2,1,0:T(8,128)(2,1)S(1)}, bf16[16,128,128]{2,1,0:T(8,128)(2,1)}, u32[]{:S(2)}, u32[]{:S(2)}) collective-permute-start(bf16[16,128,128]{2,1,0:T(8,128)(2,1)S(1)} %all-to-all-done.refs_0_), channel_id=1, source_target_pairs={{2,0},{3,1},{4,2},{5,3},{6,4},{7,5},{0,6},{1,7},{10,8},{11,9},{12,... | collective-permute-start | bytes 1572872 | tf_op jit(solution)/shard_map/ppermute | solution.py:240
  59.2 15.5 %collective-permute-start.11 = (bf16[4,128,1024]{2,1,0:T(8,128)(2,1)S(1)}, bf16[4,128,1024]{2,1,0:T(8,128)(2,1)S(1)}, u32[]{:S(2)}, u32[]{:S(2)}) collective-permute-start(bf16[4,128,1024]{2,1,0:T(8,128)(2,1)S(1)} %slice.14), channel_id=1, source_target_pairs={{25,0},{96,1},{27,2},{98,3},{29,4},{100,5},{31,6},{102,7},{1,8},{1... | collective-permute-start | bytes 3145736 | tf_op jit(solution)/shard_map/ppermute | solution.py:260
  60.6 14.9 %collective-permute-start.10 = (bf16[4,128,1024]{2,1,0:T(8,128)(2,1)S(1)}, bf16[4,128,1024]{2,1,0:T(8,128)(2,1)S(1)}, u32[]{:S(2)}, u32[]{:S(2)}) collective-permute-start(bf16[4,128,1024]{2,1,0:T(8,128)(2,1)S(1)} %slice.13), channel_id=1, source_target_pairs={{32,0},{9,1},{34,2},{11,3},{36,4},{13,5},{38,6},{15,7},{40,8},{17,... | collective-permute-start | bytes 3145736 | tf_op jit(solution)/shard_map/ppermute | solution.py:251
  67.3 8.1 %collective-permute-start.12 = (bf16[512,1024]{1,0:T(8,128)(2,1)S(1)}, bf16[512,1024]{1,0:T(8,128)(2,1)S(1)}, u32[]{:S(2)}, u32[]{:S(2)}) collective-permute-start(bf16[512,1024]{1,0:T(8,128)(2,1)S(1)} %get-tuple-element.11), channel_id=1, source_target_pairs={{0,1},{1,0},{2,3},{3,2},{4,5},{5,4},{6,7},{7,6},{8,9},{9,8},{10,11... | collective-permute-start | bytes 3145736 | tf_op jit(solution)/shard_map/ppermute | solution.py:234
  68.6 6.8 %copy-start.12 = (s32[16,16]{1,0:T(8,128)S(1)}, s32[16,16]{1,0:T(8,128)}, u32[]{:S(2)}) copy-start(s32[16,16]{1,0:T(8,128)} %owner_ref.1) | copy-start | bytes 3076
  68.6 6.8 %copy-start.13 = (s32[16,16]{1,0:T(8,128)S(1)}, s32[16,16]{1,0:T(8,128)}, u32[]{:S(2)}) copy-start(s32[16,16]{1,0:T(8,128)} %offs_ref.1) | copy-start | bytes 3076
  68.6 4.8 %collective-permute-start.9 = (bf16[512,512]{1,0:T(8,128)(2,1)S(1)}, bf16[512,512]{1,0:T(8,128)(2,1)S(1)}, u32[]{:S(2)}, u32[]{:S(2)}) collective-permute-start(bf16[512,512]{1,0:T(8,128)(2,1)S(1)} %get-tuple-element.10.lhs_ref), channel_id=1, source_target_pairs={{0,1},{1,0},{2,3},{3,2},{4,5},{5,4},{6,7},{7,6},{8,9},{9,8},{10,11... | collective-permute-start | bytes 1572872 | tf_op jit(solution)/shard_map/ppermute | solution.py:234
  78.7 30.2 %all-to-all-start.1 = ((bf16[48,32,512]{2,1,0:T(8,128)(2,1)}), bf16[48,32,512]{2,1,0:T(8,128)(2,1)S(1)}, u32[]{:S(2)}, u32[]{:S(2)}) async-start(bf16[48,32,512]{2,1,0:T(8,128)(2,1)} %shard_map.72), calls=%async_computation.1 | async-start | bytes 3145728 | tf_op jit(solution)/shard_map/all_to_all | solution.py:295
  84.8 2.8 %copy-start = (f32[3,2,512,512]{3,2,1,0:T(8,128)S(1)}, f32[3,2,512,512]{3,2,1,0:T(8,128)}, u32[]{:S(2)}) copy-start(f32[3,2,512,512]{3,2,1,0:T(8,128)} %param.9) | copy-start | bytes 18874372
  92.5 1.7 %copy-start.1 = (bf16[6,512,512]{2,1,0:T(8,128)(2,1)}, bf16[6,512,512]{2,1,0:T(8,128)(2,1)S(1)}, u32[]{:S(2)}) copy-start(bf16[6,512,512]{2,1,0:T(8,128)(2,1)S(1)} %get-tuple-element.12) | copy-start | bytes 9437188
  94.1 1.6 %copy-start.3 = (bf16[6,512,512]{2,1,0:T(8,128)(2,1)}, bf16[6,512,512]{2,1,0:T(8,128)(2,1)S(1)}, u32[]{:S(2)}) copy-start(bf16[6,512,512]{2,1,0:T(8,128)(2,1)S(1)} %get-tuple-element.13) | copy-start | bytes 9437188
  108.9 1.9 %copy-start.2 = (bf16[6,512,512]{2,1,0:T(8,128)(2,1)S(1)}, bf16[6,512,512]{2,1,0:T(8,128)(2,1)}, u32[]{:S(2)}) copy-start(bf16[6,512,512]{2,1,0:T(8,128)(2,1)} %copy-done.1) | copy-start | bytes 9437188
  110.8 1.9 %copy-start.4 = (bf16[6,512,512]{2,1,0:T(8,128)(2,1)S(1)}, bf16[6,512,512]{2,1,0:T(8,128)(2,1)}, u32[]{:S(2)}) copy-start(bf16[6,512,512]{2,1,0:T(8,128)(2,1)} %copy-done.3) | copy-start | bytes 9437188

commit v3 on v2

--- a/solution.py
+++ b/solution.py
@@ -8,7 +8,9 @@
 ITERS = 2
 BF = jnp.bfloat16
 F32 = jnp.float32
-VMEM = 20 * 1024 * 1024
+VMEM = 12 * 1024 * 1024
+MIDDLE_VMEM = 12 * 1024 * 1024
+LARGE_VMEM = 20 * 1024 * 1024
 SHORT = pl.CostEstimate(flops=1, bytes_accessed=1, transcendentals=0)
 
 
@@ -61,24 +63,26 @@
         grid=(n,),
         in_specs=[spec],
         out_specs=[spec, spec],
-        out_shape=[jax.ShapeDtypeStruct((n, b, b), BF)] * 2,
-        compiler_params=params(),
+        out_shape=[pltpu.HBM((n, b, b), BF)] * 2,
+        compiler_params=pltpu.CompilerParams(vmem_limit_bytes=MIDDLE_VMEM),
         cost_estimate=SHORT,
     )(roots)
 
 
 def join_kernel(*refs):
-    for i, v in enumerate(refs[:-1]):
-        refs[-1][i] = v[0]
+    parts, o_ref = refs[:-1], refs[-1]
+    for o in range(2):
+        for i, v in enumerate(parts):
+            o_ref[o * len(parts) + i] = v[o]
 
 
 def join(parts):
     n, rows, cols = parts[0].shape
+    vmem = pl.BlockSpec(memory_space=pltpu.VMEM)
     return pl.pallas_call(
         join_kernel,
-        grid=(n,),
-        in_specs=[pl.BlockSpec((1, rows, cols), lambda i: (i, 0, 0))] * len(parts),
-        out_specs=pl.BlockSpec((len(parts), rows, cols), lambda i: (i, 0, 0)),
+        in_specs=[vmem] * len(parts),
+        out_specs=vmem,
         out_shape=jax.ShapeDtypeStruct((n * len(parts), rows, cols), BF),
         compiler_params=params(),
         cost_estimate=SHORT,
@@ -101,55 +105,49 @@
     return jnp.concatenate(rows, axis=0)
 
 
-def product(lhs, b):
-    return dot(lhs, b.reshape(lhs.shape[1], b.shape[-1]))
+def product(lhs, *b):
+    return dot(lhs, jnp.concatenate([v.reshape(-1, v.shape[-1]) for v in b], axis=0))
 
 
 def first_kernel(place_ref, *refs):
-    a_refs, b_refs, o_ref, lhs = refs[:4], refs[4:7], refs[7], refs[-1]
-
-    @pl.when(pl.program_id(0) == 0)
-    def _():
-        for n, j in enumerate((0, 1, 3)):
-            lhs[n] = left_operand(place_ref, a_refs, j)
-        if len(refs) == 10:
-            refs[8][...] = left_operand(place_ref, a_refs, 2)
-
-    o_ref[...] = sum(product(lhs[n], b_refs[n][...]) for n in range(3)).astype(o_ref.dtype)
-
-
-def first_chunks(place, a_list, chunks, other):
+    a_refs, b_refs, shares, (acc_ref, last_ref) = refs[:4], refs[4:7], refs[7:9], refs[9:]
+    lhs = jnp.concatenate([left_operand(place_ref, a_refs, j) for j in (0, 1, 3)], axis=1)
+    block = shares[0].shape[1]
+    for o in (1, 0):
+        for c in range(2):
+            at = slice(c * block, (c + 1) * block)
+            total = product(lhs, *[v[4 * o : 4 * o + 4, :, at] for v in b_refs])
+            if o:
+                shares[c][...] = total.astype(BF)
+            else:
+                acc_ref[:, at] = total
+    last_ref[...] = left_operand(place_ref, a_refs, 2)
+
+
+def first_chunks(place, a_list, chunks):
     n, rows, tokens = a_list[0].shape
     cols = chunks[0].shape[-1]
-    width = cols // 4
     full = (4 * rows, 4 * tokens)
-    out_specs = [pl.BlockSpec((4 * rows, width), lambda i: (0, i))]
-    out_shape = [jax.ShapeDtypeStruct((4 * rows, cols), BF if other else F32)]
-    if other:
-        out_specs.append(pl.BlockSpec(full, lambda i: (0, 0)))
-        out_shape.append(jax.ShapeDtypeStruct(full, BF))
+    vmem = pl.BlockSpec(memory_space=pltpu.VMEM)
     return pl.pallas_call(
         first_kernel,
-        grid=(cols // width,),
-        in_specs=[pl.BlockSpec(memory_space=pltpu.SMEM)]
-        + [pl.BlockSpec((n, rows, tokens), lambda i: (0, 0, 0))] * 4
-        + [pl.BlockSpec((4, tokens, width), lambda i: (int(other), 0, i))] * 3,
-        out_specs=out_specs,
-        out_shape=out_shape,
-        scratch_shapes=[pltpu.VMEM((3,) + full, BF)],
-        compiler_params=params(),
-        cost_estimate=SHORT,
+        in_specs=[pl.BlockSpec(memory_space=pltpu.SMEM)] + [vmem] * 7,
+        out_specs=[vmem] * 4,
+        out_shape=[jax.ShapeDtypeStruct(full, BF)] * 2
+        + [jax.ShapeDtypeStruct((4 * rows, cols), F32), jax.ShapeDtypeStruct(full, BF)],
+        compiler_params=params(),
+        cost_estimate=pl.CostEstimate(flops=3 * 2**30, bytes_accessed=12 * 2**20, transcendentals=0),
     )(place, *a_list, *chunks)
 
 
-def last_kernel(place_ref, owner_ref, offs_ref, lhs_ref, cross_ref, own_ref, far_ref, acc_ref, share_ref, o_ref):
+def last_kernel(place_ref, owner_ref, offs_ref, lhs_ref, cross_ref, own_ref, far_ref, acc_ref, share_0, share_1, o_ref):
     x, core = place_ref[2], place_ref[3]
     part, block = o_ref.shape[1:]
     o_ref[...] = jnp.zeros_like(o_ref)
     for c in range(2):
         at_cols = slice(c * block, (c + 1) * block)
         total = acc_ref[:, at_cols] + product(lhs_ref[...], own_ref[:, :, at_cols])
-        cross = share_ref[:, at_cols].astype(F32) + product(cross_ref[...], far_ref[:, :, at_cols])
+        cross = (share_0, share_1)[c][...].astype(F32) + product(cross_ref[...], far_ref[:, :, at_cols])
         col = 2 * (2 * x + core) + c
         for dx in range(4):
             for o in range(2):
@@ -162,15 +160,13 @@
                     o_ref[key] = (total[at : at + part] + cross[to : to + part]).astype(BF)
 
 
-def last_chunk(place, owner, offsets, lhs, cross_lhs, own, far, acc, share):
-    rows, cols = acc.shape
-    operands = (lhs, cross_lhs, own, far, acc, share)
+def last_chunk(place, owner, offsets, *operands):
+    rows, cols = operands[4].shape
     return pl.pallas_call(
         last_kernel,
-        grid=(1,),
         in_specs=[pl.BlockSpec(memory_space=pltpu.SMEM)] * 3
-        + [pl.BlockSpec(v.shape, lambda i, n=v.ndim: (0,) * n) for v in operands],
-        out_specs=pl.BlockSpec((48, rows // 16, cols // 2), lambda i: (0, 0, 0)),
+        + [pl.BlockSpec(memory_space=pltpu.VMEM)] * len(operands),
+        out_specs=pl.BlockSpec(memory_space=pltpu.VMEM),
         out_shape=jax.ShapeDtypeStruct((48, rows // 16, cols // 2), BF),
         compiler_params=params(),
         cost_estimate=SHORT,
@@ -183,26 +179,25 @@
     gt = g.T
     g32 = g.astype(F32)
     scale = 0.1 / (jnp.sum(g32 * g32) / size + 1e-6)
-    eye = (
-        lax.broadcasted_iota(jnp.int32, (size, size), 0) == lax.broadcasted_iota(jnp.int32, (size, size), 1)
-    ).astype(F32)
-    roots = []
+    rows, cols = (lax.broadcasted_iota(jnp.int32, (size, size), d) for d in range(2))
+    diagonal = rows == cols
+    stats = [dot(g, gt), dot(gt, g)]
+    damped = [(v * scale + jnp.where(diagonal, 1.0, 0.0)).astype(BF) for v in stats]
+    ms = [dot(f_ref[0, k], damped[k]) for k in range(2)]
+    xs = [xb_ref[0, k] for k in range(2)]
+    for it in range(ITERS):
+        fs = [(jnp.where(diagonal, 5.0 - m, -m) * 0.25).astype(BF) for m in ms]
+        if it < ITERS - 1:
+            twos = [dot(f, f).astype(BF) for f in fs]
+            xs = [dot(x, f).astype(BF) for x, f in zip(xs, fs)]
+            fours = [dot(v, v).astype(BF) for v in twos]
+            ms = [dot(v, m.astype(BF)) for v, m in zip(fours, ms)]
+        else:
+            xs = [dot(x, f) for x, f in zip(xs, fs)]
     for k in range(2):
-        stat = dot(g, gt) if k == 0 else dot(gt, g)
-        damped = (stat * scale + eye).astype(BF)
-        m = dot(f_ref[0, k], damped)
-        x = xb_ref[0, k]
-        for it in range(ITERS):
-            f = ((5.0 * eye - m) * 0.25).astype(BF)
-            x32 = dot(x, f)
-            x = x32.astype(BF)
-            if it < ITERS - 1:
-                f2 = dot(f, f).astype(BF)
-                f4 = dot(f2, f2).astype(BF)
-                m = dot(f4, m.astype(BF))
-        n_ref[0, k] = x32
-        roots.append(x)
-    u_ref[0] = dot(dot(roots[0], g).astype(BF), roots[1]).astype(BF)
+        n_ref[0, k] = xs[k]
+    left, right = (x.astype(BF) for x in xs)
+    u_ref[0] = dot(dot(left, g).astype(BF), right).astype(BF)
 
 
 def newton(pieces, roots, fourth):
@@ -217,7 +212,7 @@
             jax.ShapeDtypeStruct((slots, b, b), BF),
             jax.ShapeDtypeStruct((slots, 2, b, b), F32),
         ],
-        compiler_params=params(),
+        compiler_params=pltpu.CompilerParams(vmem_limit_bytes=LARGE_VMEM),
         cost_estimate=SHORT,
     )(pieces, roots, fourth)
 
@@ -283,20 +278,18 @@
     up = from_ring(both, 1, 1)
     down = from_ring(both, 1, 3)
     a_list = [mine, from_x(mine, 1), from_x(mine, 2), from_x(mine, 3)]
+    xb, fourth = fourth_powers(prev_roots.reshape(slots * 2, b, b))
+    up, xb, fourth = lax.optimization_barrier((up, xb, fourth))
+    xb, fourth = (v.reshape(prev_roots.shape) for v in (xb, fourth))
     own_2 = from_ring(up[:4], 1, 1)
     far_2 = from_ring_across(down[4:], 3)
 
-    xb, fourth = fourth_powers(prev_roots.reshape(slots * 2, b, b))
-    share, lhs = first_chunks(place, a_list, [both, up, down], True)
-    (acc,) = first_chunks(place, a_list, [both, up, down], False)
+    share_0, share_1, acc, lhs = first_chunks(place, a_list, [both, up, down])
     pieces = last_chunk(
-        place, owner, offsets, lhs, swap_cores(lhs), own_2, far_2, acc, swap_cores(share)
+        place, owner, offsets, lhs, swap_cores(lhs), own_2, far_2, acc, swap_cores(share_0), swap_cores(share_1)
     )
     pieces = lax.all_to_all(pieces, "fsdp", 0, 0, tiled=True)
-    update, roots = newton(
-        pieces.reshape(16, slots, -1, b), xb.reshape(slots, 2, b, b), fourth.reshape(slots, 2, b, b)
-    )
-    return update, roots
+    return tuple(newton(pieces.reshape(16, slots, -1, b), xb, fourth))
 
 
 def solution(mesh):

time: 130 us -> 123 us (0.946)
  blocking collectives: 0 us -> 25 us
  waiting for transfers between devices: 43.8 us -> 31.8 us
  starting transfers between devices: 30 us -> 21.1 us
  Pallas kernels: 35.7 us -> 29.7 us
  local copies, waits for them, and re-layouts: 19.2 us -> 14.5 us
    all_to_all x0 -> x1, blocking collectives: none -> 25 us  [body(): pieces = lax.all_to_all(pieces, 'fsdp', 0, 0, tiled=True)]
    all_to_all x1 -> x0, waiting for transfers between devices: 13.1 us -> none  [body(): pieces = lax.all_to_all(pieces, 'fsdp', 0, 0, tiled=True)]
    all_to_all x1 -> x0, starting transfers between devices: 6.12 us -> none  [body(): pieces = lax.all_to_all(pieces, 'fsdp', 0, 0, tiled=True)]
    pallas_call x4 -> x3, Pallas kernels: 12.9 us -> 7.84 us  [the longest x1 4.98 us: first_chunks(): pl.pallas_call(first_kernel, in_specs=[pl.BlockSpec(memory_space=pltpu.SM...]
    ppermute x6, waiting for transfers between devices: 24.7 us -> 19.7 us  [from_ring(): return lax.ppermute(v, ('fsdp', 'pre'), pairs)]
    unnamed x28, local copies, waits for them, and re-layouts: 15.4 us -> 11 us
    ppermute x3 -> x4, waiting for transfers between devices: 1.9 us -> 4.7 us  [swap_cores(): lax.ppermute(v, ('fsdp', 'pre'), [(device(*p, c), device(*p, 1 - c)) for...]
    ppermute x1, waiting for transfers between devices: 1.25 us -> 3.99 us  [from_ring_across(): return lax.ppermute(v, ('fsdp', 'pre'), pairs)]
  transfers between devices with their start and end apart: 15 -> 15, of which waited for: 7 -> 9; matrix products, arithmetic and copies ran while one was open for 2% -> 2% of each run, Pallas kernels for 12% -> 10%
where the time goes in v3:
time: 123 us
  waiting for transfers between devices  31.8 us (26%)
  Pallas kernels  29.7 us (24%)
  blocking collectives  25 us (20%)
  starting transfers between devices  21.1 us (17%)
  local copies, waits for them, and re-layouts  14.5 us (12%)
    all_to_all x1, blocking collectives, body(): pieces = lax.all_to_all(pieces, 'fsdp', 0, 0, tiled=True)  25 us
    ppermute x6, waiting for transfers between devices, from_ring(): return lax.ppermute(v, ('fsdp', 'pre'), pairs)  19.7 us
    pallas_call x1, Pallas kernels, newton(): pl.pallas_call(newton_kernel, grid=(slots,), in_specs=[pl.BlockSpec((n_sr...  15.2 us
    unnamed x28, local copies, waits for them, and re-layouts  11 us
    ppermute x6, starting transfers between devices, from_ring(): return lax.ppermute(v, ('fsdp', 'pre'), pairs)  8.68 us
    all_to_all x1, starting transfers between devices, body(): mine = lax.all_to_all(mine, 'fsdp', 0, 0, tiled=True)  7.17 us
    pallas_call x1, Pallas kernels, fourth_powers(): pl.pallas_call(fourth_kernel, grid=(n,), in_specs=[spec], out_specs=[spec...  5.63 us
    pallas_call x1, Pallas kernels, first_chunks(): pl.pallas_call(first_kernel, in_specs=[pl.BlockSpec(memory_space=pltpu.SM...  4.98 us
  transfers between devices with their start and end apart: 15, of which 9 were waited for; matrix products, arithmetic and copies ran while one was open for 2% of the time, Pallas kernels for 10%

profile of v3, /device:TPU:0, one launch (start us, length us, event | category | flops | bytes accessed | tf_op | source)
XLA Modules:
  0.0 122.9 jit_solution(636690551749625733)
XLA Ops:
  0.7 0.0 copy-start.3
  0.7 1.2 dynamic-slice_bitcast_fusion.2
  1.9 0.1 pad_maximum_fusion
  1.9 0.1 collective-permute-start
  2.0 1.9 %collective-permute-done.r_ref = bf16[2,128,1024]{2,1,0:T(8,128)(2,1)S(1)} collective-permute-done((bf16[2,128,1024]{2,1,0:T(8,128)(2,1)S(1)}, bf16[2,128,1024]{2,1,0:T(8,128)(2,1)S(1)}, u32[]{:S(2)}, u32[]{:S(2)}) %collective-permute-start) | collective-permute-done | bytes 524320 | tf_op jit(solution)/shard_map/ppermute | solution.py:229
  4.0 0.1 pad_maximum_fusion.1.refs_0_
  4.0 3.2 %collective-permute-start.1 = (bf16[2,128,1024]{2,1,0:T(8,128)(2,1)S(1)}, bf16[2,128,1024]{2,1,0:T(8,128)(2,1)S(1)}, u32[]{:S(2)}, u32[]{:S(2)}) collective-permute-start(bf16[2,128,1024]{2,1,0:T(8,128)(2,1)S(1)} %pad_maximum_fusion.1.refs_0_), channel_id=1, source_target_pairs={{8,0},{33,1},{10,2},{35,3},{12,4},{37,5},{14,6},{39,7},{16,8},{41,... | collective-permute-start | bytes 1572872 | tf_op jit(solution)/shard_map/ppermute | solution.py:246
  7.2 0.6 collective-permute-start.2
  7.8 1.0 collective-permute-start.3
  8.8 0.0 copy-done.3
  8.8 1.0 shard_map.69
  9.8 7.2 %all-to-all-start = ((bf16[16,128,128]{2,1,0:T(8,128)(2,1)}), bf16[16,128,128]{2,1,0:T(8,128)(2,1)}, u32[]{:S(2)}, u32[]{:S(2)}) async-start(bf16[16,128,128]{2,1,0:T(8,128)(2,1)} %shard_map.69), calls=%async_computation | async-start | bytes 1048576 | tf_op jit(solution)/shard_map/all_to_all | solution.py:276
  17.0 6.4 %collective-permute-done.1.refs_1_ = bf16[2,128,1024]{2,1,0:T(8,128)(2,1)S(1)} collective-permute-done((bf16[2,128,1024]{2,1,0:T(8,128)(2,1)S(1)}, bf16[2,128,1024]{2,1,0:T(8,128)(2,1)S(1)}, u32[]{:S(2)}, u32[]{:S(2)}) %collective-permute-start.1) | collective-permute-done | bytes 524320 | tf_op jit(solution)/shard_map/ppermute | solution.py:246
  23.4 0.0 collective-permute-done.2.refs_2_
  23.4 0.0 copy-start.8
  23.4 0.8 copy-done.8
  24.2 2.1 %collective-permute-done.3.refs_3_ = bf16[2,128,1024]{2,1,0:T(8,128)(2,1)S(1)} collective-permute-done((bf16[2,128,1024]{2,1,0:T(8,128)(2,1)S(1)}, bf16[2,128,1024]{2,1,0:T(8,128)(2,1)S(1)}, u32[]{:S(2)}, u32[]{:S(2)}) %collective-permute-start.3) | collective-permute-done | bytes 524320 | tf_op jit(solution)/shard_map/ppermute | solution.py:246
  26.3 0.0 copy-start.10
  26.3 0.8 copy-done.10
  27.1 0.0 copy-start.9
  27.1 1.0 copy-done.9
  28.1 0.0 copy-start.11
  28.2 1.0 copy-done.11
  29.2 0.1 shard_map.68.refs_4_
  29.3 3.4 %all-to-all-done.refs_0_ = bf16[16,128,128]{2,1,0:T(8,128)(2,1)} async-done(((bf16[16,128,128]{2,1,0:T(8,128)(2,1)}), bf16[16,128,128]{2,1,0:T(8,128)(2,1)}, u32[]{:S(2)}, u32[]{:S(2)}) %all-to-all-start) | async-done | bytes 524320 | tf_op jit(solution)/shard_map/all_to_all | solution.py:276
  32.8 0.7 collective-permute-start.7
  33.4 1.4 %collective-permute-start.8 = (bf16[8,128,1024]{2,1,0:T(8,128)(2,1)S(1)}, bf16[8,128,1024]{2,1,0:T(8,128)(2,1)S(1)}, u32[]{:S(2)}, u32[]{:S(2)}) collective-permute-start(bf16[8,128,1024]{2,1,0:T(8,128)(2,1)S(1)} %shard_map.68.refs_4_), channel_id=1, source_target_pairs={{96,0},{25,1},{98,2},{27,3},{100,4},{29,5},{102,6},{31,7},{104,8},... | collective-permute-start | bytes 6291464 | tf_op jit(solution)/shard_map/ppermute | solution.py:246
  34.8 2.8 %collective-permute-start.4 = (bf16[16,128,128]{2,1,0:T(8,128)(2,1)}, bf16[16,128,128]{2,1,0:T(8,128)(2,1)}, u32[]{:S(2)}, u32[]{:S(2)}) collective-permute-start(bf16[16,128,128]{2,1,0:T(8,128)(2,1)} %all-to-all-done.refs_0_), channel_id=1, source_target_pairs={{2,0},{3,1},{4,2},{5,3},{6,4},{7,5},{0,6},{1,7},{10,8},{11,9},{12,... | collective-permute-start | bytes 1572872 | tf_op jit(solution)/shard_map/ppermute | solution.py:235
  37.6 0.8 collective-permute-start.5
  38.4 0.9 collective-permute-start.6
  39.2 2.8 %copy-done = f32[3,2,512,512]{3,2,1,0:T(8,128)S(1)} copy-done((f32[3,2,512,512]{3,2,1,0:T(8,128)S(1)}, f32[3,2,512,512]{3,2,1,0:T(8,128)}, u32[]{:S(2)}) %copy-start) | copy-done | bytes 6291480
  42.0 5.6 %shard_map.70 = (bf16[6,512,512]{2,1,0:T(8,128)(2,1)}, bf16[6,512,512]{2,1,0:T(8,128)(2,1)}) custom-call(f32[6,512,512]{2,1,0:T(8,128)S(1)} %bitcast.14), custom_call_target="tpu_custom_call" | custom-call | flops 1 | bytes 1 | tf_op jit(solution)/shard_map/pallas_call | solution.py:61
  47.7 11.2 %collective-permute-done.7.refs_5_ = bf16[8,128,1024]{2,1,0:T(8,128)(2,1)S(1)} collective-permute-done((bf16[8,128,1024]{2,1,0:T(8,128)(2,1)S(1)}, bf16[8,128,1024]{2,1,0:T(8,128)(2,1)S(1)}, u32[]{:S(2)}, u32[]{:S(2)}) %collective-permute-start.7) | collective-permute-done | bytes 2097184 | tf_op jit(solution)/shard_map/ppermute | solution.py:246
  58.8 1.1 slice.10
  59.9 1.9 %collective-permute-start.10 = (bf16[4,128,1024]{2,1,0:T(8,128)(2,1)}, bf16[4,128,1024]{2,1,0:T(8,128)(2,1)S(1)}, u32[]{:S(2)}, u32[]{:S(2)}) collective-permute-start(bf16[4,128,1024]{2,1,0:T(8,128)(2,1)} %slice.10), channel_id=1, source_target_pairs={{32,0},{9,1},{34,2},{11,3},{36,4},{13,5},{38,6},{15,7},{40,8},{17,... | collective-permute-start | bytes 3145736 | tf_op jit(solution)/shard_map/ppermute | solution.py:246
  61.8 0.0 collective-permute-done.8.refs_6_
  61.8 1.1 slice.13
  62.9 0.0 copy-done.4
  62.9 1.3 %copy-done.6 = bf16[8,128,1024]{2,1,0:T(8,128)(2,1)} copy-done((bf16[8,128,1024]{2,1,0:T(8,128)(2,1)}, bf16[8,128,1024]{2,1,0:T(8,128)(2,1)S(1)}, u32[]{:S(2)}) %copy-start.6) | copy-done | bytes 2097176
  64.2 0.0 collective-permute-start.11
  64.3 0.1 pad_add_fusion.place_ref
  64.3 0.0 collective-permute-done.4.refs_1_
  64.3 0.0 collective-permute-done.5.refs_2_
  64.3 0.0 collective-permute-done.6.refs_3_
  64.3 0.0 copy-start.5
  64.4 1.6 %copy-done.5 = bf16[8,128,1024]{2,1,0:T(8,128)(2,1)S(1)} copy-done((bf16[8,128,1024]{2,1,0:T(8,128)(2,1)S(1)}, bf16[8,128,1024]{2,1,0:T(8,128)(2,1)}, u32[]{:S(2)}) %copy-start.5) | copy-done | bytes 2097176
  65.9 1.6 %copy-done.7 = bf16[8,128,1024]{2,1,0:T(8,128)(2,1)S(1)} copy-done((bf16[8,128,1024]{2,1,0:T(8,128)(2,1)S(1)}, bf16[8,128,1024]{2,1,0:T(8,128)(2,1)}, u32[]{:S(2)}) %copy-start.7) | copy-done | bytes 2097176
  67.5 5.0 %shard_map.71 = (bf16[512,512]{1,0:T(8,128)(2,1)S(1)}, bf16[512,512]{1,0:T(8,128)(2,1)S(1)}, f32[512,1024]{1,0:T(8,128)S(1)}, bf16[512,512]{1,0:T(8,128)(2,1)S(1)}) custom-call(s32[4]{0:T(128)S(1)} %pad_add_fusion.place_ref, bf16[16,128,128]{2,1,0:T(8,128)(2,1)} %all-to-all-done.refs_0_, bf16[16,128,128]{2,1,0:T(8,128)(2,1)} %collective-permute-done.4.refs_1_, ...), custom_call_target="tpu_custom_call" | custom-call | flops 3221225472 | bytes 12582912 | tf_op jit(solution)/shard_map/pallas_call | solution.py:132
  72.5 0.1 collective-permute-start.12
  72.6 0.5 collective-permute-start.13
  73.1 0.1 collective-permute-start.9
  73.2 1.3 %collective-permute-done.12.share_0 = bf16[512,512]{1,0:T(8,128)(2,1)S(1)} collective-permute-done((bf16[512,512]{1,0:T(8,128)(2,1)S(1)}, bf16[512,512]{1,0:T(8,128)(2,1)S(1)}, u32[]{:S(2)}, u32[]{:S(2)}) %collective-permute-start.12) | collective-permute-done | bytes 524320 | tf_op jit(solution)/shard_map/ppermute | solution.py:229
  74.5 0.7 collective-permute-done.13.share_1
  75.3 0.7 collective-permute-done.9.cross_ref
  76.0 0.0 collective-permute-done.10.own_ref
  76.0 4.0 %collective-permute-done.11.far_ref = bf16[4,128,1024]{2,1,0:T(8,128)(2,1)} collective-permute-done((bf16[4,128,1024]{2,1,0:T(8,128)(2,1)}, bf16[4,128,1024]{2,1,0:T(8,128)(2,1)}, u32[]{:S(2)}, u32[]{:S(2)}) %collective-permute-start.11) | collective-permute-done | bytes 1048608 | tf_op jit(solution)/shard_map/ppermute | solution.py:255
  80.0 0.0 copy-done.12
  80.0 0.0 copy-done.13
  80.0 2.7 %shard_map.72 = bf16[48,32,512]{2,1,0:T(8,128)(2,1)S(1)} custom-call(s32[4]{0:T(128)S(1)} %pad_add_fusion.place_ref, s32[16,16]{1,0:T(8,128)S(1)} %copy-done.12, s32[16,16]{1,0:T(8,128)S(1)} %copy-done.13, bf16[512,512]{1,0:T(8,128)(2,1)S(1)} %get-tuple-element.18.lhs_ref, bf16[512,512]{1,0:T(8,128)(2,1)S(1)} %collective-permute-done.9.cross_ref, ...), custom_call_target="tpu_custom_call" | custom-call | flops 1 | bytes 1 | tf_op jit(solution)/shard_map/pallas_call | solution.py:165
  82.7 0.0 copy-start.1
  82.7 25.0 %all_to_all.10 = bf16[48,32,512]{2,1,0:T(8,128)(2,1)S(1)} all-to-all(bf16[48,32,512]{2,1,0:T(8,128)(2,1)S(1)} %shard_map.72), channel_id=1, replica_groups=mesh['fsdp'=16,'pre'=8] {'fsdp'}, dimensions={0} | all-to-all | bytes 3145728 | tf_op jit(solution)/shard_map/all_to_all | solution.py:291
  107.7 0.0 copy-done.2
  107.7 0.0 copy-done.1
  107.7 15.2 %shard_map.73 = (bf16[3,512,512]{2,1,0:T(8,128)(2,1)}, f32[3,2,512,512]{3,2,1,0:T(8,128)}) custom-call(bf16[16,3,32,512]{3,2,1,0:T(8,128)(2,1)S(1)} %bitcast.15, bf16[3,2,512,512]{3,2,1,0:T(8,128)(2,1)S(1)} %bitcast.16, bf16[3,2,512,512]{3,2,1,0:T(8,128)(2,1)S(1)} %bitcast.17), custom_call_target="tpu_custom_call" | custom-call | flops 1 | bytes 1 | tf_op jit(solution)/shard_map/pallas_call | solution.py:206
  (8 shorter events, 0.0 us)
Async XLA Ops:
  0.7 8.1 %copy-start.3 = (bf16[256,1024]{1,0:T(8,128)(2,1)S(1)}, bf16[256,1024]{1,0:T(8,128)(2,1)}, u32[]{:S(2)}) copy-start(bf16[256,1024]{1,0:T(8,128)(2,1)} %a_ref.1) | copy-start | bytes 1572868
  1.9 2.0 %collective-permute-start = (bf16[2,128,1024]{2,1,0:T(8,128)(2,1)S(1)}, bf16[2,128,1024]{2,1,0:T(8,128)(2,1)S(1)}, u32[]{:S(2)}, u32[]{:S(2)}) collective-permute-start(bf16[2,128,1024]{2,1,0:T(8,128)(2,1)S(1)} %pad_maximum_fusion), channel_id=1, source_target_pairs={{0,1},{1,0},{2,3},{3,2},{4,5},{5,4},{6,7},{7,6},{8,9},{9,8},{10,11... | collective-permute-start | bytes 1572872 | tf_op jit(solution)/shard_map/ppermute | solution.py:229
  4.0 19.4 %collective-permute-start.1 = (bf16[2,128,1024]{2,1,0:T(8,128)(2,1)S(1)}, bf16[2,128,1024]{2,1,0:T(8,128)(2,1)S(1)}, u32[]{:S(2)}, u32[]{:S(2)}) collective-permute-start(bf16[2,128,1024]{2,1,0:T(8,128)(2,1)S(1)} %pad_maximum_fusion.1.refs_0_), channel_id=1, source_target_pairs={{8,0},{33,1},{10,2},{35,3},{12,4},{37,5},{14,6},{39,7},{16,8},{41,... | collective-permute-start | bytes 1572872 | tf_op jit(solution)/shard_map/ppermute | solution.py:246
  7.2 16.2 %collective-permute-start.2 = (bf16[2,128,1024]{2,1,0:T(8,128)(2,1)S(1)}, bf16[2,128,1024]{2,1,0:T(8,128)(2,1)S(1)}, u32[]{:S(2)}, u32[]{:S(2)}) collective-permute-start(bf16[2,128,1024]{2,1,0:T(8,128)(2,1)S(1)} %pad_maximum_fusion.1.refs_0_), channel_id=1, source_target_pairs={{16,0},{65,1},{18,2},{67,3},{20,4},{69,5},{22,6},{71,7},{24,8},{73... | collective-permute-start | bytes 1572872 | tf_op jit(solution)/shard_map/ppermute | solution.py:246
  7.8 18.5 %collective-permute-start.3 = (bf16[2,128,1024]{2,1,0:T(8,128)(2,1)S(1)}, bf16[2,128,1024]{2,1,0:T(8,128)(2,1)S(1)}, u32[]{:S(2)}, u32[]{:S(2)}) collective-permute-start(bf16[2,128,1024]{2,1,0:T(8,128)(2,1)S(1)} %pad_maximum_fusion.1.refs_0_), channel_id=1, source_target_pairs={{24,0},{97,1},{26,2},{99,3},{28,4},{101,5},{30,6},{103,7},{0,8},{1... | collective-permute-start | bytes 1572872 | tf_op jit(solution)/shard_map/ppermute | solution.py:246
  9.8 23.0 %all-to-all-start = ((bf16[16,128,128]{2,1,0:T(8,128)(2,1)}), bf16[16,128,128]{2,1,0:T(8,128)(2,1)}, u32[]{:S(2)}, u32[]{:S(2)}) async-start(bf16[16,128,128]{2,1,0:T(8,128)(2,1)} %shard_map.69), calls=%async_computation | async-start | bytes 1048576 | tf_op jit(solution)/shard_map/all_to_all | solution.py:276
  23.4 0.8 copy-start.8
  26.3 0.8 copy-start.10
  27.1 1.0 copy-start.9
  28.1 1.0 copy-start.11
  32.8 26.0 %collective-permute-start.7 = (bf16[8,128,1024]{2,1,0:T(8,128)(2,1)S(1)}, bf16[8,128,1024]{2,1,0:T(8,128)(2,1)S(1)}, u32[]{:S(2)}, u32[]{:S(2)}) collective-permute-start(bf16[8,128,1024]{2,1,0:T(8,128)(2,1)S(1)} %shard_map.68.refs_4_), channel_id=1, source_target_pairs={{32,0},{9,1},{34,2},{11,3},{36,4},{13,5},{38,6},{15,7},{40,8},{17,... | collective-permute-start | bytes 6291464 | tf_op jit(solution)/shard_map/ppermute | solution.py:246
  33.4 28.3 %collective-permute-start.8 = (bf16[8,128,1024]{2,1,0:T(8,128)(2,1)S(1)}, bf16[8,128,1024]{2,1,0:T(8,128)(2,1)S(1)}, u32[]{:S(2)}, u32[]{:S(2)}) collective-permute-start(bf16[8,128,1024]{2,1,0:T(8,128)(2,1)S(1)} %shard_map.68.refs_4_), channel_id=1, source_target_pairs={{96,0},{25,1},{98,2},{27,3},{100,4},{29,5},{102,6},{31,7},{104,8},... | collective-permute-start | bytes 6291464 | tf_op jit(solution)/shard_map/ppermute | solution.py:246
  34.8 29.5 %collective-permute-start.4 = (bf16[16,128,128]{2,1,0:T(8,128)(2,1)}, bf16[16,128,128]{2,1,0:T(8,128)(2,1)}, u32[]{:S(2)}, u32[]{:S(2)}) collective-permute-start(bf16[16,128,128]{2,1,0:T(8,128)(2,1)} %all-to-all-done.refs_0_), channel_id=1, source_target_pairs={{2,0},{3,1},{4,2},{5,3},{6,4},{7,5},{0,6},{1,7},{10,8},{11,9},{12,... | collective-permute-start | bytes 1572872 | tf_op jit(solution)/shard_map/ppermute | solution.py:235
  37.6 26.8 %collective-permute-start.5 = (bf16[16,128,128]{2,1,0:T(8,128)(2,1)}, bf16[16,128,128]{2,1,0:T(8,128)(2,1)}, u32[]{:S(2)}, u32[]{:S(2)}) collective-permute-start(bf16[16,128,128]{2,1,0:T(8,128)(2,1)} %all-to-all-done.refs_0_), channel_id=1, source_target_pairs={{4,0},{5,1},{6,2},{7,3},{0,4},{1,5},{2,6},{3,7},{12,8},{13,9},{14,... | collective-permute-start | bytes 1572872 | tf_op jit(solution)/shard_map/ppermute | solution.py:235
  38.4 26.0 %collective-permute-start.6 = (bf16[16,128,128]{2,1,0:T(8,128)(2,1)}, bf16[16,128,128]{2,1,0:T(8,128)(2,1)}, u32[]{:S(2)}, u32[]{:S(2)}) collective-permute-start(bf16[16,128,128]{2,1,0:T(8,128)(2,1)} %all-to-all-done.refs_0_), channel_id=1, source_target_pairs={{6,0},{7,1},{0,2},{1,3},{2,4},{3,5},{4,6},{5,7},{14,8},{15,9},{8,1... | collective-permute-start | bytes 1572872 | tf_op jit(solution)/shard_map/ppermute | solution.py:235
  39.2 2.8 %copy-start = (f32[3,2,512,512]{3,2,1,0:T(8,128)S(1)}, f32[3,2,512,512]{3,2,1,0:T(8,128)}, u32[]{:S(2)}) copy-start(f32[3,2,512,512]{3,2,1,0:T(8,128)} %param.9) | copy-start | bytes 18874372
  58.8 4.1 %copy-start.4 = (bf16[8,128,1024]{2,1,0:T(8,128)(2,1)}, bf16[8,128,1024]{2,1,0:T(8,128)(2,1)S(1)}, u32[]{:S(2)}) copy-start(bf16[8,128,1024]{2,1,0:T(8,128)(2,1)S(1)} %collective-permute-done.7.refs_5_) | copy-start | bytes 6291460
  59.9 16.1 %collective-permute-start.10 = (bf16[4,128,1024]{2,1,0:T(8,128)(2,1)}, bf16[4,128,1024]{2,1,0:T(8,128)(2,1)S(1)}, u32[]{:S(2)}, u32[]{:S(2)}) collective-permute-start(bf16[4,128,1024]{2,1,0:T(8,128)(2,1)} %slice.10), channel_id=1, source_target_pairs={{32,0},{9,1},{34,2},{11,3},{36,4},{13,5},{38,6},{15,7},{40,8},{17,... | collective-permute-start | bytes 3145736 | tf_op jit(solution)/shard_map/ppermute | solution.py:246
  62.9 1.3 %copy-start.6 = (bf16[8,128,1024]{2,1,0:T(8,128)(2,1)}, bf16[8,128,1024]{2,1,0:T(8,128)(2,1)S(1)}, u32[]{:S(2)}) copy-start(bf16[8,128,1024]{2,1,0:T(8,128)(2,1)S(1)} %collective-permute-done.8.refs_6_) | copy-start | bytes 6291460
  64.2 15.8 %collective-permute-start.11 = (bf16[4,128,1024]{2,1,0:T(8,128)(2,1)}, bf16[4,128,1024]{2,1,0:T(8,128)(2,1)}, u32[]{:S(2)}, u32[]{:S(2)}) collective-permute-start(bf16[4,128,1024]{2,1,0:T(8,128)(2,1)} %slice.13), channel_id=1, source_target_pairs={{25,0},{96,1},{27,2},{98,3},{29,4},{100,5},{31,6},{102,7},{1,8},{1... | collective-permute-start | bytes 3145736 | tf_op jit(solution)/shard_map/ppermute | solution.py:255
  64.3 1.6 %copy-start.5 = (bf16[8,128,1024]{2,1,0:T(8,128)(2,1)S(1)}, bf16[8,128,1024]{2,1,0:T(8,128)(2,1)}, u32[]{:S(2)}) copy-start(bf16[8,128,1024]{2,1,0:T(8,128)(2,1)} %copy-done.4) | copy-start | bytes 6291460
  65.9 1.6 %copy-start.7 = (bf16[8,128,1024]{2,1,0:T(8,128)(2,1)S(1)}, bf16[8,128,1024]{2,1,0:T(8,128)(2,1)}, u32[]{:S(2)}) copy-start(bf16[8,128,1024]{2,1,0:T(8,128)(2,1)} %copy-done.6) | copy-start | bytes 6291460
  67.5 12.5 %copy-start.12 = (s32[16,16]{1,0:T(8,128)S(1)}, s32[16,16]{1,0:T(8,128)}, u32[]{:S(2)}) copy-start(s32[16,16]{1,0:T(8,128)} %owner_ref.1) | copy-start | bytes 3076
  67.5 12.5 %copy-start.13 = (s32[16,16]{1,0:T(8,128)S(1)}, s32[16,16]{1,0:T(8,128)}, u32[]{:S(2)}) copy-start(s32[16,16]{1,0:T(8,128)} %offs_ref.1) | copy-start | bytes 3076
  72.5 2.0 %collective-permute-start.12 = (bf16[512,512]{1,0:T(8,128)(2,1)S(1)}, bf16[512,512]{1,0:T(8,128)(2,1)S(1)}, u32[]{:S(2)}, u32[]{:S(2)}) collective-permute-start(bf16[512,512]{1,0:T(8,128)(2,1)S(1)} %get-tuple-element.20), channel_id=1, source_target_pairs={{0,1},{1,0},{2,3},{3,2},{4,5},{5,4},{6,7},{7,6},{8,9},{9,8},{10,11... | collective-permute-start | bytes 1572872 | tf_op jit(solution)/shard_map/ppermute | solution.py:229
  72.6 2.6 %collective-permute-start.13 = (bf16[512,512]{1,0:T(8,128)(2,1)S(1)}, bf16[512,512]{1,0:T(8,128)(2,1)S(1)}, u32[]{:S(2)}, u32[]{:S(2)}) collective-permute-start(bf16[512,512]{1,0:T(8,128)(2,1)S(1)} %get-tuple-element.21), channel_id=1, source_target_pairs={{0,1},{1,0},{2,3},{3,2},{4,5},{5,4},{6,7},{7,6},{8,9},{9,8},{10,11... | collective-permute-start | bytes 1572872 | tf_op jit(solution)/shard_map/ppermute | solution.py:229
  73.1 2.9 %collective-permute-start.9 = (bf16[512,512]{1,0:T(8,128)(2,1)S(1)}, bf16[512,512]{1,0:T(8,128)(2,1)S(1)}, u32[]{:S(2)}, u32[]{:S(2)}) collective-permute-start(bf16[512,512]{1,0:T(8,128)(2,1)S(1)} %get-tuple-element.18.lhs_ref), channel_id=1, source_target_pairs={{0,1},{1,0},{2,3},{3,2},{4,5},{5,4},{6,7},{7,6},{8,9},{9,8},{10,11... | collective-permute-start | bytes 1572872 | tf_op jit(solution)/shard_map/ppermute | solution.py:229
  80.0 27.7 %copy-start.2 = (bf16[6,512,512]{2,1,0:T(8,128)(2,1)S(1)}, bf16[6,512,512]{2,1,0:T(8,128)(2,1)}, u32[]{:S(2)}) copy-start(bf16[6,512,512]{2,1,0:T(8,128)(2,1)} %get-tuple-element.23) | copy-start | bytes 9437188
  82.7 25.0 %copy-start.1 = (bf16[6,512,512]{2,1,0:T(8,128)(2,1)S(1)}, bf16[6,512,512]{2,1,0:T(8,128)(2,1)}, u32[]{:S(2)}) copy-start(bf16[6,512,512]{2,1,0:T(8,128)(2,1)} %get-tuple-element.22) | copy-start | bytes 9437188

commit v4 on v3

--- a/solution.py
+++ b/solution.py
@@ -5,7 +5,6 @@
 from jax.experimental.pallas import tpu as pltpu
 from jax.sharding import PartitionSpec as P
 
-ITERS = 2
 BF = jnp.bfloat16
 F32 = jnp.float32
 VMEM = 12 * 1024 * 1024
@@ -52,7 +51,7 @@
     xb = x_ref[0].astype(BF)
     xb_ref[0] = xb
     sq = dot(xb, xb).astype(BF)
-    f_ref[0] = dot(sq, sq).astype(BF)
+    f_ref[0] = (0.25 * dot(sq, sq)).astype(BF)
 
 
 def fourth_powers(roots):
@@ -179,21 +178,15 @@
     gt = g.T
     g32 = g.astype(F32)
     scale = 0.1 / (jnp.sum(g32 * g32) / size + 1e-6)
-    rows, cols = (lax.broadcasted_iota(jnp.int32, (size, size), d) for d in range(2))
-    diagonal = rows == cols
-    stats = [dot(g, gt), dot(gt, g)]
-    damped = [(v * scale + jnp.where(diagonal, 1.0, 0.0)).astype(BF) for v in stats]
-    ms = [dot(f_ref[0, k], damped[k]) for k in range(2)]
-    xs = [xb_ref[0, k] for k in range(2)]
-    for it in range(ITERS):
-        fs = [(jnp.where(diagonal, 5.0 - m, -m) * 0.25).astype(BF) for m in ms]
-        if it < ITERS - 1:
-            twos = [dot(f, f).astype(BF) for f in fs]
-            xs = [dot(x, f).astype(BF) for x, f in zip(xs, fs)]
-            fours = [dot(v, v).astype(BF) for v in twos]
-            ms = [dot(v, m.astype(BF)) for v, m in zip(fours, ms)]
-        else:
-            xs = [dot(x, f) for x, f in zip(xs, fs)]
+    stats = [dot(g, gt).astype(BF), dot(gt, g).astype(BF)]
+    es = [(scale * dot(f_ref[0, k], stats[k]) + f_ref[0, k].astype(F32)).astype(BF) for k in range(2)]
+    squares = [dot(e, e) for e in es]
+    f_es = [(1.25 * e.astype(F32) - square).astype(BF) for e, square in zip(es, squares)]
+    ts = [(square - 2.5 * e.astype(F32)).astype(BF) for e, square in zip(es, squares)]
+    f_es = [(dot(t, v) + 1.5625 * v.astype(F32)).astype(BF) for t, v in zip(ts, f_es)]
+    f_es = [dot(t, v) + 1.5625 * v.astype(F32) for t, v in zip(ts, f_es)]
+    ws = [(1.25 * e.astype(F32) + v).astype(BF) for e, v in zip(es, f_es)]
+    xs = [1.5625 * xb_ref[0, k].astype(F32) - dot(xb_ref[0, k], ws[k]) for k in range(2)]
     for k in range(2):
         n_ref[0, k] = xs[k]
     left, right = (x.astype(BF) for x in xs)

time: 123 us -> 122 us (level)
  no operation moved by 1% of the time
where the time goes in v4:
time: 122 us
  waiting for transfers between devices  31.8 us (26%)
  Pallas kernels  28.7 us (24%)
  blocking collectives  25 us (20%)
  starting transfers between devices  21.1 us (17%)
  local copies, waits for them, and re-layouts  14.5 us (12%)
    all_to_all x1, blocking collectives, body(): pieces = lax.all_to_all(pieces, 'fsdp', 0, 0, tiled=True)  25 us
    ppermute x6, waiting for transfers between devices, from_ring(): return lax.ppermute(v, ('fsdp', 'pre'), pairs)  19.7 us
    pallas_call x1, Pallas kernels, newton(): pl.pallas_call(newton_kernel, grid=(slots,), in_specs=[pl.BlockSpec((n_sr...  14.3 us
    unnamed x28, local copies, waits for them, and re-layouts  11 us
    ppermute x6, starting transfers between devices, from_ring(): return lax.ppermute(v, ('fsdp', 'pre'), pairs)  8.68 us
    all_to_all x1, starting transfers between devices, body(): mine = lax.all_to_all(mine, 'fsdp', 0, 0, tiled=True)  7.17 us
    pallas_call x1, Pallas kernels, fourth_powers(): pl.pallas_call(fourth_kernel, grid=(n,), in_specs=[spec], out_specs=[spec...  5.63 us
    pallas_call x1, Pallas kernels, first_chunks(): pl.pallas_call(first_kernel, in_specs=[pl.BlockSpec(memory_space=pltpu.SM...  4.98 us
  transfers between devices with their start and end apart: 15, of which 9 were waited for; matrix products, arithmetic and copies ran while one was open for 2% of the time, Pallas kernels for 10%

profile of v4, /device:TPU:0, one launch (start us, length us, event | category | flops | bytes accessed | tf_op | source)
XLA Modules:
  0.0 122.0 jit_solution(5306805260068216948)
XLA Ops:
  0.7 0.0 copy-start.3
  0.7 1.2 %dynamic-slice_bitcast_fusion.2 = (bf16[1,128,1024]{2,1,0:T(8,128)(2,1)S(1)}, bf16[1,128,1024]{2,1,0:T(8,128)(2,1)S(1)}, bf16[1,128,1024]{2,1,0:T(8,128)(2,1)S(1)}) fusion(bf16[256,1024]{1,0:T(8,128)(2,1)} %param.6, s32[]{:T(128)S(6)} %select_n.29, s32[]{:T(128)S(6)} %select_n.30, bf16[256,1024]{1,0:T(8,128)(2,1)} %a_ref.1), kind=kLoop, calls=%fused_computation.4 | loop fusion | bytes 1572872 | tf_op jit(solution)/shard_map/stack | solution.py:263
  1.9 0.1 pad_maximum_fusion
  1.9 0.1 collective-permute-start
  2.0 1.9 %collective-permute-done.r_ref = bf16[2,128,1024]{2,1,0:T(8,128)(2,1)S(1)} collective-permute-done((bf16[2,128,1024]{2,1,0:T(8,128)(2,1)S(1)}, bf16[2,128,1024]{2,1,0:T(8,128)(2,1)S(1)}, u32[]{:S(2)}, u32[]{:S(2)}) %collective-permute-start) | collective-permute-done | bytes 524320 | tf_op jit(solution)/shard_map/ppermute | solution.py:222
  4.0 0.1 pad_maximum_fusion.1.refs_0_
  4.0 3.2 %collective-permute-start.1 = (bf16[2,128,1024]{2,1,0:T(8,128)(2,1)S(1)}, bf16[2,128,1024]{2,1,0:T(8,128)(2,1)S(1)}, u32[]{:S(2)}, u32[]{:S(2)}) collective-permute-start(bf16[2,128,1024]{2,1,0:T(8,128)(2,1)S(1)} %pad_maximum_fusion.1.refs_0_), channel_id=1, source_target_pairs={{8,0},{33,1},{10,2},{35,3},{12,4},{37,5},{14,6},{39,7},{16,8},{41,... | collective-permute-start | bytes 1572872 | tf_op jit(solution)/shard_map/ppermute | solution.py:239
  7.2 0.6 collective-permute-start.2
  7.8 1.0 collective-permute-start.3
  8.8 0.0 copy-done.3
  8.8 1.0 shard_map.69
  9.8 7.2 %all-to-all-start = ((bf16[16,128,128]{2,1,0:T(8,128)(2,1)}), bf16[16,128,128]{2,1,0:T(8,128)(2,1)}, u32[]{:S(2)}, u32[]{:S(2)}) async-start(bf16[16,128,128]{2,1,0:T(8,128)(2,1)} %shard_map.69), calls=%async_computation | async-start | bytes 1048576 | tf_op jit(solution)/shard_map/all_to_all | solution.py:269
  17.0 6.4 %collective-permute-done.1.refs_1_ = bf16[2,128,1024]{2,1,0:T(8,128)(2,1)S(1)} collective-permute-done((bf16[2,128,1024]{2,1,0:T(8,128)(2,1)S(1)}, bf16[2,128,1024]{2,1,0:T(8,128)(2,1)S(1)}, u32[]{:S(2)}, u32[]{:S(2)}) %collective-permute-start.1) | collective-permute-done | bytes 524320 | tf_op jit(solution)/shard_map/ppermute | solution.py:239
  23.4 0.0 collective-permute-done.2.refs_2_
  23.4 0.0 copy-start.8
  23.4 0.8 copy-done.8
  24.2 2.1 %collective-permute-done.3.refs_3_ = bf16[2,128,1024]{2,1,0:T(8,128)(2,1)S(1)} collective-permute-done((bf16[2,128,1024]{2,1,0:T(8,128)(2,1)S(1)}, bf16[2,128,1024]{2,1,0:T(8,128)(2,1)S(1)}, u32[]{:S(2)}, u32[]{:S(2)}) %collective-permute-start.3) | collective-permute-done | bytes 524320 | tf_op jit(solution)/shard_map/ppermute | solution.py:239
  26.3 0.0 copy-start.10
  26.3 0.8 copy-done.10
  27.1 0.0 copy-start.9
  27.1 1.0 copy-done.9
  28.1 0.0 copy-start.11
  28.2 1.0 copy-done.11
  29.2 0.1 shard_map.68.refs_4_
  29.3 3.4 %all-to-all-done.refs_0_ = bf16[16,128,128]{2,1,0:T(8,128)(2,1)} async-done(((bf16[16,128,128]{2,1,0:T(8,128)(2,1)}), bf16[16,128,128]{2,1,0:T(8,128)(2,1)}, u32[]{:S(2)}, u32[]{:S(2)}) %all-to-all-start) | async-done | bytes 524320 | tf_op jit(solution)/shard_map/all_to_all | solution.py:269
  32.8 0.7 collective-permute-start.7
  33.4 1.4 %collective-permute-start.8 = (bf16[8,128,1024]{2,1,0:T(8,128)(2,1)S(1)}, bf16[8,128,1024]{2,1,0:T(8,128)(2,1)S(1)}, u32[]{:S(2)}, u32[]{:S(2)}) collective-permute-start(bf16[8,128,1024]{2,1,0:T(8,128)(2,1)S(1)} %shard_map.68.refs_4_), channel_id=1, source_target_pairs={{96,0},{25,1},{98,2},{27,3},{100,4},{29,5},{102,6},{31,7},{104,8},... | collective-permute-start | bytes 6291464 | tf_op jit(solution)/shard_map/ppermute | solution.py:239
  34.8 2.8 %collective-permute-start.4 = (bf16[16,128,128]{2,1,0:T(8,128)(2,1)}, bf16[16,128,128]{2,1,0:T(8,128)(2,1)}, u32[]{:S(2)}, u32[]{:S(2)}) collective-permute-start(bf16[16,128,128]{2,1,0:T(8,128)(2,1)} %all-to-all-done.refs_0_), channel_id=1, source_target_pairs={{2,0},{3,1},{4,2},{5,3},{6,4},{7,5},{0,6},{1,7},{10,8},{11,9},{12,... | collective-permute-start | bytes 1572872 | tf_op jit(solution)/shard_map/ppermute | solution.py:228
  37.6 0.8 collective-permute-start.5
  38.4 0.9 collective-permute-start.6
  39.2 2.8 %copy-done = f32[3,2,512,512]{3,2,1,0:T(8,128)S(1)} copy-done((f32[3,2,512,512]{3,2,1,0:T(8,128)S(1)}, f32[3,2,512,512]{3,2,1,0:T(8,128)}, u32[]{:S(2)}) %copy-start) | copy-done | bytes 6291480
  42.0 5.6 %shard_map.70 = (bf16[6,512,512]{2,1,0:T(8,128)(2,1)}, bf16[6,512,512]{2,1,0:T(8,128)(2,1)}) custom-call(f32[6,512,512]{2,1,0:T(8,128)S(1)} %bitcast.14), custom_call_target="tpu_custom_call" | custom-call | flops 1 | bytes 1 | tf_op jit(solution)/shard_map/pallas_call | solution.py:60
  47.7 11.1 %collective-permute-done.7.refs_5_ = bf16[8,128,1024]{2,1,0:T(8,128)(2,1)S(1)} collective-permute-done((bf16[8,128,1024]{2,1,0:T(8,128)(2,1)S(1)}, bf16[8,128,1024]{2,1,0:T(8,128)(2,1)S(1)}, u32[]{:S(2)}, u32[]{:S(2)}) %collective-permute-start.7) | collective-permute-done | bytes 2097184 | tf_op jit(solution)/shard_map/ppermute | solution.py:239
  58.8 1.1 slice.10
  59.9 1.9 %collective-permute-start.10 = (bf16[4,128,1024]{2,1,0:T(8,128)(2,1)}, bf16[4,128,1024]{2,1,0:T(8,128)(2,1)S(1)}, u32[]{:S(2)}, u32[]{:S(2)}) collective-permute-start(bf16[4,128,1024]{2,1,0:T(8,128)(2,1)} %slice.10), channel_id=1, source_target_pairs={{32,0},{9,1},{34,2},{11,3},{36,4},{13,5},{38,6},{15,7},{40,8},{17,... | collective-permute-start | bytes 3145736 | tf_op jit(solution)/shard_map/ppermute | solution.py:239
  61.8 0.0 collective-permute-done.8.refs_6_
  61.8 1.1 slice.13
  62.9 0.0 copy-done.4
  62.9 1.3 %copy-done.6 = bf16[8,128,1024]{2,1,0:T(8,128)(2,1)} copy-done((bf16[8,128,1024]{2,1,0:T(8,128)(2,1)}, bf16[8,128,1024]{2,1,0:T(8,128)(2,1)S(1)}, u32[]{:S(2)}) %copy-start.6) | copy-done | bytes 2097176
  64.2 0.0 collective-permute-start.11
  64.3 0.1 pad_add_fusion.place_ref
  64.3 0.0 collective-permute-done.4.refs_1_
  64.3 0.0 collective-permute-done.5.refs_2_
  64.3 0.0 collective-permute-done.6.refs_3_
  64.3 0.0 copy-start.5
  64.4 1.6 %copy-done.5 = bf16[8,128,1024]{2,1,0:T(8,128)(2,1)S(1)} copy-done((bf16[8,128,1024]{2,1,0:T(8,128)(2,1)S(1)}, bf16[8,128,1024]{2,1,0:T(8,128)(2,1)}, u32[]{:S(2)}) %copy-start.5) | copy-done | bytes 2097176
  65.9 1.6 %copy-done.7 = bf16[8,128,1024]{2,1,0:T(8,128)(2,1)S(1)} copy-done((bf16[8,128,1024]{2,1,0:T(8,128)(2,1)S(1)}, bf16[8,128,1024]{2,1,0:T(8,128)(2,1)}, u32[]{:S(2)}) %copy-start.7) | copy-done | bytes 2097176
  67.5 5.0 %shard_map.71 = (bf16[512,512]{1,0:T(8,128)(2,1)S(1)}, bf16[512,512]{1,0:T(8,128)(2,1)S(1)}, f32[512,1024]{1,0:T(8,128)S(1)}, bf16[512,512]{1,0:T(8,128)(2,1)S(1)}) custom-call(s32[4]{0:T(128)S(1)} %pad_add_fusion.place_ref, bf16[16,128,128]{2,1,0:T(8,128)(2,1)} %all-to-all-done.refs_0_, bf16[16,128,128]{2,1,0:T(8,128)(2,1)} %collective-permute-done.4.refs_1_, ...), custom_call_target="tpu_custom_call" | custom-call | flops 3221225472 | bytes 12582912 | tf_op jit(solution)/shard_map/pallas_call | solution.py:131
  72.5 0.1 collective-permute-start.12
  72.6 0.5 collective-permute-start.13
  73.1 0.1 collective-permute-start.9
  73.2 1.3 %collective-permute-done.12.share_0 = bf16[512,512]{1,0:T(8,128)(2,1)S(1)} collective-permute-done((bf16[512,512]{1,0:T(8,128)(2,1)S(1)}, bf16[512,512]{1,0:T(8,128)(2,1)S(1)}, u32[]{:S(2)}, u32[]{:S(2)}) %collective-permute-start.12) | collective-permute-done | bytes 524320 | tf_op jit(solution)/shard_map/ppermute | solution.py:222
  74.5 0.7 collective-permute-done.13.share_1
  75.3 0.7 collective-permute-done.9.cross_ref
  76.0 0.0 collective-permute-done.10.own_ref
  76.0 4.0 %collective-permute-done.11.far_ref = bf16[4,128,1024]{2,1,0:T(8,128)(2,1)} collective-permute-done((bf16[4,128,1024]{2,1,0:T(8,128)(2,1)}, bf16[4,128,1024]{2,1,0:T(8,128)(2,1)}, u32[]{:S(2)}, u32[]{:S(2)}) %collective-permute-start.11) | collective-permute-done | bytes 1048608 | tf_op jit(solution)/shard_map/ppermute | solution.py:248
  80.0 0.0 copy-done.12
  80.0 0.0 copy-done.13
  80.0 2.7 %shard_map.72 = bf16[48,32,512]{2,1,0:T(8,128)(2,1)S(1)} custom-call(s32[4]{0:T(128)S(1)} %pad_add_fusion.place_ref, s32[16,16]{1,0:T(8,128)S(1)} %copy-done.12, s32[16,16]{1,0:T(8,128)S(1)} %copy-done.13, bf16[512,512]{1,0:T(8,128)(2,1)S(1)} %get-tuple-element.18.lhs_ref, bf16[512,512]{1,0:T(8,128)(2,1)S(1)} %collective-permute-done.9.cross_ref, ...), custom_call_target="tpu_custom_call" | custom-call | flops 1 | bytes 1 | tf_op jit(solution)/shard_map/pallas_call | solution.py:164
  82.7 0.0 copy-start.1
  82.7 25.0 %all_to_all.10 = bf16[48,32,512]{2,1,0:T(8,128)(2,1)S(1)} all-to-all(bf16[48,32,512]{2,1,0:T(8,128)(2,1)S(1)} %shard_map.72), channel_id=1, replica_groups=mesh['fsdp'=16,'pre'=8] {'fsdp'}, dimensions={0} | all-to-all | bytes 3145728 | tf_op jit(solution)/shard_map/all_to_all | solution.py:284
  107.7 0.0 copy-done.2
  107.7 0.0 copy-done.1
  107.7 14.3 %shard_map.73 = (bf16[3,512,512]{2,1,0:T(8,128)(2,1)}, f32[3,2,512,512]{3,2,1,0:T(8,128)}) custom-call(bf16[16,3,32,512]{3,2,1,0:T(8,128)(2,1)S(1)} %bitcast.15, bf16[3,2,512,512]{3,2,1,0:T(8,128)(2,1)S(1)} %bitcast.16, bf16[3,2,512,512]{3,2,1,0:T(8,128)(2,1)S(1)} %bitcast.17), custom_call_target="tpu_custom_call" | custom-call | flops 1 | bytes 1 | tf_op jit(solution)/shard_map/pallas_call | solution.py:199
  (8 shorter events, 0.0 us)
Async XLA Ops:
  0.7 8.1 %copy-start.3 = (bf16[256,1024]{1,0:T(8,128)(2,1)S(1)}, bf16[256,1024]{1,0:T(8,128)(2,1)}, u32[]{:S(2)}) copy-start(bf16[256,1024]{1,0:T(8,128)(2,1)} %a_ref.1) | copy-start | bytes 1572868
  1.9 2.0 %collective-permute-start = (bf16[2,128,1024]{2,1,0:T(8,128)(2,1)S(1)}, bf16[2,128,1024]{2,1,0:T(8,128)(2,1)S(1)}, u32[]{:S(2)}, u32[]{:S(2)}) collective-permute-start(bf16[2,128,1024]{2,1,0:T(8,128)(2,1)S(1)} %pad_maximum_fusion), channel_id=1, source_target_pairs={{0,1},{1,0},{2,3},{3,2},{4,5},{5,4},{6,7},{7,6},{8,9},{9,8},{10,11... | collective-permute-start | bytes 1572872 | tf_op jit(solution)/shard_map/ppermute | solution.py:222
  4.0 19.4 %collective-permute-start.1 = (bf16[2,128,1024]{2,1,0:T(8,128)(2,1)S(1)}, bf16[2,128,1024]{2,1,0:T(8,128)(2,1)S(1)}, u32[]{:S(2)}, u32[]{:S(2)}) collective-permute-start(bf16[2,128,1024]{2,1,0:T(8,128)(2,1)S(1)} %pad_maximum_fusion.1.refs_0_), channel_id=1, source_target_pairs={{8,0},{33,1},{10,2},{35,3},{12,4},{37,5},{14,6},{39,7},{16,8},{41,... | collective-permute-start | bytes 1572872 | tf_op jit(solution)/shard_map/ppermute | solution.py:239
  7.2 16.2 %collective-permute-start.2 = (bf16[2,128,1024]{2,1,0:T(8,128)(2,1)S(1)}, bf16[2,128,1024]{2,1,0:T(8,128)(2,1)S(1)}, u32[]{:S(2)}, u32[]{:S(2)}) collective-permute-start(bf16[2,128,1024]{2,1,0:T(8,128)(2,1)S(1)} %pad_maximum_fusion.1.refs_0_), channel_id=1, source_target_pairs={{16,0},{65,1},{18,2},{67,3},{20,4},{69,5},{22,6},{71,7},{24,8},{73... | collective-permute-start | bytes 1572872 | tf_op jit(solution)/shard_map/ppermute | solution.py:239
  7.8 18.5 %collective-permute-start.3 = (bf16[2,128,1024]{2,1,0:T(8,128)(2,1)S(1)}, bf16[2,128,1024]{2,1,0:T(8,128)(2,1)S(1)}, u32[]{:S(2)}, u32[]{:S(2)}) collective-permute-start(bf16[2,128,1024]{2,1,0:T(8,128)(2,1)S(1)} %pad_maximum_fusion.1.refs_0_), channel_id=1, source_target_pairs={{24,0},{97,1},{26,2},{99,3},{28,4},{101,5},{30,6},{103,7},{0,8},{1... | collective-permute-start | bytes 1572872 | tf_op jit(solution)/shard_map/ppermute | solution.py:239
  9.8 23.0 %all-to-all-start = ((bf16[16,128,128]{2,1,0:T(8,128)(2,1)}), bf16[16,128,128]{2,1,0:T(8,128)(2,1)}, u32[]{:S(2)}, u32[]{:S(2)}) async-start(bf16[16,128,128]{2,1,0:T(8,128)(2,1)} %shard_map.69), calls=%async_computation | async-start | bytes 1048576 | tf_op jit(solution)/shard_map/all_to_all | solution.py:269
  23.4 0.8 copy-start.8
  26.3 0.8 copy-start.10
  27.1 1.0 copy-start.9
  28.1 1.0 copy-start.11
  32.8 26.0 %collective-permute-start.7 = (bf16[8,128,1024]{2,1,0:T(8,128)(2,1)S(1)}, bf16[8,128,1024]{2,1,0:T(8,128)(2,1)S(1)}, u32[]{:S(2)}, u32[]{:S(2)}) collective-permute-start(bf16[8,128,1024]{2,1,0:T(8,128)(2,1)S(1)} %shard_map.68.refs_4_), channel_id=1, source_target_pairs={{32,0},{9,1},{34,2},{11,3},{36,4},{13,5},{38,6},{15,7},{40,8},{17,... | collective-permute-start | bytes 6291464 | tf_op jit(solution)/shard_map/ppermute | solution.py:239
  33.4 28.3 %collective-permute-start.8 = (bf16[8,128,1024]{2,1,0:T(8,128)(2,1)S(1)}, bf16[8,128,1024]{2,1,0:T(8,128)(2,1)S(1)}, u32[]{:S(2)}, u32[]{:S(2)}) collective-permute-start(bf16[8,128,1024]{2,1,0:T(8,128)(2,1)S(1)} %shard_map.68.refs_4_), channel_id=1, source_target_pairs={{96,0},{25,1},{98,2},{27,3},{100,4},{29,5},{102,6},{31,7},{104,8},... | collective-permute-start | bytes 6291464 | tf_op jit(solution)/shard_map/ppermute | solution.py:239
  34.8 29.5 %collective-permute-start.4 = (bf16[16,128,128]{2,1,0:T(8,128)(2,1)}, bf16[16,128,128]{2,1,0:T(8,128)(2,1)}, u32[]{:S(2)}, u32[]{:S(2)}) collective-permute-start(bf16[16,128,128]{2,1,0:T(8,128)(2,1)} %all-to-all-done.refs_0_), channel_id=1, source_target_pairs={{2,0},{3,1},{4,2},{5,3},{6,4},{7,5},{0,6},{1,7},{10,8},{11,9},{12,... | collective-permute-start | bytes 1572872 | tf_op jit(solution)/shard_map/ppermute | solution.py:228
  37.6 26.8 %collective-permute-start.5 = (bf16[16,128,128]{2,1,0:T(8,128)(2,1)}, bf16[16,128,128]{2,1,0:T(8,128)(2,1)}, u32[]{:S(2)}, u32[]{:S(2)}) collective-permute-start(bf16[16,128,128]{2,1,0:T(8,128)(2,1)} %all-to-all-done.refs_0_), channel_id=1, source_target_pairs={{4,0},{5,1},{6,2},{7,3},{0,4},{1,5},{2,6},{3,7},{12,8},{13,9},{14,... | collective-permute-start | bytes 1572872 | tf_op jit(solution)/shard_map/ppermute | solution.py:228
  38.4 26.0 %collective-permute-start.6 = (bf16[16,128,128]{2,1,0:T(8,128)(2,1)}, bf16[16,128,128]{2,1,0:T(8,128)(2,1)}, u32[]{:S(2)}, u32[]{:S(2)}) collective-permute-start(bf16[16,128,128]{2,1,0:T(8,128)(2,1)} %all-to-all-done.refs_0_), channel_id=1, source_target_pairs={{6,0},{7,1},{0,2},{1,3},{2,4},{3,5},{4,6},{5,7},{14,8},{15,9},{8,1... | collective-permute-start | bytes 1572872 | tf_op jit(solution)/shard_map/ppermute | solution.py:228
  39.2 2.8 %copy-start = (f32[3,2,512,512]{3,2,1,0:T(8,128)S(1)}, f32[3,2,512,512]{3,2,1,0:T(8,128)}, u32[]{:S(2)}) copy-start(f32[3,2,512,512]{3,2,1,0:T(8,128)} %param.9) | copy-start | bytes 18874372
  58.8 4.1 %copy-start.4 = (bf16[8,128,1024]{2,1,0:T(8,128)(2,1)}, bf16[8,128,1024]{2,1,0:T(8,128)(2,1)S(1)}, u32[]{:S(2)}) copy-start(bf16[8,128,1024]{2,1,0:T(8,128)(2,1)S(1)} %collective-permute-done.7.refs_5_) | copy-start | bytes 6291460
  59.9 16.1 %collective-permute-start.10 = (bf16[4,128,1024]{2,1,0:T(8,128)(2,1)}, bf16[4,128,1024]{2,1,0:T(8,128)(2,1)S(1)}, u32[]{:S(2)}, u32[]{:S(2)}) collective-permute-start(bf16[4,128,1024]{2,1,0:T(8,128)(2,1)} %slice.10), channel_id=1, source_target_pairs={{32,0},{9,1},{34,2},{11,3},{36,4},{13,5},{38,6},{15,7},{40,8},{17,... | collective-permute-start | bytes 3145736 | tf_op jit(solution)/shard_map/ppermute | solution.py:239
  62.9 1.3 %copy-start.6 = (bf16[8,128,1024]{2,1,0:T(8,128)(2,1)}, bf16[8,128,1024]{2,1,0:T(8,128)(2,1)S(1)}, u32[]{:S(2)}) copy-start(bf16[8,128,1024]{2,1,0:T(8,128)(2,1)S(1)} %collective-permute-done.8.refs_6_) | copy-start | bytes 6291460
  64.2 15.8 %collective-permute-start.11 = (bf16[4,128,1024]{2,1,0:T(8,128)(2,1)}, bf16[4,128,1024]{2,1,0:T(8,128)(2,1)}, u32[]{:S(2)}, u32[]{:S(2)}) collective-permute-start(bf16[4,128,1024]{2,1,0:T(8,128)(2,1)} %slice.13), channel_id=1, source_target_pairs={{25,0},{96,1},{27,2},{98,3},{29,4},{100,5},{31,6},{102,7},{1,8},{1... | collective-permute-start | bytes 3145736 | tf_op jit(solution)/shard_map/ppermute | solution.py:248
  64.3 1.6 %copy-start.5 = (bf16[8,128,1024]{2,1,0:T(8,128)(2,1)S(1)}, bf16[8,128,1024]{2,1,0:T(8,128)(2,1)}, u32[]{:S(2)}) copy-start(bf16[8,128,1024]{2,1,0:T(8,128)(2,1)} %copy-done.4) | copy-start | bytes 6291460
  65.9 1.6 %copy-start.7 = (bf16[8,128,1024]{2,1,0:T(8,128)(2,1)S(1)}, bf16[8,128,1024]{2,1,0:T(8,128)(2,1)}, u32[]{:S(2)}) copy-start(bf16[8,128,1024]{2,1,0:T(8,128)(2,1)} %copy-done.6) | copy-start | bytes 6291460
  67.5 12.5 %copy-start.12 = (s32[16,16]{1,0:T(8,128)S(1)}, s32[16,16]{1,0:T(8,128)}, u32[]{:S(2)}) copy-start(s32[16,16]{1,0:T(8,128)} %owner_ref.1) | copy-start | bytes 3076
  67.5 12.5 %copy-start.13 = (s32[16,16]{1,0:T(8,128)S(1)}, s32[16,16]{1,0:T(8,128)}, u32[]{:S(2)}) copy-start(s32[16,16]{1,0:T(8,128)} %offs_ref.1) | copy-start | bytes 3076
  72.5 2.0 %collective-permute-start.12 = (bf16[512,512]{1,0:T(8,128)(2,1)S(1)}, bf16[512,512]{1,0:T(8,128)(2,1)S(1)}, u32[]{:S(2)}, u32[]{:S(2)}) collective-permute-start(bf16[512,512]{1,0:T(8,128)(2,1)S(1)} %get-tuple-element.20), channel_id=1, source_target_pairs={{0,1},{1,0},{2,3},{3,2},{4,5},{5,4},{6,7},{7,6},{8,9},{9,8},{10,11... | collective-permute-start | bytes 1572872 | tf_op jit(solution)/shard_map/ppermute | solution.py:222
  72.6 2.6 %collective-permute-start.13 = (bf16[512,512]{1,0:T(8,128)(2,1)S(1)}, bf16[512,512]{1,0:T(8,128)(2,1)S(1)}, u32[]{:S(2)}, u32[]{:S(2)}) collective-permute-start(bf16[512,512]{1,0:T(8,128)(2,1)S(1)} %get-tuple-element.21), channel_id=1, source_target_pairs={{0,1},{1,0},{2,3},{3,2},{4,5},{5,4},{6,7},{7,6},{8,9},{9,8},{10,11... | collective-permute-start | bytes 1572872 | tf_op jit(solution)/shard_map/ppermute | solution.py:222
  73.1 2.9 %collective-permute-start.9 = (bf16[512,512]{1,0:T(8,128)(2,1)S(1)}, bf16[512,512]{1,0:T(8,128)(2,1)S(1)}, u32[]{:S(2)}, u32[]{:S(2)}) collective-permute-start(bf16[512,512]{1,0:T(8,128)(2,1)S(1)} %get-tuple-element.18.lhs_ref), channel_id=1, source_target_pairs={{0,1},{1,0},{2,3},{3,2},{4,5},{5,4},{6,7},{7,6},{8,9},{9,8},{10,11... | collective-permute-start | bytes 1572872 | tf_op jit(solution)/shard_map/ppermute | solution.py:222
  80.0 27.7 %copy-start.2 = (bf16[6,512,512]{2,1,0:T(8,128)(2,1)S(1)}, bf16[6,512,512]{2,1,0:T(8,128)(2,1)}, u32[]{:S(2)}) copy-start(bf16[6,512,512]{2,1,0:T(8,128)(2,1)} %get-tuple-element.23) | copy-start | bytes 9437188
  82.7 25.0 %copy-start.1 = (bf16[6,512,512]{2,1,0:T(8,128)(2,1)S(1)}, bf16[6,512,512]{2,1,0:T(8,128)(2,1)}, u32[]{:S(2)}) copy-start(bf16[6,512,512]{2,1,0:T(8,128)(2,1)} %get-tuple-element.22) | copy-start | bytes 9437188

commit v5 on v4

--- a/solution.py
+++ b/solution.py
@@ -21,10 +21,10 @@
     return pltpu.CompilerParams(vmem_limit_bytes=VMEM, **kw)
 
 
-def split_kernel(core_ref, a_ref, r_ref, o_ref):
+def split_kernel(place_ref, a_ref, r_ref, o_ref):
     pieces, rows, tokens = o_ref.shape
     part = rows // 4
-    start = pl.multiple_of(core_ref[0] * tokens, tokens)
+    start = pl.multiple_of(place_ref[3] * tokens, tokens)
     for o in range(2):
         flipped = (a_ref[pl.ds(start, tokens), :] if o == 0 else r_ref[0]).T
         for r in range(2):
@@ -33,7 +33,7 @@
                 o_ref[f, to : to + part, :] = flipped[at : at + part, :]
 
 
-def split_features(core, a, recv):
+def split_features(place, a, recv):
     tokens, feats = a.shape
     whole = lambda s: pl.BlockSpec(s, lambda i: (0,) * len(s))
     return pl.pallas_call(
@@ -44,7 +44,7 @@
         out_shape=jax.ShapeDtypeStruct((16, feats // 8, tokens // 2), BF),
         compiler_params=params(),
         cost_estimate=SHORT,
-    )(core, a, recv)
+    )(place, a, recv)
 
 
 def fourth_kernel(x_ref, xb_ref, f_ref):
@@ -66,6 +66,22 @@
         compiler_params=pltpu.CompilerParams(vmem_limit_bytes=MIDDLE_VMEM),
         cost_estimate=SHORT,
     )(roots)
+
+
+def copy_kernel(v_ref, o_ref):
+    o_ref[...] = v_ref[...]
+
+
+def to_vmem(v):
+    vmem = pl.BlockSpec(memory_space=pltpu.VMEM)
+    return pl.pallas_call(
+        copy_kernel,
+        in_specs=[vmem],
+        out_specs=vmem,
+        out_shape=jax.ShapeDtypeStruct(v.shape, v.dtype),
+        compiler_params=params(),
+        cost_estimate=SHORT,
+    )(v)
 
 
 def join_kernel(*refs):
@@ -265,11 +281,12 @@
     near = [shard, from_ring(shard, 0, 1), from_ring(shard, 0, 2), from_ring(shard, 0, 3)]
     both = join(near)
 
-    mine = split_features(core.reshape(1), inputs, recv)
+    mine = split_features(place, inputs, recv)
     mine = lax.all_to_all(mine, "fsdp", 0, 0, tiled=True)
     both, mine = lax.optimization_barrier((both, mine))
     up = from_ring(both, 1, 1)
     down = from_ring(both, 1, 3)
+    mine = to_vmem(mine)
     a_list = [mine, from_x(mine, 1), from_x(mine, 2), from_x(mine, 3)]
     xb, fourth = fourth_powers(prev_roots.reshape(slots * 2, b, b))
     up, xb, fourth = lax.optimization_barrier((up, xb, fourth))

time: 122 us -> 120 us (0.984)
  local copies, waits for them, and re-layouts: 14.5 us -> 7.91 us
  waiting for transfers between devices: 31.8 us -> 33.9 us
    unnamed x28 -> x20, local copies, waits for them, and re-layouts: 11 us -> 6.5 us
    ppermute x6, waiting for transfers between devices: 19.7 us -> 22.5 us  [from_ring(): return lax.ppermute(v, ('fsdp', 'pre'), pairs)]
  transfers between devices with their start and end apart: 15 -> 15, of which waited for: 9 -> 11; matrix products, arithmetic and copies ran while one was open for 2% -> 0% of each run, Pallas kernels for 10% -> 10%
where the time goes in v5:
time: 120 us; the launch traced here: 119 us
  waiting for transfers between devices  33.9 us (28%)
  Pallas kernels  28.8 us (24%)
  blocking collectives  25.9 us (22%)
  starting transfers between devices  21.7 us (18%)
  local copies, waits for them, and re-layouts  7.91 us (7%)
    all_to_all x1, blocking collectives, body(): pieces = lax.all_to_all(pieces, 'fsdp', 0, 0, tiled=True)  25.9 us
    ppermute x6, waiting for transfers between devices, from_ring(): return lax.ppermute(v, ('fsdp', 'pre'), pairs)  22.5 us
    pallas_call x1, Pallas kernels, newton(): pl.pallas_call(newton_kernel, grid=(slots,), in_specs=[pl.BlockSpec((n_sr...  14.3 us
    ppermute x6, starting transfers between devices, from_ring(): return lax.ppermute(v, ('fsdp', 'pre'), pairs)  9.19 us
    all_to_all x1, starting transfers between devices, body(): mine = lax.all_to_all(mine, 'fsdp', 0, 0, tiled=True)  7.12 us
    unnamed x20, local copies, waits for them, and re-layouts  6.5 us
    pallas_call x1, Pallas kernels, fourth_powers(): pl.pallas_call(fourth_kernel, grid=(n,), in_specs=[spec], out_specs=[spec...  5.65 us
    ppermute x4, waiting for transfers between devices, swap_cores(): lax.ppermute(v, ('fsdp', 'pre'), [(device(*p, c), device(*p, 1 - c)) for...  4.67 us
  transfers between devices with their start and end apart: 15, of which 11 were waited for; matrix products, arithmetic and copies ran while one was open for 0% of the time, Pallas kernels for 10%

profile of v5, /device:TPU:0, one launch (start us, length us, event | category | flops | bytes accessed | tf_op | source)
XLA Modules:
  0.0 119.2 jit_solution(7129530238030892507)
XLA Ops:
  0.7 0.0 copy-start.3
  0.7 1.2 %dynamic-slice_bitcast_fusion.2 = (bf16[1,128,1024]{2,1,0:T(8,128)(2,1)S(1)}, bf16[1,128,1024]{2,1,0:T(8,128)(2,1)S(1)}, bf16[1,128,1024]{2,1,0:T(8,128)(2,1)S(1)}) fusion(bf16[256,1024]{1,0:T(8,128)(2,1)} %param.6, s32[]{:T(128)S(6)} %select_n.29, s32[]{:T(128)S(6)} %select_n.30, bf16[256,1024]{1,0:T(8,128)(2,1)} %a_ref.1), kind=kLoop, calls=%fused_computation.4 | loop fusion | bytes 1572872 | tf_op jit(solution)/shard_map/stack | solution.py:279
  1.9 0.1 pad_maximum_fusion
  2.0 0.1 collective-permute-start
  2.1 1.9 %collective-permute-done.r_ref = bf16[2,128,1024]{2,1,0:T(8,128)(2,1)S(1)} collective-permute-done((bf16[2,128,1024]{2,1,0:T(8,128)(2,1)S(1)}, bf16[2,128,1024]{2,1,0:T(8,128)(2,1)S(1)}, u32[]{:S(2)}, u32[]{:S(2)}) %collective-permute-start) | collective-permute-done | bytes 524320 | tf_op jit(solution)/shard_map/ppermute | solution.py:238
  4.0 0.1 pad_maximum_fusion.1.refs_0_
  4.0 3.2 %collective-permute-start.1 = (bf16[2,128,1024]{2,1,0:T(8,128)(2,1)S(1)}, bf16[2,128,1024]{2,1,0:T(8,128)(2,1)S(1)}, u32[]{:S(2)}, u32[]{:S(2)}) collective-permute-start(bf16[2,128,1024]{2,1,0:T(8,128)(2,1)S(1)} %pad_maximum_fusion.1.refs_0_), channel_id=1, source_target_pairs={{8,0},{33,1},{10,2},{35,3},{12,4},{37,5},{14,6},{39,7},{16,8},{41,... | collective-permute-start | bytes 1572872 | tf_op jit(solution)/shard_map/ppermute | solution.py:255
  7.2 0.6 collective-permute-start.2
  7.8 1.0 collective-permute-start.3
  8.8 0.1 pad_add_fusion.place_ref
  8.9 0.0 copy-done.3
  8.9 1.5 %shard_map.69 = bf16[16,128,128]{2,1,0:T(8,128)(2,1)} custom-call(s32[4]{0:T(128)S(1)} %pad_add_fusion.place_ref, bf16[256,1024]{1,0:T(8,128)(2,1)S(1)} %copy-done.3, bf16[2,128,1024]{2,1,0:T(8,128)(2,1)S(1)} %collective-permute-done.r_ref), custom_call_target="tpu_custom_call" | custom-call | flops 1 | bytes 1 | tf_op jit(solution)/shard_map/pallas_call | solution.py:39
  10.4 7.1 %all-to-all-start = ((bf16[16,128,128]{2,1,0:T(8,128)(2,1)}), bf16[16,128,128]{2,1,0:T(8,128)(2,1)S(1)}, u32[]{:S(2)}, u32[]{:S(2)}) async-start(bf16[16,128,128]{2,1,0:T(8,128)(2,1)} %shard_map.69), calls=%async_computation | async-start | bytes 1048576 | tf_op jit(solution)/shard_map/all_to_all | solution.py:285
  17.5 5.8 %collective-permute-done.1.refs_1_ = bf16[2,128,1024]{2,1,0:T(8,128)(2,1)S(1)} collective-permute-done((bf16[2,128,1024]{2,1,0:T(8,128)(2,1)S(1)}, bf16[2,128,1024]{2,1,0:T(8,128)(2,1)S(1)}, u32[]{:S(2)}, u32[]{:S(2)}) %collective-permute-start.1) | collective-permute-done | bytes 524320 | tf_op jit(solution)/shard_map/ppermute | solution.py:255
  23.3 0.0 copy-start.4
  23.3 0.8 copy-done.4
  24.1 0.0 collective-permute-done.2.refs_2_
  24.1 0.0 copy-start.6
  24.1 0.8 copy-done.6
  24.9 1.2 %collective-permute-done.3.refs_3_ = bf16[2,128,1024]{2,1,0:T(8,128)(2,1)} collective-permute-done((bf16[2,128,1024]{2,1,0:T(8,128)(2,1)S(1)}, bf16[2,128,1024]{2,1,0:T(8,128)(2,1)}, u32[]{:S(2)}, u32[]{:S(2)}) %collective-permute-start.3) | collective-permute-done | bytes 524320 | tf_op jit(solution)/shard_map/ppermute | solution.py:255
  26.2 0.0 copy-start.5
  26.2 1.0 copy-done.5
  27.2 0.0 copy-start.7
  27.2 1.0 copy-done.7
  28.2 1.2 shard_map.68.refs_4_
  29.4 3.3 %all-to-all-done.v_ref = bf16[16,128,128]{2,1,0:T(8,128)(2,1)S(1)} async-done(((bf16[16,128,128]{2,1,0:T(8,128)(2,1)}), bf16[16,128,128]{2,1,0:T(8,128)(2,1)S(1)}, u32[]{:S(2)}, u32[]{:S(2)}) %all-to-all-start) | async-done | bytes 524320 | tf_op jit(solution)/shard_map/all_to_all | solution.py:285
  32.7 1.1 collective-permute-start.7
  33.8 0.9 collective-permute-start.8
  34.7 2.8 %collective-permute-start.4 = (bf16[16,128,128]{2,1,0:T(8,128)(2,1)S(1)}, bf16[16,128,128]{2,1,0:T(8,128)(2,1)S(1)}, u32[]{:S(2)}, u32[]{:S(2)}) collective-permute-start(bf16[16,128,128]{2,1,0:T(8,128)(2,1)S(1)} %shard_map.70.refs_0_), channel_id=1, source_target_pairs={{2,0},{3,1},{4,2},{5,3},{6,4},{7,5},{0,6},{1,7},{10,8},{11,9},{12,... | collective-permute-start | bytes 1572872 | tf_op jit(solution)/shard_map/ppermute | solution.py:244
  37.6 0.8 collective-permute-start.5
  38.4 0.9 collective-permute-start.6
  39.3 0.0 copy-start
  39.3 2.8 %copy-done = f32[3,2,512,512]{3,2,1,0:T(8,128)S(1)} copy-done((f32[3,2,512,512]{3,2,1,0:T(8,128)S(1)}, f32[3,2,512,512]{3,2,1,0:T(8,128)}, u32[]{:S(2)}) %copy-start) | copy-done | bytes 6291480
  42.0 5.7 %shard_map.71 = (bf16[6,512,512]{2,1,0:T(8,128)(2,1)}, bf16[6,512,512]{2,1,0:T(8,128)(2,1)}) custom-call(f32[6,512,512]{2,1,0:T(8,128)S(1)} %bitcast.14), custom_call_target="tpu_custom_call" | custom-call | flops 1 | bytes 1 | tf_op jit(solution)/shard_map/pallas_call | solution.py:60
  47.7 11.0 %collective-permute-done.7.refs_5_ = bf16[8,128,1024]{2,1,0:T(8,128)(2,1)S(1)} collective-permute-done((bf16[8,128,1024]{2,1,0:T(8,128)(2,1)S(1)}, bf16[8,128,1024]{2,1,0:T(8,128)(2,1)S(1)}, u32[]{:S(2)}, u32[]{:S(2)}) %collective-permute-start.7) | collective-permute-done | bytes 2097184 | tf_op jit(solution)/shard_map/ppermute | solution.py:255
  58.7 0.1 slice.10
  58.8 2.4 %collective-permute-start.10 = (bf16[4,128,1024]{2,1,0:T(8,128)(2,1)S(1)}, bf16[4,128,1024]{2,1,0:T(8,128)(2,1)S(1)}, u32[]{:S(2)}, u32[]{:S(2)}) collective-permute-start(bf16[4,128,1024]{2,1,0:T(8,128)(2,1)S(1)} %slice.10), channel_id=1, source_target_pairs={{32,0},{9,1},{34,2},{11,3},{36,4},{13,5},{38,6},{15,7},{40,8},{17,... | collective-permute-start | bytes 3145736 | tf_op jit(solution)/shard_map/ppermute | solution.py:255
  61.2 0.0 collective-permute-done.8.refs_6_
  61.2 0.1 slice.13
  61.3 0.0 copy-start.8
  61.3 0.0 copy-start.9
  61.3 0.1 collective-permute-start.11
  61.4 0.0 collective-permute-done.4.refs_1_
  61.4 0.0 collective-permute-done.5.refs_2_
  61.4 0.3 collective-permute-done.6.refs_3_
  61.7 4.0 %shard_map.72 = (bf16[512,512]{1,0:T(8,128)(2,1)S(1)}, bf16[512,512]{1,0:T(8,128)(2,1)S(1)}, f32[512,1024]{1,0:T(8,128)S(1)}, bf16[512,512]{1,0:T(8,128)(2,1)S(1)}) custom-call(s32[4]{0:T(128)S(1)} %pad_add_fusion.place_ref, bf16[16,128,128]{2,1,0:T(8,128)(2,1)S(1)} %shard_map.70.refs_0_, bf16[16,128,128]{2,1,0:T(8,128)(2,1)S(1)} %collective-permute-done.4.refs_1_, ...), custom_call_target="tpu_custom_call" | custom-call | flops 3221225472 | bytes 12582912 | tf_op jit(solution)/shard_map/pallas_call | solution.py:147
  65.7 0.1 collective-permute-start.12
  65.8 0.5 collective-permute-start.13
  66.3 0.1 collective-permute-start.9
  66.4 1.3 %collective-permute-done.12.share_0 = bf16[512,512]{1,0:T(8,128)(2,1)S(1)} collective-permute-done((bf16[512,512]{1,0:T(8,128)(2,1)S(1)}, bf16[512,512]{1,0:T(8,128)(2,1)S(1)}, u32[]{:S(2)}, u32[]{:S(2)}) %collective-permute-start.12) | collective-permute-done | bytes 524320 | tf_op jit(solution)/shard_map/ppermute | solution.py:238
  67.7 0.7 collective-permute-done.13.share_1
  68.5 0.7 collective-permute-done.9.cross_ref
  69.2 4.5 %collective-permute-done.10.own_ref = bf16[4,128,1024]{2,1,0:T(8,128)(2,1)S(1)} collective-permute-done((bf16[4,128,1024]{2,1,0:T(8,128)(2,1)S(1)}, bf16[4,128,1024]{2,1,0:T(8,128)(2,1)S(1)}, u32[]{:S(2)}, u32[]{:S(2)}) %collective-permute-start.10) | collective-permute-done | bytes 1048608 | tf_op jit(solution)/shard_map/ppermute | solution.py:255
  73.7 3.1 %collective-permute-done.11.far_ref = bf16[4,128,1024]{2,1,0:T(8,128)(2,1)S(1)} collective-permute-done((bf16[4,128,1024]{2,1,0:T(8,128)(2,1)S(1)}, bf16[4,128,1024]{2,1,0:T(8,128)(2,1)S(1)}, u32[]{:S(2)}, u32[]{:S(2)}) %collective-permute-start.11) | collective-permute-done | bytes 1048608 | tf_op jit(solution)/shard_map/ppermute | solution.py:264
  76.8 0.0 copy-done.8
  76.8 0.0 copy-done.9
  76.8 0.0 copy-start.2
  76.8 2.1 %shard_map.73 = bf16[48,32,512]{2,1,0:T(8,128)(2,1)S(1)} custom-call(s32[4]{0:T(128)S(1)} %pad_add_fusion.place_ref, s32[16,16]{1,0:T(8,128)S(1)} %copy-done.8, s32[16,16]{1,0:T(8,128)S(1)} %copy-done.9, bf16[512,512]{1,0:T(8,128)(2,1)S(1)} %get-tuple-element.18.lhs_ref, bf16[512,512]{1,0:T(8,128)(2,1)S(1)} %collective-permute-done.9.cross_ref, ...), custom_call_target="tpu_custom_call" | custom-call | flops 1 | bytes 1 | tf_op jit(solution)/shard_map/pallas_call | solution.py:180
  78.9 0.0 copy-start.1
  79.0 25.9 %all_to_all.10 = bf16[48,32,512]{2,1,0:T(8,128)(2,1)S(1)} all-to-all(bf16[48,32,512]{2,1,0:T(8,128)(2,1)S(1)} %shard_map.73), channel_id=1, replica_groups=mesh['fsdp'=16,'pre'=8] {'fsdp'}, dimensions={0} | all-to-all | bytes 3145728 | tf_op jit(solution)/shard_map/all_to_all | solution.py:301
  104.9 0.0 copy-done.2
  104.9 0.0 copy-done.1
  104.9 14.3 %shard_map.74 = (bf16[3,512,512]{2,1,0:T(8,128)(2,1)}, f32[3,2,512,512]{3,2,1,0:T(8,128)}) custom-call(bf16[16,3,32,512]{3,2,1,0:T(8,128)(2,1)S(1)} %bitcast.15, bf16[3,2,512,512]{3,2,1,0:T(8,128)(2,1)S(1)} %bitcast.16, bf16[3,2,512,512]{3,2,1,0:T(8,128)(2,1)S(1)} %bitcast.17), custom_call_target="tpu_custom_call" | custom-call | flops 1 | bytes 1 | tf_op jit(solution)/shard_map/pallas_call | solution.py:215
  (2 shorter events, 0.1 us)
Async XLA Ops:
  0.7 8.2 %copy-start.3 = (bf16[256,1024]{1,0:T(8,128)(2,1)S(1)}, bf16[256,1024]{1,0:T(8,128)(2,1)}, u32[]{:S(2)}) copy-start(bf16[256,1024]{1,0:T(8,128)(2,1)} %a_ref.1) | copy-start | bytes 1572868
  2.0 2.0 %collective-permute-start = (bf16[2,128,1024]{2,1,0:T(8,128)(2,1)S(1)}, bf16[2,128,1024]{2,1,0:T(8,128)(2,1)S(1)}, u32[]{:S(2)}, u32[]{:S(2)}) collective-permute-start(bf16[2,128,1024]{2,1,0:T(8,128)(2,1)S(1)} %pad_maximum_fusion), channel_id=1, source_target_pairs={{0,1},{1,0},{2,3},{3,2},{4,5},{5,4},{6,7},{7,6},{8,9},{9,8},{10,11... | collective-permute-start | bytes 1572872 | tf_op jit(solution)/shard_map/ppermute | solution.py:238
  4.0 19.3 %collective-permute-start.1 = (bf16[2,128,1024]{2,1,0:T(8,128)(2,1)S(1)}, bf16[2,128,1024]{2,1,0:T(8,128)(2,1)S(1)}, u32[]{:S(2)}, u32[]{:S(2)}) collective-permute-start(bf16[2,128,1024]{2,1,0:T(8,128)(2,1)S(1)} %pad_maximum_fusion.1.refs_0_), channel_id=1, source_target_pairs={{8,0},{33,1},{10,2},{35,3},{12,4},{37,5},{14,6},{39,7},{16,8},{41,... | collective-permute-start | bytes 1572872 | tf_op jit(solution)/shard_map/ppermute | solution.py:255
  7.2 16.9 %collective-permute-start.2 = (bf16[2,128,1024]{2,1,0:T(8,128)(2,1)S(1)}, bf16[2,128,1024]{2,1,0:T(8,128)(2,1)S(1)}, u32[]{:S(2)}, u32[]{:S(2)}) collective-permute-start(bf16[2,128,1024]{2,1,0:T(8,128)(2,1)S(1)} %pad_maximum_fusion.1.refs_0_), channel_id=1, source_target_pairs={{16,0},{65,1},{18,2},{67,3},{20,4},{69,5},{22,6},{71,7},{24,8},{73... | collective-permute-start | bytes 1572872 | tf_op jit(solution)/shard_map/ppermute | solution.py:255
  7.8 18.3 %collective-permute-start.3 = (bf16[2,128,1024]{2,1,0:T(8,128)(2,1)S(1)}, bf16[2,128,1024]{2,1,0:T(8,128)(2,1)}, u32[]{:S(2)}, u32[]{:S(2)}) collective-permute-start(bf16[2,128,1024]{2,1,0:T(8,128)(2,1)S(1)} %pad_maximum_fusion.1.refs_0_), channel_id=1, source_target_pairs={{24,0},{97,1},{26,2},{99,3},{28,4},{101,5},{30,6},{103,7},{0,8},{1... | collective-permute-start | bytes 1572872 | tf_op jit(solution)/shard_map/ppermute | solution.py:255
  10.4 22.3 %all-to-all-start = ((bf16[16,128,128]{2,1,0:T(8,128)(2,1)}), bf16[16,128,128]{2,1,0:T(8,128)(2,1)S(1)}, u32[]{:S(2)}, u32[]{:S(2)}) async-start(bf16[16,128,128]{2,1,0:T(8,128)(2,1)} %shard_map.69), calls=%async_computation | async-start | bytes 1048576 | tf_op jit(solution)/shard_map/all_to_all | solution.py:285
  23.3 0.8 copy-start.4
  24.1 0.8 copy-start.6
  26.2 1.0 copy-start.5
  27.2 1.0 copy-start.7
  32.7 26.0 %collective-permute-start.7 = (bf16[8,128,1024]{2,1,0:T(8,128)(2,1)S(1)}, bf16[8,128,1024]{2,1,0:T(8,128)(2,1)S(1)}, u32[]{:S(2)}, u32[]{:S(2)}) collective-permute-start(bf16[8,128,1024]{2,1,0:T(8,128)(2,1)S(1)} %shard_map.68.refs_4_), channel_id=1, source_target_pairs={{32,0},{9,1},{34,2},{11,3},{36,4},{13,5},{38,6},{15,7},{40,8},{17,... | collective-permute-start | bytes 6291464 | tf_op jit(solution)/shard_map/ppermute | solution.py:255
  33.8 27.4 %collective-permute-start.8 = (bf16[8,128,1024]{2,1,0:T(8,128)(2,1)S(1)}, bf16[8,128,1024]{2,1,0:T(8,128)(2,1)S(1)}, u32[]{:S(2)}, u32[]{:S(2)}) collective-permute-start(bf16[8,128,1024]{2,1,0:T(8,128)(2,1)S(1)} %shard_map.68.refs_4_), channel_id=1, source_target_pairs={{96,0},{25,1},{98,2},{27,3},{100,4},{29,5},{102,6},{31,7},{104,8},... | collective-permute-start | bytes 6291464 | tf_op jit(solution)/shard_map/ppermute | solution.py:255
  34.7 26.7 %collective-permute-start.4 = (bf16[16,128,128]{2,1,0:T(8,128)(2,1)S(1)}, bf16[16,128,128]{2,1,0:T(8,128)(2,1)S(1)}, u32[]{:S(2)}, u32[]{:S(2)}) collective-permute-start(bf16[16,128,128]{2,1,0:T(8,128)(2,1)S(1)} %shard_map.70.refs_0_), channel_id=1, source_target_pairs={{2,0},{3,1},{4,2},{5,3},{6,4},{7,5},{0,6},{1,7},{10,8},{11,9},{12,... | collective-permute-start | bytes 1572872 | tf_op jit(solution)/shard_map/ppermute | solution.py:244
  37.6 23.8 %collective-permute-start.5 = (bf16[16,128,128]{2,1,0:T(8,128)(2,1)S(1)}, bf16[16,128,128]{2,1,0:T(8,128)(2,1)S(1)}, u32[]{:S(2)}, u32[]{:S(2)}) collective-permute-start(bf16[16,128,128]{2,1,0:T(8,128)(2,1)S(1)} %shard_map.70.refs_0_), channel_id=1, source_target_pairs={{4,0},{5,1},{6,2},{7,3},{0,4},{1,5},{2,6},{3,7},{12,8},{13,9},{14,... | collective-permute-start | bytes 1572872 | tf_op jit(solution)/shard_map/ppermute | solution.py:244
  38.4 23.4 %collective-permute-start.6 = (bf16[16,128,128]{2,1,0:T(8,128)(2,1)S(1)}, bf16[16,128,128]{2,1,0:T(8,128)(2,1)S(1)}, u32[]{:S(2)}, u32[]{:S(2)}) collective-permute-start(bf16[16,128,128]{2,1,0:T(8,128)(2,1)S(1)} %shard_map.70.refs_0_), channel_id=1, source_target_pairs={{6,0},{7,1},{0,2},{1,3},{2,4},{3,5},{4,6},{5,7},{14,8},{15,9},{8,1... | collective-permute-start | bytes 1572872 | tf_op jit(solution)/shard_map/ppermute | solution.py:244
  39.3 2.8 %copy-start = (f32[3,2,512,512]{3,2,1,0:T(8,128)S(1)}, f32[3,2,512,512]{3,2,1,0:T(8,128)}, u32[]{:S(2)}) copy-start(f32[3,2,512,512]{3,2,1,0:T(8,128)} %param.9) | copy-start | bytes 18874372
  58.8 14.9 %collective-permute-start.10 = (bf16[4,128,1024]{2,1,0:T(8,128)(2,1)S(1)}, bf16[4,128,1024]{2,1,0:T(8,128)(2,1)S(1)}, u32[]{:S(2)}, u32[]{:S(2)}) collective-permute-start(bf16[4,128,1024]{2,1,0:T(8,128)(2,1)S(1)} %slice.10), channel_id=1, source_target_pairs={{32,0},{9,1},{34,2},{11,3},{36,4},{13,5},{38,6},{15,7},{40,8},{17,... | collective-permute-start | bytes 3145736 | tf_op jit(solution)/shard_map/ppermute | solution.py:255
  61.3 15.5 %copy-start.8 = (s32[16,16]{1,0:T(8,128)S(1)}, s32[16,16]{1,0:T(8,128)}, u32[]{:S(2)}) copy-start(s32[16,16]{1,0:T(8,128)} %owner_ref.1) | copy-start | bytes 3076
  61.3 15.5 %copy-start.9 = (s32[16,16]{1,0:T(8,128)S(1)}, s32[16,16]{1,0:T(8,128)}, u32[]{:S(2)}) copy-start(s32[16,16]{1,0:T(8,128)} %offs_ref.1) | copy-start | bytes 3076
  61.3 15.5 %collective-permute-start.11 = (bf16[4,128,1024]{2,1,0:T(8,128)(2,1)S(1)}, bf16[4,128,1024]{2,1,0:T(8,128)(2,1)S(1)}, u32[]{:S(2)}, u32[]{:S(2)}) collective-permute-start(bf16[4,128,1024]{2,1,0:T(8,128)(2,1)S(1)} %slice.13), channel_id=1, source_target_pairs={{25,0},{96,1},{27,2},{98,3},{29,4},{100,5},{31,6},{102,7},{1,8},{1... | collective-permute-start | bytes 3145736 | tf_op jit(solution)/shard_map/ppermute | solution.py:264
  65.7 2.0 %collective-permute-start.12 = (bf16[512,512]{1,0:T(8,128)(2,1)S(1)}, bf16[512,512]{1,0:T(8,128)(2,1)S(1)}, u32[]{:S(2)}, u32[]{:S(2)}) collective-permute-start(bf16[512,512]{1,0:T(8,128)(2,1)S(1)} %get-tuple-element.20), channel_id=1, source_target_pairs={{0,1},{1,0},{2,3},{3,2},{4,5},{5,4},{6,7},{7,6},{8,9},{9,8},{10,11... | collective-permute-start | bytes 1572872 | tf_op jit(solution)/shard_map/ppermute | solution.py:238
  65.8 2.6 %collective-permute-start.13 = (bf16[512,512]{1,0:T(8,128)(2,1)S(1)}, bf16[512,512]{1,0:T(8,128)(2,1)S(1)}, u32[]{:S(2)}, u32[]{:S(2)}) collective-permute-start(bf16[512,512]{1,0:T(8,128)(2,1)S(1)} %get-tuple-element.21), channel_id=1, source_target_pairs={{0,1},{1,0},{2,3},{3,2},{4,5},{5,4},{6,7},{7,6},{8,9},{9,8},{10,11... | collective-permute-start | bytes 1572872 | tf_op jit(solution)/shard_map/ppermute | solution.py:238
  66.3 2.9 %collective-permute-start.9 = (bf16[512,512]{1,0:T(8,128)(2,1)S(1)}, bf16[512,512]{1,0:T(8,128)(2,1)S(1)}, u32[]{:S(2)}, u32[]{:S(2)}) collective-permute-start(bf16[512,512]{1,0:T(8,128)(2,1)S(1)} %get-tuple-element.18.lhs_ref), channel_id=1, source_target_pairs={{0,1},{1,0},{2,3},{3,2},{4,5},{5,4},{6,7},{7,6},{8,9},{9,8},{10,11... | collective-permute-start | bytes 1572872 | tf_op jit(solution)/shard_map/ppermute | solution.py:238
  76.8 28.1 %copy-start.2 = (bf16[6,512,512]{2,1,0:T(8,128)(2,1)S(1)}, bf16[6,512,512]{2,1,0:T(8,128)(2,1)}, u32[]{:S(2)}) copy-start(bf16[6,512,512]{2,1,0:T(8,128)(2,1)} %get-tuple-element.23) | copy-start | bytes 9437188
  78.9 25.9 %copy-start.1 = (bf16[6,512,512]{2,1,0:T(8,128)(2,1)S(1)}, bf16[6,512,512]{2,1,0:T(8,128)(2,1)}, u32[]{:S(2)}) copy-start(bf16[6,512,512]{2,1,0:T(8,128)(2,1)} %get-tuple-element.22) | copy-start | bytes 9437188

commit v6 on v5

--- a/solution.py
+++ b/solution.py
@@ -85,10 +85,9 @@
 
 
 def join_kernel(*refs):
-    parts, o_ref = refs[:-1], refs[-1]
-    for o in range(2):
-        for i, v in enumerate(parts):
-            o_ref[o * len(parts) + i] = v[o]
+    for o, o_ref in enumerate(refs[-2:]):
+        for i, v in enumerate(refs[:-2]):
+            o_ref[i] = v[o]
 
 
 def join(parts):
@@ -97,8 +96,8 @@
     return pl.pallas_call(
         join_kernel,
         in_specs=[vmem] * len(parts),
-        out_specs=vmem,
-        out_shape=jax.ShapeDtypeStruct((n * len(parts), rows, cols), BF),
+        out_specs=[vmem] * n,
+        out_shape=[jax.ShapeDtypeStruct((len(parts), rows, cols), BF)] * n,
         compiler_params=params(),
         cost_estimate=SHORT,
     )(*parts)
@@ -125,13 +124,13 @@
 
 
 def first_kernel(place_ref, *refs):
-    a_refs, b_refs, shares, (acc_ref, last_ref) = refs[:4], refs[4:7], refs[7:9], refs[9:]
+    a_refs, b_refs, shares, (acc_ref, last_ref) = refs[:4], refs[4:10], refs[10:12], refs[12:]
     lhs = jnp.concatenate([left_operand(place_ref, a_refs, j) for j in (0, 1, 3)], axis=1)
     block = shares[0].shape[1]
     for o in (1, 0):
         for c in range(2):
             at = slice(c * block, (c + 1) * block)
-            total = product(lhs, *[v[4 * o : 4 * o + 4, :, at] for v in b_refs])
+            total = product(lhs, *[v[:, :, at] for v in b_refs[o::2]])
             if o:
                 shares[c][...] = total.astype(BF)
             else:
@@ -146,7 +145,7 @@
     vmem = pl.BlockSpec(memory_space=pltpu.VMEM)
     return pl.pallas_call(
         first_kernel,
-        in_specs=[pl.BlockSpec(memory_space=pltpu.SMEM)] + [vmem] * 7,
+        in_specs=[pl.BlockSpec(memory_space=pltpu.SMEM)] + [vmem] * 10,
         out_specs=[vmem] * 4,
         out_shape=[jax.ShapeDtypeStruct(full, BF)] * 2
         + [jax.ShapeDtypeStruct((4 * rows, cols), F32), jax.ShapeDtypeStruct(full, BF)],
@@ -279,22 +278,25 @@
     shard = jnp.stack([rows_of(grads_out, core), recv[1]])
 
     near = [shard, from_ring(shard, 0, 1), from_ring(shard, 0, 2), from_ring(shard, 0, 3)]
-    both = join(near)
+    own, other = join(near)
 
     mine = split_features(place, inputs, recv)
     mine = lax.all_to_all(mine, "fsdp", 0, 0, tiled=True)
-    both, mine = lax.optimization_barrier((both, mine))
-    up = from_ring(both, 1, 1)
-    down = from_ring(both, 1, 3)
+    own, other, mine = lax.optimization_barrier((own, other, mine))
     mine = to_vmem(mine)
-    a_list = [mine, from_x(mine, 1), from_x(mine, 2), from_x(mine, 3)]
+    own_1, other_3 = from_ring(own, 1, 1), from_ring(other, 1, 3)
+    next_x, last_x = from_x(mine, 1), from_x(mine, 3)
+    far_x = from_x(mine, 2)
+    own_t, other_t, next_x, last_x = lax.optimization_barrier((own, other, next_x, last_x))
+    other_1, own_3 = from_ring(other_t, 1, 1), from_ring(own_t, 1, 3)
     xb, fourth = fourth_powers(prev_roots.reshape(slots * 2, b, b))
-    up, xb, fourth = lax.optimization_barrier((up, xb, fourth))
+    other_1, xb, fourth = lax.optimization_barrier((other_1, xb, fourth))
     xb, fourth = (v.reshape(prev_roots.shape) for v in (xb, fourth))
-    own_2 = from_ring(up[:4], 1, 1)
-    far_2 = from_ring_across(down[4:], 3)
-
-    share_0, share_1, acc, lhs = first_chunks(place, a_list, [both, up, down])
+    own_2 = from_ring(own_1, 1, 1)
+    far_2 = from_ring_across(other_3, 3)
+
+    chunks = [own, other, own_1, other_1, own_3, other_3]
+    share_0, share_1, acc, lhs = first_chunks(place, [mine, next_x, far_x, last_x], chunks)
     pieces = last_chunk(
         place, owner, offsets, lhs, swap_cores(lhs), own_2, far_2, acc, swap_cores(share_0), swap_cores(share_1)
     )

time: 120 us -> 119 us (level)
  blocking collectives: 25.9 us -> 29.2 us
  local copies, waits for them, and re-layouts: 7.91 us -> 5.97 us
    ppermute x3, waiting for transfers between devices: 0.32 us -> 8.55 us  [from_x(): lax.ppermute(v, ('fsdp', 'pre'), [(device(z, y, x + d, c), device(z, y, x...]
    ppermute x6 -> x8, waiting for transfers between devices: 22.5 us -> 18.7 us  [from_ring(): return lax.ppermute(v, ('fsdp', 'pre'), pairs)]
    all_to_all x1, blocking collectives: 25.9 us -> 29.2 us  [body(): pieces = lax.all_to_all(pieces, 'fsdp', 0, 0, tiled=True)]
    ppermute x1, waiting for transfers between devices: 3.13 us -> 0.01 us  [from_ring_across(): return lax.ppermute(v, ('fsdp', 'pre'), pairs)]
    ppermute x4, waiting for transfers between devices: 4.67 us -> 1.87 us  [swap_cores(): lax.ppermute(v, ('fsdp', 'pre'), [(device(*p, c), device(*p, 1 - c)) for...]
    unnamed x20, local copies, waits for them, and re-layouts: 6.5 us -> 4.74 us
    ppermute x3, starting transfers between devices: 4.51 us -> 2.83 us  [from_x(): lax.ppermute(v, ('fsdp', 'pre'), [(device(z, y, x + d, c), device(z, y, x...]
    all_to_all x1, waiting for transfers between devices: 3.26 us -> 4.55 us  [body(): mine = lax.all_to_all(mine, 'fsdp', 0, 0, tiled=True)]
  transfers between devices with their start and end apart: 15 -> 17, of which waited for: 11 -> 10; matrix products, arithmetic and copies ran while one was open for 0% -> 0% of each run, Pallas kernels for 10% -> 9%
where the time goes in v6:
time: 119 us
  waiting for transfers between devices  33.6 us (28%)
  blocking collectives  29.2 us (25%)
  Pallas kernels  27.7 us (23%)
  starting transfers between devices  21.1 us (18%)
  local copies, waits for them, and re-layouts  5.97 us (5%)
    all_to_all x1, blocking collectives, body(): pieces = lax.all_to_all(pieces, 'fsdp', 0, 0, tiled=True)  29.2 us
    ppermute x8, waiting for transfers between devices, from_ring(): return lax.ppermute(v, ('fsdp', 'pre'), pairs)  18.7 us
    pallas_call x1, Pallas kernels, newton(): pl.pallas_call(newton_kernel, grid=(slots,), in_specs=[pl.BlockSpec((n_sr...  14.3 us
    ppermute x8, starting transfers between devices, from_ring(): return lax.ppermute(v, ('fsdp', 'pre'), pairs)  10.4 us
    ppermute x3, waiting for transfers between devices, from_x(): lax.ppermute(v, ('fsdp', 'pre'), [(device(z, y, x + d, c), device(z, y, x...  8.55 us
    all_to_all x1, starting transfers between devices, body(): mine = lax.all_to_all(mine, 'fsdp', 0, 0, tiled=True)  7.12 us
    pallas_call x1, Pallas kernels, fourth_powers(): pl.pallas_call(fourth_kernel, grid=(n,), in_specs=[spec], out_specs=[spec...  5.63 us
    unnamed x20, local copies, waits for them, and re-layouts  4.74 us
  transfers between devices with their start and end apart: 17, of which 10 were waited for; matrix products, arithmetic and copies ran while one was open for 0% of the time, Pallas kernels for 9%

profile of v6, /device:TPU:0, one launch (start us, length us, event | category | flops | bytes accessed | tf_op | source)
XLA Modules:
  0.0 118.8 jit_solution(16947008947186657594)
XLA Ops:
  0.6 0.0 copy-start.3
  0.7 1.2 %dynamic-slice_bitcast_fusion.2 = (bf16[1,128,1024]{2,1,0:T(8,128)(2,1)S(1)}, bf16[1,128,1024]{2,1,0:T(8,128)(2,1)S(1)}, bf16[1,128,1024]{2,1,0:T(8,128)(2,1)S(1)}) fusion(bf16[256,1024]{1,0:T(8,128)(2,1)} %param.6, s32[]{:T(128)S(6)} %select_n.29, s32[]{:T(128)S(6)} %select_n.30, bf16[256,1024]{1,0:T(8,128)(2,1)} %a_ref.1), kind=kLoop, calls=%fused_computation.4 | loop fusion | bytes 1572872 | tf_op jit(solution)/shard_map/stack | solution.py:278
  1.9 0.1 pad_maximum_fusion
  1.9 0.1 collective-permute-start
  2.1 1.9 %collective-permute-done.r_ref = bf16[2,128,1024]{2,1,0:T(8,128)(2,1)S(1)} collective-permute-done((bf16[2,128,1024]{2,1,0:T(8,128)(2,1)S(1)}, bf16[2,128,1024]{2,1,0:T(8,128)(2,1)S(1)}, u32[]{:S(2)}, u32[]{:S(2)}) %collective-permute-start) | collective-permute-done | bytes 524320 | tf_op jit(solution)/shard_map/ppermute | solution.py:237
  4.0 0.1 pad_maximum_fusion.1.refs_0_
  4.0 3.2 %collective-permute-start.1 = (bf16[2,128,1024]{2,1,0:T(8,128)(2,1)S(1)}, bf16[2,128,1024]{2,1,0:T(8,128)(2,1)S(1)}, u32[]{:S(2)}, u32[]{:S(2)}) collective-permute-start(bf16[2,128,1024]{2,1,0:T(8,128)(2,1)S(1)} %pad_maximum_fusion.1.refs_0_), channel_id=1, source_target_pairs={{8,0},{33,1},{10,2},{35,3},{12,4},{37,5},{14,6},{39,7},{16,8},{41,... | collective-permute-start | bytes 1572872 | tf_op jit(solution)/shard_map/ppermute | solution.py:254
  7.2 0.6 collective-permute-start.2
  7.8 1.0 collective-permute-start.3
  8.8 0.1 pad_add_fusion.place_ref
  8.9 0.0 copy-done.3
  8.9 1.5 %shard_map.69 = bf16[16,128,128]{2,1,0:T(8,128)(2,1)} custom-call(s32[4]{0:T(128)S(1)} %pad_add_fusion.place_ref, bf16[256,1024]{1,0:T(8,128)(2,1)S(1)} %copy-done.3, bf16[2,128,1024]{2,1,0:T(8,128)(2,1)S(1)} %collective-permute-done.r_ref), custom_call_target="tpu_custom_call" | custom-call | flops 1 | bytes 1 | tf_op jit(solution)/shard_map/pallas_call | solution.py:39
  10.4 7.1 %all-to-all-start = ((bf16[16,128,128]{2,1,0:T(8,128)(2,1)}), bf16[16,128,128]{2,1,0:T(8,128)(2,1)S(1)}, u32[]{:S(2)}, u32[]{:S(2)}) async-start(bf16[16,128,128]{2,1,0:T(8,128)(2,1)} %shard_map.69), calls=%async_computation | async-start | bytes 1048576 | tf_op jit(solution)/shard_map/all_to_all | solution.py:284
  17.5 5.8 %collective-permute-done.1.refs_1_ = bf16[2,128,1024]{2,1,0:T(8,128)(2,1)S(1)} collective-permute-done((bf16[2,128,1024]{2,1,0:T(8,128)(2,1)S(1)}, bf16[2,128,1024]{2,1,0:T(8,128)(2,1)S(1)}, u32[]{:S(2)}, u32[]{:S(2)}) %collective-permute-start.1) | collective-permute-done | bytes 524320 | tf_op jit(solution)/shard_map/ppermute | solution.py:254
  23.3 0.0 collective-permute-done.2.refs_2_
  23.3 2.7 %collective-permute-done.3.refs_3_ = bf16[2,128,1024]{2,1,0:T(8,128)(2,1)S(1)} collective-permute-done((bf16[2,128,1024]{2,1,0:T(8,128)(2,1)S(1)}, bf16[2,128,1024]{2,1,0:T(8,128)(2,1)S(1)}, u32[]{:S(2)}, u32[]{:S(2)}) %collective-permute-start.3) | collective-permute-done | bytes 524320 | tf_op jit(solution)/shard_map/ppermute | solution.py:254
  26.0 0.1 shard_map.68
  26.2 0.0 copy-start.6
  26.2 1.0 copy-done.6
  27.1 0.0 copy-start.8
  27.1 1.0 copy-done.8
  28.1 4.6 %all-to-all-done.v_ref = bf16[16,128,128]{2,1,0:T(8,128)(2,1)S(1)} async-done(((bf16[16,128,128]{2,1,0:T(8,128)(2,1)}), bf16[16,128,128]{2,1,0:T(8,128)(2,1)S(1)}, u32[]{:S(2)}, u32[]{:S(2)}) %all-to-all-start) | async-done | bytes 524320 | tf_op jit(solution)/shard_map/all_to_all | solution.py:284
  32.7 2.8 %collective-permute-start.4 = (bf16[16,128,128]{2,1,0:T(8,128)(2,1)S(1)}, bf16[16,128,128]{2,1,0:T(8,128)(2,1)S(1)}, u32[]{:S(2)}, u32[]{:S(2)}) collective-permute-start(bf16[16,128,128]{2,1,0:T(8,128)(2,1)S(1)} %shard_map.70.refs_0_), channel_id=1, source_target_pairs={{2,0},{3,1},{4,2},{5,3},{6,4},{7,5},{0,6},{1,7},{10,8},{11,9},{12,... | collective-permute-start | bytes 1572872 | tf_op jit(solution)/shard_map/ppermute | solution.py:243
  35.5 0.0 collective-permute-start.5
  35.5 0.4 collective-permute-start.7
  35.9 1.6 %collective-permute-start.10 = (bf16[4,128,1024]{2,1,0:T(8,128)(2,1)}, bf16[4,128,1024]{2,1,0:T(8,128)(2,1)S(1)}, u32[]{:S(2)}, u32[]{:S(2)}) collective-permute-start(bf16[4,128,1024]{2,1,0:T(8,128)(2,1)} %copy-done.8), channel_id=1, source_target_pairs={{96,0},{25,1},{98,2},{27,3},{100,4},{29,5},{102,6},{31,7},{104,8},... | collective-permute-start | bytes 3145736 | tf_op jit(solution)/shard_map/ppermute | solution.py:254
  37.6 5.1 %collective-permute-done.4.refs_1_ = bf16[16,128,128]{2,1,0:T(8,128)(2,1)S(1)} collective-permute-done((bf16[16,128,128]{2,1,0:T(8,128)(2,1)S(1)}, bf16[16,128,128]{2,1,0:T(8,128)(2,1)S(1)}, u32[]{:S(2)}, u32[]{:S(2)}) %collective-permute-start.4) | collective-permute-done | bytes 524320 | tf_op jit(solution)/shard_map/ppermute | solution.py:243
  42.7 3.4 %collective-permute-done.5.refs_3_ = bf16[16,128,128]{2,1,0:T(8,128)(2,1)S(1)} collective-permute-done((bf16[16,128,128]{2,1,0:T(8,128)(2,1)S(1)}, bf16[16,128,128]{2,1,0:T(8,128)(2,1)S(1)}, u32[]{:S(2)}, u32[]{:S(2)}) %collective-permute-start.5) | collective-permute-done | bytes 524320 | tf_op jit(solution)/shard_map/ppermute | solution.py:243
  46.1 1.1 collective-permute-start.8
  47.3 0.9 collective-permute-start.9
  48.1 0.0 collective-permute-start.6
  48.1 2.4 %collective-permute-done.7.refs_6_ = bf16[4,128,1024]{2,1,0:T(8,128)(2,1)S(1)} collective-permute-done((bf16[4,128,1024]{2,1,0:T(8,128)(2,1)}, bf16[4,128,1024]{2,1,0:T(8,128)(2,1)S(1)}, u32[]{:S(2)}, u32[]{:S(2)}) %collective-permute-start.7) | collective-permute-done | bytes 1048608 | tf_op jit(solution)/shard_map/ppermute | solution.py:254
  50.5 1.6 %collective-permute-start.12 = (bf16[4,128,1024]{2,1,0:T(8,128)(2,1)S(1)}, bf16[4,128,1024]{2,1,0:T(8,128)(2,1)S(1)}, u32[]{:S(2)}, u32[]{:S(2)}) collective-permute-start(bf16[4,128,1024]{2,1,0:T(8,128)(2,1)S(1)} %collective-permute-done.7.refs_6_), channel_id=1, source_target_pairs={{32,0},{9,1},{34,2},{11,3},{36,4},{13,5},{38,6},{15,7},{40,8},{17,... | collective-permute-start | bytes 3145736 | tf_op jit(solution)/shard_map/ppermute | solution.py:254
  52.2 0.0 collective-permute-done.10.refs_9_
  52.2 0.0 collective-permute-start.13
  52.2 2.8 %copy-done = f32[3,2,512,512]{3,2,1,0:T(8,128)S(1)} copy-done((f32[3,2,512,512]{3,2,1,0:T(8,128)S(1)}, f32[3,2,512,512]{3,2,1,0:T(8,128)}, u32[]{:S(2)}) %copy-start) | copy-done | bytes 6291480
  54.9 0.0 copy-start.7
  55.0 0.0 copy-start.9
  55.0 5.6 %shard_map.71 = (bf16[6,512,512]{2,1,0:T(8,128)(2,1)}, bf16[6,512,512]{2,1,0:T(8,128)(2,1)}) custom-call(f32[6,512,512]{2,1,0:T(8,128)S(1)} %bitcast.14), custom_call_target="tpu_custom_call" | custom-call | flops 1 | bytes 1 | tf_op jit(solution)/shard_map/pallas_call | solution.py:60
  60.6 1.2 %collective-permute-done.8.refs_7_ = bf16[4,128,1024]{2,1,0:T(8,128)(2,1)S(1)} collective-permute-done((bf16[4,128,1024]{2,1,0:T(8,128)(2,1)}, bf16[4,128,1024]{2,1,0:T(8,128)(2,1)S(1)}, u32[]{:S(2)}, u32[]{:S(2)}) %collective-permute-start.8) | collective-permute-done | bytes 1048608 | tf_op jit(solution)/shard_map/ppermute | solution.py:254
  61.8 0.0 copy-start.4
  61.8 0.0 copy-start.5
  61.8 0.0 collective-permute-done.6.refs_2_
  61.8 1.7 %collective-permute-done.9.refs_8_ = bf16[4,128,1024]{2,1,0:T(8,128)(2,1)S(1)} collective-permute-done((bf16[4,128,1024]{2,1,0:T(8,128)(2,1)}, bf16[4,128,1024]{2,1,0:T(8,128)(2,1)S(1)}, u32[]{:S(2)}, u32[]{:S(2)}) %collective-permute-start.9) | collective-permute-done | bytes 1048608 | tf_op jit(solution)/shard_map/ppermute | solution.py:254
  63.5 0.0 copy-done.7
  63.5 0.0 copy-done.9
  63.5 4.0 %shard_map.72 = (bf16[512,512]{1,0:T(8,128)(2,1)S(1)}, bf16[512,512]{1,0:T(8,128)(2,1)S(1)}, f32[512,1024]{1,0:T(8,128)S(1)}, bf16[512,512]{1,0:T(8,128)(2,1)S(1)}) custom-call(s32[4]{0:T(128)S(1)} %pad_add_fusion.place_ref, bf16[16,128,128]{2,1,0:T(8,128)(2,1)S(1)} %shard_map.70.refs_0_, bf16[16,128,128]{2,1,0:T(8,128)(2,1)S(1)} %collective-permute-done.4.refs_1_, ...), custom_call_target="tpu_custom_call" | custom-call | flops 3221225472 | bytes 12582912 | tf_op jit(solution)/shard_map/pallas_call | solution.py:146
  67.5 0.1 collective-permute-start.11
  67.6 0.5 collective-permute-start.14
  68.1 0.1 collective-permute-start.15
  68.2 4.9 %collective-permute-done.12.own_ref = bf16[4,128,1024]{2,1,0:T(8,128)(2,1)S(1)} collective-permute-done((bf16[4,128,1024]{2,1,0:T(8,128)(2,1)S(1)}, bf16[4,128,1024]{2,1,0:T(8,128)(2,1)S(1)}, u32[]{:S(2)}, u32[]{:S(2)}) %collective-permute-start.12) | collective-permute-done | bytes 1048608 | tf_op jit(solution)/shard_map/ppermute | solution.py:254
  73.0 0.0 collective-permute-done.13.far_ref
  73.0 0.0 collective-permute-done.11.cross_ref
  73.0 0.0 collective-permute-done.14.share_0
  73.0 0.0 collective-permute-done.15.share_1
  73.0 0.0 copy-done.4
  73.0 0.0 copy-done.5
  73.1 0.0 copy-start.2
  73.1 2.1 %shard_map.73 = bf16[48,32,512]{2,1,0:T(8,128)(2,1)S(1)} custom-call(s32[4]{0:T(128)S(1)} %pad_add_fusion.place_ref, s32[16,16]{1,0:T(8,128)S(1)} %copy-done.4, s32[16,16]{1,0:T(8,128)S(1)} %copy-done.5, bf16[512,512]{1,0:T(8,128)(2,1)S(1)} %get-tuple-element.32.lhs_ref, bf16[512,512]{1,0:T(8,128)(2,1)S(1)} %collective-permute-done.11.cross_ref, ...), custom_call_target="tpu_custom_call" | custom-call | flops 1 | bytes 1 | tf_op jit(solution)/shard_map/pallas_call | solution.py:179
  75.2 0.0 copy-start.1
  75.2 29.2 %all_to_all.10 = bf16[48,32,512]{2,1,0:T(8,128)(2,1)S(1)} all-to-all(bf16[48,32,512]{2,1,0:T(8,128)(2,1)S(1)} %shard_map.73), channel_id=1, replica_groups=mesh['fsdp'=16,'pre'=8] {'fsdp'}, dimensions={0} | all-to-all | bytes 3145728 | tf_op jit(solution)/shard_map/all_to_all | solution.py:303
  104.5 0.0 copy-done.2
  104.5 0.0 copy-done.1
  104.5 14.3 %shard_map.74 = (bf16[3,512,512]{2,1,0:T(8,128)(2,1)}, f32[3,2,512,512]{3,2,1,0:T(8,128)}) custom-call(bf16[16,3,32,512]{3,2,1,0:T(8,128)(2,1)S(1)} %bitcast.15, bf16[3,2,512,512]{3,2,1,0:T(8,128)(2,1)S(1)} %bitcast.16, bf16[3,2,512,512]{3,2,1,0:T(8,128)(2,1)S(1)} %bitcast.17), custom_call_target="tpu_custom_call" | custom-call | flops 1 | bytes 1 | tf_op jit(solution)/shard_map/pallas_call | solution.py:214
  (3 shorter events, 0.1 us)
Async XLA Ops:
  0.6 8.2 %copy-start.3 = (bf16[256,1024]{1,0:T(8,128)(2,1)S(1)}, bf16[256,1024]{1,0:T(8,128)(2,1)}, u32[]{:S(2)}) copy-start(bf16[256,1024]{1,0:T(8,128)(2,1)} %a_ref.1) | copy-start | bytes 1572868
  1.9 2.0 %collective-permute-start = (bf16[2,128,1024]{2,1,0:T(8,128)(2,1)S(1)}, bf16[2,128,1024]{2,1,0:T(8,128)(2,1)S(1)}, u32[]{:S(2)}, u32[]{:S(2)}) collective-permute-start(bf16[2,128,1024]{2,1,0:T(8,128)(2,1)S(1)} %pad_maximum_fusion), channel_id=1, source_target_pairs={{0,1},{1,0},{2,3},{3,2},{4,5},{5,4},{6,7},{7,6},{8,9},{9,8},{10,11... | collective-permute-start | bytes 1572872 | tf_op jit(solution)/shard_map/ppermute | solution.py:237
  4.0 19.3 %collective-permute-start.1 = (bf16[2,128,1024]{2,1,0:T(8,128)(2,1)S(1)}, bf16[2,128,1024]{2,1,0:T(8,128)(2,1)S(1)}, u32[]{:S(2)}, u32[]{:S(2)}) collective-permute-start(bf16[2,128,1024]{2,1,0:T(8,128)(2,1)S(1)} %pad_maximum_fusion.1.refs_0_), channel_id=1, source_target_pairs={{8,0},{33,1},{10,2},{35,3},{12,4},{37,5},{14,6},{39,7},{16,8},{41,... | collective-permute-start | bytes 1572872 | tf_op jit(solution)/shard_map/ppermute | solution.py:254
  7.2 16.1 %collective-permute-start.2 = (bf16[2,128,1024]{2,1,0:T(8,128)(2,1)S(1)}, bf16[2,128,1024]{2,1,0:T(8,128)(2,1)S(1)}, u32[]{:S(2)}, u32[]{:S(2)}) collective-permute-start(bf16[2,128,1024]{2,1,0:T(8,128)(2,1)S(1)} %pad_maximum_fusion.1.refs_0_), channel_id=1, source_target_pairs={{16,0},{65,1},{18,2},{67,3},{20,4},{69,5},{22,6},{71,7},{24,8},{73... | collective-permute-start | bytes 1572872 | tf_op jit(solution)/shard_map/ppermute | solution.py:254
  7.8 18.2 %collective-permute-start.3 = (bf16[2,128,1024]{2,1,0:T(8,128)(2,1)S(1)}, bf16[2,128,1024]{2,1,0:T(8,128)(2,1)S(1)}, u32[]{:S(2)}, u32[]{:S(2)}) collective-permute-start(bf16[2,128,1024]{2,1,0:T(8,128)(2,1)S(1)} %pad_maximum_fusion.1.refs_0_), channel_id=1, source_target_pairs={{24,0},{97,1},{26,2},{99,3},{28,4},{101,5},{30,6},{103,7},{0,8},{1... | collective-permute-start | bytes 1572872 | tf_op jit(solution)/shard_map/ppermute | solution.py:254
  10.4 22.3 %all-to-all-start = ((bf16[16,128,128]{2,1,0:T(8,128)(2,1)}), bf16[16,128,128]{2,1,0:T(8,128)(2,1)S(1)}, u32[]{:S(2)}, u32[]{:S(2)}) async-start(bf16[16,128,128]{2,1,0:T(8,128)(2,1)} %shard_map.69), calls=%async_computation | async-start | bytes 1048576 | tf_op jit(solution)/shard_map/all_to_all | solution.py:284
  26.2 1.0 copy-start.6
  27.1 1.0 copy-start.8
  32.7 10.0 %collective-permute-start.4 = (bf16[16,128,128]{2,1,0:T(8,128)(2,1)S(1)}, bf16[16,128,128]{2,1,0:T(8,128)(2,1)S(1)}, u32[]{:S(2)}, u32[]{:S(2)}) collective-permute-start(bf16[16,128,128]{2,1,0:T(8,128)(2,1)S(1)} %shard_map.70.refs_0_), channel_id=1, source_target_pairs={{2,0},{3,1},{4,2},{5,3},{6,4},{7,5},{0,6},{1,7},{10,8},{11,9},{12,... | collective-permute-start | bytes 1572872 | tf_op jit(solution)/shard_map/ppermute | solution.py:243
  35.5 10.6 %collective-permute-start.5 = (bf16[16,128,128]{2,1,0:T(8,128)(2,1)S(1)}, bf16[16,128,128]{2,1,0:T(8,128)(2,1)S(1)}, u32[]{:S(2)}, u32[]{:S(2)}) collective-permute-start(bf16[16,128,128]{2,1,0:T(8,128)(2,1)S(1)} %shard_map.70.refs_0_), channel_id=1, source_target_pairs={{6,0},{7,1},{0,2},{1,3},{2,4},{3,5},{4,6},{5,7},{14,8},{15,9},{8,1... | collective-permute-start | bytes 1572872 | tf_op jit(solution)/shard_map/ppermute | solution.py:243
  35.5 15.0 %collective-permute-start.7 = (bf16[4,128,1024]{2,1,0:T(8,128)(2,1)}, bf16[4,128,1024]{2,1,0:T(8,128)(2,1)S(1)}, u32[]{:S(2)}, u32[]{:S(2)}) collective-permute-start(bf16[4,128,1024]{2,1,0:T(8,128)(2,1)} %copy-done.6), channel_id=1, source_target_pairs={{32,0},{9,1},{34,2},{11,3},{36,4},{13,5},{38,6},{15,7},{40,8},{17,... | collective-permute-start | bytes 3145736 | tf_op jit(solution)/shard_map/ppermute | solution.py:254
  35.9 16.2 %collective-permute-start.10 = (bf16[4,128,1024]{2,1,0:T(8,128)(2,1)}, bf16[4,128,1024]{2,1,0:T(8,128)(2,1)S(1)}, u32[]{:S(2)}, u32[]{:S(2)}) collective-permute-start(bf16[4,128,1024]{2,1,0:T(8,128)(2,1)} %copy-done.8), channel_id=1, source_target_pairs={{96,0},{25,1},{98,2},{27,3},{100,4},{29,5},{102,6},{31,7},{104,8},... | collective-permute-start | bytes 3145736 | tf_op jit(solution)/shard_map/ppermute | solution.py:254
  46.1 15.7 %collective-permute-start.8 = (bf16[4,128,1024]{2,1,0:T(8,128)(2,1)}, bf16[4,128,1024]{2,1,0:T(8,128)(2,1)S(1)}, u32[]{:S(2)}, u32[]{:S(2)}) collective-permute-start(bf16[4,128,1024]{2,1,0:T(8,128)(2,1)} %copy-done.8), channel_id=1, source_target_pairs={{32,0},{9,1},{34,2},{11,3},{36,4},{13,5},{38,6},{15,7},{40,8},{17,... | collective-permute-start | bytes 3145736 | tf_op jit(solution)/shard_map/ppermute | solution.py:254
  47.3 16.2 %collective-permute-start.9 = (bf16[4,128,1024]{2,1,0:T(8,128)(2,1)}, bf16[4,128,1024]{2,1,0:T(8,128)(2,1)S(1)}, u32[]{:S(2)}, u32[]{:S(2)}) collective-permute-start(bf16[4,128,1024]{2,1,0:T(8,128)(2,1)} %copy-done.6), channel_id=1, source_target_pairs={{96,0},{25,1},{98,2},{27,3},{100,4},{29,5},{102,6},{31,7},{104,8},... | collective-permute-start | bytes 3145736 | tf_op jit(solution)/shard_map/ppermute | solution.py:254
  48.1 13.6 %collective-permute-start.6 = (bf16[16,128,128]{2,1,0:T(8,128)(2,1)S(1)}, bf16[16,128,128]{2,1,0:T(8,128)(2,1)S(1)}, u32[]{:S(2)}, u32[]{:S(2)}) collective-permute-start(bf16[16,128,128]{2,1,0:T(8,128)(2,1)S(1)} %shard_map.70.refs_0_), channel_id=1, source_target_pairs={{4,0},{5,1},{6,2},{7,3},{0,4},{1,5},{2,6},{3,7},{12,8},{13,9},{14,... | collective-permute-start | bytes 1572872 | tf_op jit(solution)/shard_map/ppermute | solution.py:243
  50.5 22.5 %collective-permute-start.12 = (bf16[4,128,1024]{2,1,0:T(8,128)(2,1)S(1)}, bf16[4,128,1024]{2,1,0:T(8,128)(2,1)S(1)}, u32[]{:S(2)}, u32[]{:S(2)}) collective-permute-start(bf16[4,128,1024]{2,1,0:T(8,128)(2,1)S(1)} %collective-permute-done.7.refs_6_), channel_id=1, source_target_pairs={{32,0},{9,1},{34,2},{11,3},{36,4},{13,5},{38,6},{15,7},{40,8},{17,... | collective-permute-start | bytes 3145736 | tf_op jit(solution)/shard_map/ppermute | solution.py:254
  52.2 20.9 %collective-permute-start.13 = (bf16[4,128,1024]{2,1,0:T(8,128)(2,1)S(1)}, bf16[4,128,1024]{2,1,0:T(8,128)(2,1)S(1)}, u32[]{:S(2)}, u32[]{:S(2)}) collective-permute-start(bf16[4,128,1024]{2,1,0:T(8,128)(2,1)S(1)} %collective-permute-done.10.refs_9_), channel_id=1, source_target_pairs={{25,0},{96,1},{27,2},{98,3},{29,4},{100,5},{31,6},{102,7},{1,8},{1... | collective-permute-start | bytes 3145736 | tf_op jit(solution)/shard_map/ppermute | solution.py:263
  52.2 2.8 %copy-start = (f32[3,2,512,512]{3,2,1,0:T(8,128)S(1)}, f32[3,2,512,512]{3,2,1,0:T(8,128)}, u32[]{:S(2)}) copy-start(f32[3,2,512,512]{3,2,1,0:T(8,128)} %param.9) | copy-start | bytes 18874372
  54.9 8.5 %copy-start.7 = (bf16[4,128,1024]{2,1,0:T(8,128)(2,1)S(1)}, bf16[4,128,1024]{2,1,0:T(8,128)(2,1)}, u32[]{:S(2)}) copy-start(bf16[4,128,1024]{2,1,0:T(8,128)(2,1)} %copy-done.6) | copy-start | bytes 3145732
  55.0 8.5 %copy-start.9 = (bf16[4,128,1024]{2,1,0:T(8,128)(2,1)S(1)}, bf16[4,128,1024]{2,1,0:T(8,128)(2,1)}, u32[]{:S(2)}) copy-start(bf16[4,128,1024]{2,1,0:T(8,128)(2,1)} %copy-done.8) | copy-start | bytes 3145732
  61.8 11.3 %copy-start.4 = (s32[16,16]{1,0:T(8,128)S(1)}, s32[16,16]{1,0:T(8,128)}, u32[]{:S(2)}) copy-start(s32[16,16]{1,0:T(8,128)} %owner_ref.1) | copy-start | bytes 3076
  61.8 11.3 %copy-start.5 = (s32[16,16]{1,0:T(8,128)S(1)}, s32[16,16]{1,0:T(8,128)}, u32[]{:S(2)}) copy-start(s32[16,16]{1,0:T(8,128)} %offs_ref.1) | copy-start | bytes 3076
  67.5 5.5 %collective-permute-start.11 = (bf16[512,512]{1,0:T(8,128)(2,1)S(1)}, bf16[512,512]{1,0:T(8,128)(2,1)S(1)}, u32[]{:S(2)}, u32[]{:S(2)}) collective-permute-start(bf16[512,512]{1,0:T(8,128)(2,1)S(1)} %get-tuple-element.32.lhs_ref), channel_id=1, source_target_pairs={{0,1},{1,0},{2,3},{3,2},{4,5},{5,4},{6,7},{7,6},{8,9},{9,8},{10,11... | collective-permute-start | bytes 1572872 | tf_op jit(solution)/shard_map/ppermute | solution.py:237
  67.6 5.5 %collective-permute-start.14 = (bf16[512,512]{1,0:T(8,128)(2,1)S(1)}, bf16[512,512]{1,0:T(8,128)(2,1)S(1)}, u32[]{:S(2)}, u32[]{:S(2)}) collective-permute-start(bf16[512,512]{1,0:T(8,128)(2,1)S(1)} %get-tuple-element.34), channel_id=1, source_target_pairs={{0,1},{1,0},{2,3},{3,2},{4,5},{5,4},{6,7},{7,6},{8,9},{9,8},{10,11... | collective-permute-start | bytes 1572872 | tf_op jit(solution)/shard_map/ppermute | solution.py:237
  68.1 5.0 %collective-permute-start.15 = (bf16[512,512]{1,0:T(8,128)(2,1)S(1)}, bf16[512,512]{1,0:T(8,128)(2,1)S(1)}, u32[]{:S(2)}, u32[]{:S(2)}) collective-permute-start(bf16[512,512]{1,0:T(8,128)(2,1)S(1)} %get-tuple-element.35), channel_id=1, source_target_pairs={{0,1},{1,0},{2,3},{3,2},{4,5},{5,4},{6,7},{7,6},{8,9},{9,8},{10,11... | collective-permute-start | bytes 1572872 | tf_op jit(solution)/shard_map/ppermute | solution.py:237
  73.1 31.4 %copy-start.2 = (bf16[6,512,512]{2,1,0:T(8,128)(2,1)S(1)}, bf16[6,512,512]{2,1,0:T(8,128)(2,1)}, u32[]{:S(2)}) copy-start(bf16[6,512,512]{2,1,0:T(8,128)(2,1)} %get-tuple-element.37) | copy-start | bytes 9437188
  75.2 29.3 %copy-start.1 = (bf16[6,512,512]{2,1,0:T(8,128)(2,1)S(1)}, bf16[6,512,512]{2,1,0:T(8,128)(2,1)}, u32[]{:S(2)}) copy-start(bf16[6,512,512]{2,1,0:T(8,128)(2,1)} %get-tuple-element.36) | copy-start | bytes 9437188

commit v7 on v6

--- a/solution.py
+++ b/solution.py
@@ -62,7 +62,7 @@
         grid=(n,),
         in_specs=[spec],
         out_specs=[spec, spec],
-        out_shape=[pltpu.HBM((n, b, b), BF)] * 2,
+        out_shape=[jax.ShapeDtypeStruct((n, b, b), BF)] * 2,
         compiler_params=pltpu.CompilerParams(vmem_limit_bytes=MIDDLE_VMEM),
         cost_estimate=SHORT,
     )(roots)
@@ -189,19 +189,20 @@
 
 def newton_kernel(g_ref, xb_ref, f_ref, u_ref, n_ref):
     size = g_ref.shape[3]
+    slot = pl.program_id(0)
     g = g_ref[...].reshape(size, size)
     gt = g.T
     g32 = g.astype(F32)
     scale = 0.1 / (jnp.sum(g32 * g32) / size + 1e-6)
     stats = [dot(g, gt).astype(BF), dot(gt, g).astype(BF)]
-    es = [(scale * dot(f_ref[0, k], stats[k]) + f_ref[0, k].astype(F32)).astype(BF) for k in range(2)]
+    es = [(scale * dot(f_ref[slot, k], stats[k]) + f_ref[slot, k].astype(F32)).astype(BF) for k in range(2)]
     squares = [dot(e, e) for e in es]
     f_es = [(1.25 * e.astype(F32) - square).astype(BF) for e, square in zip(es, squares)]
     ts = [(square - 2.5 * e.astype(F32)).astype(BF) for e, square in zip(es, squares)]
     f_es = [(dot(t, v) + 1.5625 * v.astype(F32)).astype(BF) for t, v in zip(ts, f_es)]
     f_es = [dot(t, v) + 1.5625 * v.astype(F32) for t, v in zip(ts, f_es)]
     ws = [(1.25 * e.astype(F32) + v).astype(BF) for e, v in zip(es, f_es)]
-    xs = [1.5625 * xb_ref[0, k].astype(F32) - dot(xb_ref[0, k], ws[k]) for k in range(2)]
+    xs = [1.5625 * xb_ref[slot, k].astype(F32) - dot(xb_ref[slot, k], ws[k]) for k in range(2)]
     for k in range(2):
         n_ref[0, k] = xs[k]
     left, right = (x.astype(BF) for x in xs)
@@ -214,7 +215,7 @@
     return pl.pallas_call(
         newton_kernel,
         grid=(slots,),
-        in_specs=[pl.BlockSpec((n_src, 1, rows, b), lambda i: (0, i, 0, 0)), pair, pair],
+        in_specs=[pl.BlockSpec((n_src, 1, rows, b), lambda i: (0, i, 0, 0))] + [pl.BlockSpec(memory_space=pltpu.VMEM)] * 2,
         out_specs=[pl.BlockSpec((1, b, b), lambda i: (i, 0, 0)), pair],
         out_shape=[
             jax.ShapeDtypeStruct((slots, b, b), BF),

time: 119 us -> 119 us (level)
    unnamed x20 -> x16, local copies, waits for them, and re-layouts: 4.74 us -> 4.74 us
where the time goes in v7:
time: 119 us; the launch traced here: 118 us
  waiting for transfers between devices  34.4 us (29%)
  blocking collectives  29 us (24%)
  Pallas kernels  26.9 us (23%)
  starting transfers between devices  21.1 us (18%)
  local copies, waits for them, and re-layouts  5.97 us (5%)
    all_to_all x1, blocking collectives, body(): pieces = lax.all_to_all(pieces, 'fsdp', 0, 0, tiled=True)  29 us
    ppermute x8, waiting for transfers between devices, from_ring(): return lax.ppermute(v, ('fsdp', 'pre'), pairs)  19.4 us
    pallas_call x1, Pallas kernels, newton(): pl.pallas_call(newton_kernel, grid=(slots,), in_specs=[pl.BlockSpec((n_sr...  14.3 us
    ppermute x8, starting transfers between devices, from_ring(): return lax.ppermute(v, ('fsdp', 'pre'), pairs)  10.4 us
    ppermute x3, waiting for transfers between devices, from_x(): lax.ppermute(v, ('fsdp', 'pre'), [(device(z, y, x + d, c), device(z, y, x...  8.58 us
    all_to_all x1, starting transfers between devices, body(): mine = lax.all_to_all(mine, 'fsdp', 0, 0, tiled=True)  7.12 us
    pallas_call x1, Pallas kernels, fourth_powers(): pl.pallas_call(fourth_kernel, grid=(n,), in_specs=[spec], out_specs=[spec...  4.81 us
    unnamed x16, local copies, waits for them, and re-layouts  4.74 us
  transfers between devices with their start and end apart: 17, of which 10 were waited for; matrix products, arithmetic and copies ran while one was open for 0% of the time, Pallas kernels for 9%

profile of v7, /device:TPU:0, one launch (start us, length us, event | category | flops | bytes accessed | tf_op | source)
XLA Modules:
  0.0 118.4 jit_solution(13795530373723057362)
XLA Ops:
  0.6 0.0 copy-start.1
  0.7 1.2 %dynamic-slice_bitcast_fusion.2 = (bf16[1,128,1024]{2,1,0:T(8,128)(2,1)S(1)}, bf16[1,128,1024]{2,1,0:T(8,128)(2,1)S(1)}, bf16[1,128,1024]{2,1,0:T(8,128)(2,1)S(1)}) fusion(bf16[256,1024]{1,0:T(8,128)(2,1)} %param.6, s32[]{:T(128)S(6)} %select_n.29, s32[]{:T(128)S(6)} %select_n.30, bf16[256,1024]{1,0:T(8,128)(2,1)} %a_ref.1), kind=kLoop, calls=%fused_computation.4 | loop fusion | bytes 1572872 | tf_op jit(solution)/shard_map/stack | solution.py:279
  1.9 0.1 pad_maximum_fusion
  1.9 0.1 collective-permute-start
  2.1 1.9 %collective-permute-done.r_ref = bf16[2,128,1024]{2,1,0:T(8,128)(2,1)S(1)} collective-permute-done((bf16[2,128,1024]{2,1,0:T(8,128)(2,1)S(1)}, bf16[2,128,1024]{2,1,0:T(8,128)(2,1)S(1)}, u32[]{:S(2)}, u32[]{:S(2)}) %collective-permute-start) | collective-permute-done | bytes 524320 | tf_op jit(solution)/shard_map/ppermute | solution.py:238
  4.0 0.1 pad_maximum_fusion.1.refs_0_
  4.0 3.2 %collective-permute-start.1 = (bf16[2,128,1024]{2,1,0:T(8,128)(2,1)S(1)}, bf16[2,128,1024]{2,1,0:T(8,128)(2,1)S(1)}, u32[]{:S(2)}, u32[]{:S(2)}) collective-permute-start(bf16[2,128,1024]{2,1,0:T(8,128)(2,1)S(1)} %pad_maximum_fusion.1.refs_0_), channel_id=1, source_target_pairs={{8,0},{33,1},{10,2},{35,3},{12,4},{37,5},{14,6},{39,7},{16,8},{41,... | collective-permute-start | bytes 1572872 | tf_op jit(solution)/shard_map/ppermute | solution.py:255
  7.2 0.6 collective-permute-start.2
  7.8 1.0 collective-permute-start.3
  8.8 0.1 pad_add_fusion.place_ref
  8.9 0.0 copy-done.1
  8.9 1.5 %shard_map.69 = bf16[16,128,128]{2,1,0:T(8,128)(2,1)} custom-call(s32[4]{0:T(128)S(1)} %pad_add_fusion.place_ref, bf16[256,1024]{1,0:T(8,128)(2,1)S(1)} %copy-done.1, bf16[2,128,1024]{2,1,0:T(8,128)(2,1)S(1)} %collective-permute-done.r_ref), custom_call_target="tpu_custom_call" | custom-call | flops 1 | bytes 1 | tf_op jit(solution)/shard_map/pallas_call | solution.py:39
  10.4 7.1 %all-to-all-start = ((bf16[16,128,128]{2,1,0:T(8,128)(2,1)}), bf16[16,128,128]{2,1,0:T(8,128)(2,1)S(1)}, u32[]{:S(2)}, u32[]{:S(2)}) async-start(bf16[16,128,128]{2,1,0:T(8,128)(2,1)} %shard_map.69), calls=%async_computation | async-start | bytes 1048576 | tf_op jit(solution)/shard_map/all_to_all | solution.py:285
  17.5 5.7 %collective-permute-done.1.refs_1_ = bf16[2,128,1024]{2,1,0:T(8,128)(2,1)S(1)} collective-permute-done((bf16[2,128,1024]{2,1,0:T(8,128)(2,1)S(1)}, bf16[2,128,1024]{2,1,0:T(8,128)(2,1)S(1)}, u32[]{:S(2)}, u32[]{:S(2)}) %collective-permute-start.1) | collective-permute-done | bytes 524320 | tf_op jit(solution)/shard_map/ppermute | solution.py:255
  23.3 0.0 collective-permute-done.2.refs_2_
  23.3 2.7 %collective-permute-done.3.refs_3_ = bf16[2,128,1024]{2,1,0:T(8,128)(2,1)S(1)} collective-permute-done((bf16[2,128,1024]{2,1,0:T(8,128)(2,1)S(1)}, bf16[2,128,1024]{2,1,0:T(8,128)(2,1)S(1)}, u32[]{:S(2)}, u32[]{:S(2)}) %collective-permute-start.3) | collective-permute-done | bytes 524320 | tf_op jit(solution)/shard_map/ppermute | solution.py:255
  26.0 0.1 shard_map.68
  26.2 0.0 copy-start.4
  26.2 1.0 copy-done.4
  27.1 0.0 copy-start.6
  27.1 1.0 copy-done.6
  28.1 4.6 %all-to-all-done.v_ref = bf16[16,128,128]{2,1,0:T(8,128)(2,1)S(1)} async-done(((bf16[16,128,128]{2,1,0:T(8,128)(2,1)}), bf16[16,128,128]{2,1,0:T(8,128)(2,1)S(1)}, u32[]{:S(2)}, u32[]{:S(2)}) %all-to-all-start) | async-done | bytes 524320 | tf_op jit(solution)/shard_map/all_to_all | solution.py:285
  32.7 2.8 %collective-permute-start.4 = (bf16[16,128,128]{2,1,0:T(8,128)(2,1)S(1)}, bf16[16,128,128]{2,1,0:T(8,128)(2,1)S(1)}, u32[]{:S(2)}, u32[]{:S(2)}) collective-permute-start(bf16[16,128,128]{2,1,0:T(8,128)(2,1)S(1)} %shard_map.70.refs_0_), channel_id=1, source_target_pairs={{2,0},{3,1},{4,2},{5,3},{6,4},{7,5},{0,6},{1,7},{10,8},{11,9},{12,... | collective-permute-start | bytes 1572872 | tf_op jit(solution)/shard_map/ppermute | solution.py:244
  35.5 0.0 collective-permute-start.5
  35.5 0.4 collective-permute-start.7
  35.9 1.6 %collective-permute-start.10 = (bf16[4,128,1024]{2,1,0:T(8,128)(2,1)}, bf16[4,128,1024]{2,1,0:T(8,128)(2,1)S(1)}, u32[]{:S(2)}, u32[]{:S(2)}) collective-permute-start(bf16[4,128,1024]{2,1,0:T(8,128)(2,1)} %copy-done.6), channel_id=1, source_target_pairs={{96,0},{25,1},{98,2},{27,3},{100,4},{29,5},{102,6},{31,7},{104,8},... | collective-permute-start | bytes 3145736 | tf_op jit(solution)/shard_map/ppermute | solution.py:255
  37.6 5.2 %collective-permute-done.4.refs_1_ = bf16[16,128,128]{2,1,0:T(8,128)(2,1)S(1)} collective-permute-done((bf16[16,128,128]{2,1,0:T(8,128)(2,1)S(1)}, bf16[16,128,128]{2,1,0:T(8,128)(2,1)S(1)}, u32[]{:S(2)}, u32[]{:S(2)}) %collective-permute-start.4) | collective-permute-done | bytes 524320 | tf_op jit(solution)/shard_map/ppermute | solution.py:244
  42.7 3.4 %collective-permute-done.5.refs_3_ = bf16[16,128,128]{2,1,0:T(8,128)(2,1)S(1)} collective-permute-done((bf16[16,128,128]{2,1,0:T(8,128)(2,1)S(1)}, bf16[16,128,128]{2,1,0:T(8,128)(2,1)S(1)}, u32[]{:S(2)}, u32[]{:S(2)}) %collective-permute-start.5) | collective-permute-done | bytes 524320 | tf_op jit(solution)/shard_map/ppermute | solution.py:244
  46.1 1.1 collective-permute-start.8
  47.3 0.9 collective-permute-start.9
  48.2 0.0 collective-permute-start.6
  48.2 2.4 %collective-permute-done.7.refs_6_ = bf16[4,128,1024]{2,1,0:T(8,128)(2,1)S(1)} collective-permute-done((bf16[4,128,1024]{2,1,0:T(8,128)(2,1)}, bf16[4,128,1024]{2,1,0:T(8,128)(2,1)S(1)}, u32[]{:S(2)}, u32[]{:S(2)}) %collective-permute-start.7) | collective-permute-done | bytes 1048608 | tf_op jit(solution)/shard_map/ppermute | solution.py:255
  50.5 1.6 %collective-permute-start.12 = (bf16[4,128,1024]{2,1,0:T(8,128)(2,1)S(1)}, bf16[4,128,1024]{2,1,0:T(8,128)(2,1)S(1)}, u32[]{:S(2)}, u32[]{:S(2)}) collective-permute-start(bf16[4,128,1024]{2,1,0:T(8,128)(2,1)S(1)} %collective-permute-done.7.refs_6_), channel_id=1, source_target_pairs={{32,0},{9,1},{34,2},{11,3},{36,4},{13,5},{38,6},{15,7},{40,8},{17,... | collective-permute-start | bytes 3145736 | tf_op jit(solution)/shard_map/ppermute | solution.py:255
  52.2 0.0 collective-permute-done.10.refs_9_
  52.2 0.0 collective-permute-start.13
  52.2 0.0 copy-start
  52.2 2.8 %copy-done = f32[3,2,512,512]{3,2,1,0:T(8,128)S(1)} copy-done((f32[3,2,512,512]{3,2,1,0:T(8,128)S(1)}, f32[3,2,512,512]{3,2,1,0:T(8,128)}, u32[]{:S(2)}) %copy-start) | copy-done | bytes 6291480
  54.9 0.0 copy-start.5
  55.0 0.0 copy-start.7
  55.0 4.8 %shard_map.71 = (bf16[6,512,512]{2,1,0:T(8,128)(2,1)S(1)}, bf16[6,512,512]{2,1,0:T(8,128)(2,1)S(1)}) custom-call(f32[6,512,512]{2,1,0:T(8,128)S(1)} %bitcast.14), custom_call_target="tpu_custom_call" | custom-call | flops 1 | bytes 1 | tf_op jit(solution)/shard_map/pallas_call | solution.py:60
  59.8 2.0 %collective-permute-done.8.refs_7_ = bf16[4,128,1024]{2,1,0:T(8,128)(2,1)S(1)} collective-permute-done((bf16[4,128,1024]{2,1,0:T(8,128)(2,1)}, bf16[4,128,1024]{2,1,0:T(8,128)(2,1)S(1)}, u32[]{:S(2)}, u32[]{:S(2)}) %collective-permute-start.8) | collective-permute-done | bytes 1048608 | tf_op jit(solution)/shard_map/ppermute | solution.py:255
  61.8 0.0 copy-start.2
  61.8 0.0 copy-start.3
  61.8 0.0 collective-permute-done.6.refs_2_
  61.8 1.7 %collective-permute-done.9.refs_8_ = bf16[4,128,1024]{2,1,0:T(8,128)(2,1)S(1)} collective-permute-done((bf16[4,128,1024]{2,1,0:T(8,128)(2,1)}, bf16[4,128,1024]{2,1,0:T(8,128)(2,1)S(1)}, u32[]{:S(2)}, u32[]{:S(2)}) %collective-permute-start.9) | collective-permute-done | bytes 1048608 | tf_op jit(solution)/shard_map/ppermute | solution.py:255
  63.5 0.0 copy-done.5
  63.5 0.0 copy-done.7
  63.5 4.0 %shard_map.72 = (bf16[512,512]{1,0:T(8,128)(2,1)S(1)}, bf16[512,512]{1,0:T(8,128)(2,1)S(1)}, f32[512,1024]{1,0:T(8,128)S(1)}, bf16[512,512]{1,0:T(8,128)(2,1)S(1)}) custom-call(s32[4]{0:T(128)S(1)} %pad_add_fusion.place_ref, bf16[16,128,128]{2,1,0:T(8,128)(2,1)S(1)} %shard_map.70.refs_0_, bf16[16,128,128]{2,1,0:T(8,128)(2,1)S(1)} %collective-permute-done.4.refs_1_, ...), custom_call_target="tpu_custom_call" | custom-call | flops 3221225472 | bytes 12582912 | tf_op jit(solution)/shard_map/pallas_call | solution.py:146
  67.5 0.1 collective-permute-start.11
  67.6 0.5 collective-permute-start.14
  68.1 0.1 collective-permute-start.15
  68.2 4.8 %collective-permute-done.12.own_ref = bf16[4,128,1024]{2,1,0:T(8,128)(2,1)S(1)} collective-permute-done((bf16[4,128,1024]{2,1,0:T(8,128)(2,1)S(1)}, bf16[4,128,1024]{2,1,0:T(8,128)(2,1)S(1)}, u32[]{:S(2)}, u32[]{:S(2)}) %collective-permute-start.12) | collective-permute-done | bytes 1048608 | tf_op jit(solution)/shard_map/ppermute | solution.py:255
  73.0 0.0 collective-permute-done.13.far_ref
  73.0 0.0 collective-permute-done.11.cross_ref
  73.0 0.0 collective-permute-done.14.share_0
  73.0 0.0 collective-permute-done.15.share_1
  73.0 0.0 copy-done.2
  73.0 0.0 copy-done.3
  73.1 2.1 %shard_map.73 = bf16[48,32,512]{2,1,0:T(8,128)(2,1)S(1)} custom-call(s32[4]{0:T(128)S(1)} %pad_add_fusion.place_ref, s32[16,16]{1,0:T(8,128)S(1)} %copy-done.2, s32[16,16]{1,0:T(8,128)S(1)} %copy-done.3, bf16[512,512]{1,0:T(8,128)(2,1)S(1)} %get-tuple-element.32.lhs_ref, bf16[512,512]{1,0:T(8,128)(2,1)S(1)} %collective-permute-done.11.cross_ref, ...), custom_call_target="tpu_custom_call" | custom-call | flops 1 | bytes 1 | tf_op jit(solution)/shard_map/pallas_call | solution.py:179
  75.1 29.0 %all_to_all.10 = bf16[48,32,512]{2,1,0:T(8,128)(2,1)S(1)} all-to-all(bf16[48,32,512]{2,1,0:T(8,128)(2,1)S(1)} %shard_map.73), channel_id=1, replica_groups=mesh['fsdp'=16,'pre'=8] {'fsdp'}, dimensions={0} | all-to-all | bytes 3145728 | tf_op jit(solution)/shard_map/all_to_all | solution.py:304
  104.1 14.3 %shard_map.74 = (bf16[3,512,512]{2,1,0:T(8,128)(2,1)}, f32[3,2,512,512]{3,2,1,0:T(8,128)}) custom-call(bf16[16,3,32,512]{3,2,1,0:T(8,128)(2,1)S(1)} %bitcast.15, bf16[3,2,512,512]{3,2,1,0:T(8,128)(2,1)S(1)} %bitcast.16, bf16[3,2,512,512]{3,2,1,0:T(8,128)(2,1)S(1)} %bitcast.17), custom_call_target="tpu_custom_call" | custom-call | flops 1 | bytes 1 | tf_op jit(solution)/shard_map/pallas_call | solution.py:215
  (2 shorter events, 0.1 us)
Async XLA Ops:
  0.6 8.2 %copy-start.1 = (bf16[256,1024]{1,0:T(8,128)(2,1)S(1)}, bf16[256,1024]{1,0:T(8,128)(2,1)}, u32[]{:S(2)}) copy-start(bf16[256,1024]{1,0:T(8,128)(2,1)} %a_ref.1) | copy-start | bytes 1572868
  1.9 2.0 %collective-permute-start = (bf16[2,128,1024]{2,1,0:T(8,128)(2,1)S(1)}, bf16[2,128,1024]{2,1,0:T(8,128)(2,1)S(1)}, u32[]{:S(2)}, u32[]{:S(2)}) collective-permute-start(bf16[2,128,1024]{2,1,0:T(8,128)(2,1)S(1)} %pad_maximum_fusion), channel_id=1, source_target_pairs={{0,1},{1,0},{2,3},{3,2},{4,5},{5,4},{6,7},{7,6},{8,9},{9,8},{10,11... | collective-permute-start | bytes 1572872 | tf_op jit(solution)/shard_map/ppermute | solution.py:238
  4.0 19.3 %collective-permute-start.1 = (bf16[2,128,1024]{2,1,0:T(8,128)(2,1)S(1)}, bf16[2,128,1024]{2,1,0:T(8,128)(2,1)S(1)}, u32[]{:S(2)}, u32[]{:S(2)}) collective-permute-start(bf16[2,128,1024]{2,1,0:T(8,128)(2,1)S(1)} %pad_maximum_fusion.1.refs_0_), channel_id=1, source_target_pairs={{8,0},{33,1},{10,2},{35,3},{12,4},{37,5},{14,6},{39,7},{16,8},{41,... | collective-permute-start | bytes 1572872 | tf_op jit(solution)/shard_map/ppermute | solution.py:255
  7.2 16.1 %collective-permute-start.2 = (bf16[2,128,1024]{2,1,0:T(8,128)(2,1)S(1)}, bf16[2,128,1024]{2,1,0:T(8,128)(2,1)S(1)}, u32[]{:S(2)}, u32[]{:S(2)}) collective-permute-start(bf16[2,128,1024]{2,1,0:T(8,128)(2,1)S(1)} %pad_maximum_fusion.1.refs_0_), channel_id=1, source_target_pairs={{16,0},{65,1},{18,2},{67,3},{20,4},{69,5},{22,6},{71,7},{24,8},{73... | collective-permute-start | bytes 1572872 | tf_op jit(solution)/shard_map/ppermute | solution.py:255
  7.8 18.2 %collective-permute-start.3 = (bf16[2,128,1024]{2,1,0:T(8,128)(2,1)S(1)}, bf16[2,128,1024]{2,1,0:T(8,128)(2,1)S(1)}, u32[]{:S(2)}, u32[]{:S(2)}) collective-permute-start(bf16[2,128,1024]{2,1,0:T(8,128)(2,1)S(1)} %pad_maximum_fusion.1.refs_0_), channel_id=1, source_target_pairs={{24,0},{97,1},{26,2},{99,3},{28,4},{101,5},{30,6},{103,7},{0,8},{1... | collective-permute-start | bytes 1572872 | tf_op jit(solution)/shard_map/ppermute | solution.py:255
  10.4 22.3 %all-to-all-start = ((bf16[16,128,128]{2,1,0:T(8,128)(2,1)}), bf16[16,128,128]{2,1,0:T(8,128)(2,1)S(1)}, u32[]{:S(2)}, u32[]{:S(2)}) async-start(bf16[16,128,128]{2,1,0:T(8,128)(2,1)} %shard_map.69), calls=%async_computation | async-start | bytes 1048576 | tf_op jit(solution)/shard_map/all_to_all | solution.py:285
  26.2 1.0 copy-start.4
  27.1 1.0 copy-start.6
  32.7 10.0 %collective-permute-start.4 = (bf16[16,128,128]{2,1,0:T(8,128)(2,1)S(1)}, bf16[16,128,128]{2,1,0:T(8,128)(2,1)S(1)}, u32[]{:S(2)}, u32[]{:S(2)}) collective-permute-start(bf16[16,128,128]{2,1,0:T(8,128)(2,1)S(1)} %shard_map.70.refs_0_), channel_id=1, source_target_pairs={{2,0},{3,1},{4,2},{5,3},{6,4},{7,5},{0,6},{1,7},{10,8},{11,9},{12,... | collective-permute-start | bytes 1572872 | tf_op jit(solution)/shard_map/ppermute | solution.py:244
  35.5 10.6 %collective-permute-start.5 = (bf16[16,128,128]{2,1,0:T(8,128)(2,1)S(1)}, bf16[16,128,128]{2,1,0:T(8,128)(2,1)S(1)}, u32[]{:S(2)}, u32[]{:S(2)}) collective-permute-start(bf16[16,128,128]{2,1,0:T(8,128)(2,1)S(1)} %shard_map.70.refs_0_), channel_id=1, source_target_pairs={{6,0},{7,1},{0,2},{1,3},{2,4},{3,5},{4,6},{5,7},{14,8},{15,9},{8,1... | collective-permute-start | bytes 1572872 | tf_op jit(solution)/shard_map/ppermute | solution.py:244
  35.5 15.0 %collective-permute-start.7 = (bf16[4,128,1024]{2,1,0:T(8,128)(2,1)}, bf16[4,128,1024]{2,1,0:T(8,128)(2,1)S(1)}, u32[]{:S(2)}, u32[]{:S(2)}) collective-permute-start(bf16[4,128,1024]{2,1,0:T(8,128)(2,1)} %copy-done.4), channel_id=1, source_target_pairs={{32,0},{9,1},{34,2},{11,3},{36,4},{13,5},{38,6},{15,7},{40,8},{17,... | collective-permute-start | bytes 3145736 | tf_op jit(solution)/shard_map/ppermute | solution.py:255
  35.9 16.2 %collective-permute-start.10 = (bf16[4,128,1024]{2,1,0:T(8,128)(2,1)}, bf16[4,128,1024]{2,1,0:T(8,128)(2,1)S(1)}, u32[]{:S(2)}, u32[]{:S(2)}) collective-permute-start(bf16[4,128,1024]{2,1,0:T(8,128)(2,1)} %copy-done.6), channel_id=1, source_target_pairs={{96,0},{25,1},{98,2},{27,3},{100,4},{29,5},{102,6},{31,7},{104,8},... | collective-permute-start | bytes 3145736 | tf_op jit(solution)/shard_map/ppermute | solution.py:255
  46.1 15.6 %collective-permute-start.8 = (bf16[4,128,1024]{2,1,0:T(8,128)(2,1)}, bf16[4,128,1024]{2,1,0:T(8,128)(2,1)S(1)}, u32[]{:S(2)}, u32[]{:S(2)}) collective-permute-start(bf16[4,128,1024]{2,1,0:T(8,128)(2,1)} %copy-done.6), channel_id=1, source_target_pairs={{32,0},{9,1},{34,2},{11,3},{36,4},{13,5},{38,6},{15,7},{40,8},{17,... | collective-permute-start | bytes 3145736 | tf_op jit(solution)/shard_map/ppermute | solution.py:255
  47.3 16.2 %collective-permute-start.9 = (bf16[4,128,1024]{2,1,0:T(8,128)(2,1)}, bf16[4,128,1024]{2,1,0:T(8,128)(2,1)S(1)}, u32[]{:S(2)}, u32[]{:S(2)}) collective-permute-start(bf16[4,128,1024]{2,1,0:T(8,128)(2,1)} %copy-done.4), channel_id=1, source_target_pairs={{96,0},{25,1},{98,2},{27,3},{100,4},{29,5},{102,6},{31,7},{104,8},... | collective-permute-start | bytes 3145736 | tf_op jit(solution)/shard_map/ppermute | solution.py:255
  48.2 13.6 %collective-permute-start.6 = (bf16[16,128,128]{2,1,0:T(8,128)(2,1)S(1)}, bf16[16,128,128]{2,1,0:T(8,128)(2,1)S(1)}, u32[]{:S(2)}, u32[]{:S(2)}) collective-permute-start(bf16[16,128,128]{2,1,0:T(8,128)(2,1)S(1)} %shard_map.70.refs_0_), channel_id=1, source_target_pairs={{4,0},{5,1},{6,2},{7,3},{0,4},{1,5},{2,6},{3,7},{12,8},{13,9},{14,... | collective-permute-start | bytes 1572872 | tf_op jit(solution)/shard_map/ppermute | solution.py:244
  50.5 22.5 %collective-permute-start.12 = (bf16[4,128,1024]{2,1,0:T(8,128)(2,1)S(1)}, bf16[4,128,1024]{2,1,0:T(8,128)(2,1)S(1)}, u32[]{:S(2)}, u32[]{:S(2)}) collective-permute-start(bf16[4,128,1024]{2,1,0:T(8,128)(2,1)S(1)} %collective-permute-done.7.refs_6_), channel_id=1, source_target_pairs={{32,0},{9,1},{34,2},{11,3},{36,4},{13,5},{38,6},{15,7},{40,8},{17,... | collective-permute-start | bytes 3145736 | tf_op jit(solution)/shard_map/ppermute | solution.py:255
  52.2 20.9 %collective-permute-start.13 = (bf16[4,128,1024]{2,1,0:T(8,128)(2,1)S(1)}, bf16[4,128,1024]{2,1,0:T(8,128)(2,1)S(1)}, u32[]{:S(2)}, u32[]{:S(2)}) collective-permute-start(bf16[4,128,1024]{2,1,0:T(8,128)(2,1)S(1)} %collective-permute-done.10.refs_9_), channel_id=1, source_target_pairs={{25,0},{96,1},{27,2},{98,3},{29,4},{100,5},{31,6},{102,7},{1,8},{1... | collective-permute-start | bytes 3145736 | tf_op jit(solution)/shard_map/ppermute | solution.py:264
  52.2 2.8 %copy-start = (f32[3,2,512,512]{3,2,1,0:T(8,128)S(1)}, f32[3,2,512,512]{3,2,1,0:T(8,128)}, u32[]{:S(2)}) copy-start(f32[3,2,512,512]{3,2,1,0:T(8,128)} %param.9) | copy-start | bytes 18874372
  54.9 8.5 %copy-start.5 = (bf16[4,128,1024]{2,1,0:T(8,128)(2,1)S(1)}, bf16[4,128,1024]{2,1,0:T(8,128)(2,1)}, u32[]{:S(2)}) copy-start(bf16[4,128,1024]{2,1,0:T(8,128)(2,1)} %copy-done.4) | copy-start | bytes 3145732
  55.0 8.5 %copy-start.7 = (bf16[4,128,1024]{2,1,0:T(8,128)(2,1)S(1)}, bf16[4,128,1024]{2,1,0:T(8,128)(2,1)}, u32[]{:S(2)}) copy-start(bf16[4,128,1024]{2,1,0:T(8,128)(2,1)} %copy-done.6) | copy-start | bytes 3145732
  61.8 11.3 %copy-start.2 = (s32[16,16]{1,0:T(8,128)S(1)}, s32[16,16]{1,0:T(8,128)}, u32[]{:S(2)}) copy-start(s32[16,16]{1,0:T(8,128)} %owner_ref.1) | copy-start | bytes 3076
  61.8 11.3 %copy-start.3 = (s32[16,16]{1,0:T(8,128)S(1)}, s32[16,16]{1,0:T(8,128)}, u32[]{:S(2)}) copy-start(s32[16,16]{1,0:T(8,128)} %offs_ref.1) | copy-start | bytes 3076
  67.5 5.5 %collective-permute-start.11 = (bf16[512,512]{1,0:T(8,128)(2,1)S(1)}, bf16[512,512]{1,0:T(8,128)(2,1)S(1)}, u32[]{:S(2)}, u32[]{:S(2)}) collective-permute-start(bf16[512,512]{1,0:T(8,128)(2,1)S(1)} %get-tuple-element.32.lhs_ref), channel_id=1, source_target_pairs={{0,1},{1,0},{2,3},{3,2},{4,5},{5,4},{6,7},{7,6},{8,9},{9,8},{10,11... | collective-permute-start | bytes 1572872 | tf_op jit(solution)/shard_map/ppermute | solution.py:238
  67.6 5.4 %collective-permute-start.14 = (bf16[512,512]{1,0:T(8,128)(2,1)S(1)}, bf16[512,512]{1,0:T(8,128)(2,1)S(1)}, u32[]{:S(2)}, u32[]{:S(2)}) collective-permute-start(bf16[512,512]{1,0:T(8,128)(2,1)S(1)} %get-tuple-element.34), channel_id=1, source_target_pairs={{0,1},{1,0},{2,3},{3,2},{4,5},{5,4},{6,7},{7,6},{8,9},{9,8},{10,11... | collective-permute-start | bytes 1572872 | tf_op jit(solution)/shard_map/ppermute | solution.py:238
  68.1 5.0 %collective-permute-start.15 = (bf16[512,512]{1,0:T(8,128)(2,1)S(1)}, bf16[512,512]{1,0:T(8,128)(2,1)S(1)}, u32[]{:S(2)}, u32[]{:S(2)}) collective-permute-start(bf16[512,512]{1,0:T(8,128)(2,1)S(1)} %get-tuple-element.35), channel_id=1, source_target_pairs={{0,1},{1,0},{2,3},{3,2},{4,5},{5,4},{6,7},{7,6},{8,9},{9,8},{10,11... | collective-permute-start | bytes 1572872 | tf_op jit(solution)/shard_map/ppermute | solution.py:238
